TPU v7x, 32 devices: a whole 2x2x4 slice. The times are simulated.
32 devices in a mesh: tiles: 16 (over z, y, x), pix: 2 (over core).
Axes of the slice: x: 2, y: 2, z: 4, core: 2. Of those that a mesh axis runs over, the one named last changes fastest.
Arguments:
- frames: bfloat16 [4096, 8192], P('tiles', 'pix'), may hold values from -60 to 60
- tile_valid: int32 [4096], P('tiles'), may hold values from 0 to 1
- foreground_blocks: int32 [4096], P('tiles'), may hold values from 0 to 8, as said below
- basis_start: float32 [16, 8192], P(None, 'pix'), may hold values from -12 to 12
- dark_start: float32 [8192], P('pix'), may hold values from -4 to 4
Outputs:
- flatfield_basis: float32 [16, 8192], P(None, 'pix')
- darkfield: float32 [8192], P('pix')
- coefficients: float32 [4096, 16], P('tiles')
Inputs may be any that keep to these rules, and one draw needn't show every extreme that they name: `foreground_blocks`: some tile has exactly 8.
All inputs are finite; a program needn't handle non-finite values.
Results may differ from a plain program's by a relative error of at most 0.0003.
Values sent between devices are 32-bit elements; how exact they have to be, the bound alone decides.
No kernel may reach another device: no remote copies, remote signals or barrier semaphores. Data moves between devices by JAX's collectives and lax.ppermute only.
A program may use at most 64 MiB of HBM per device.

v0:
```python
import jax
import jax.numpy as jnp
from jax import lax
from jax.sharding import PartitionSpec as P

ROW_PX = 2048
ITERS = 2


precise = lax.Precision.HIGHEST
ridge_weight = 0.01


def solve_gram(gram_matrix, right_rows):
    factor = jnp.linalg.cholesky(gram_matrix)
    return jax.scipy.linalg.cho_solve((factor, True), right_rows)


def advance(basis, darkfield, totals, gram_c, tile_count):
    components = basis.shape[0]
    change = solve_gram(gram_c, totals[:components] / tile_count)
    return (basis + change, darkfield + totals[components] / (totals[components + 1] + 1.0))


def local(frames, tile_valid, foreground_blocks, basis_start, dark_start):
    tile_dev, pix_dev = frames.shape
    components = basis_start.shape[0]
    tiles_all = tile_dev * lax.axis_size("tiles")
    pixels_all = pix_dev * lax.axis_size("pix")
    column = jnp.arange(pix_dev, dtype=jnp.int32) % ROW_PX // 128
    valid_float = tile_valid.astype(jnp.float32)
    usable = valid_float[:, None] * (column[None, :] >= foreground_blocks[:, None]).astype(
        jnp.float32
    )
    identity = jnp.eye(components, dtype=jnp.float32)
    basis = basis_start
    darkfield = dark_start
    coefficients = jnp.zeros((tile_dev, components), jnp.float32)
    for iteration in range(ITERS):
        shifted = frames.astype(jnp.float32) - darkfield[None, :]
        local_gram = jnp.dot(basis, basis.T, precision=precise)
        local_proj = jnp.dot(shifted, basis.T, precision=precise)
        gram_total, proj_total = lax.psum((local_gram, local_proj), "pix")
        gram_f = gram_total / pixels_all + ridge_weight * identity
        coefficients = solve_gram(gram_f, (proj_total / pixels_all).T).T
        residual = shifted - jnp.dot(coefficients, basis, precision=precise)
        local_square = jnp.sum(usable * residual * residual)
        local_coef_gram = jnp.dot(
            (coefficients * valid_float[:, None]).T, coefficients, precision=precise
        )
        square_total = lax.psum(local_square, ("tiles", "pix"))
        coef_total = lax.psum(local_coef_gram, "tiles")
        spread = square_total / (tiles_all * pixels_all) + 1e-05
        weights = usable / (1.0 + residual * residual / (4.0 * spread))
        weighted = weights * residual
        column_terms = jnp.concatenate(
            [
                jnp.dot(coefficients.T, weighted, precision=precise),
                jnp.sum(weighted, axis=0, keepdims=True),
                jnp.sum(weights, axis=0, keepdims=True),
            ],
            axis=0,
        )
        gram_c = coef_total / tiles_all + ridge_weight * identity
        totals = lax.psum(column_terms, "tiles")
        basis, darkfield = advance(basis, darkfield, totals, gram_c, tiles_all)
    return (basis, darkfield, coefficients)


def solution(mesh):
    return jax.shard_map(
        local,
        mesh=mesh,
        in_specs=(P("tiles", "pix"), P("tiles"), P("tiles"), P(None, "pix"), P("pix")),
        out_specs=(P(None, "pix"), P("pix"), P("tiles", None)),
        check_vma=False,
    )
```

profile of v0, /device:TPU:0, one launch (start us, length us, event | category | flops | bytes accessed | tf_op | source)
XLA Modules:
  0.0 374.4 jit_solution(12844983570084567672)
XLA Ops:
  7.3 0.8 convert_element_type.10
  8.1 1.5 fusion.62
  9.6 5.0 %fusion.2 = f32[256,16]{1,0:T(8,128)S(1)} fusion(f32[16,4096]{1,0:T(8,128)} %param.13, bf16[256,4096]{1,0:T(8,128)(2,1)} %param.10, f32[4096]{0:T(1024)} %param.14), kind=kOutput, calls=%fused_computation.10 | convolution fusion | flops 203423744 | bytes 2392064 | tf_op jit(solution)/shard_map/dot_general | solution.py:42
  14.6 4.0 %all-reduce.1 = (f32[256,16]{1,0:T(8,128)S(1)}, f32[16,16]{0,1:T(8,128)S(1)}) all-reduce(f32[256,16]{1,0:T(8,128)S(1)} %fusion.2, f32[16,16]{0,1:T(8,128)S(1)} %fusion.62), channel_id=1, replica_groups=mesh['tiles'=16,'pix'=2] {'pix'}, use_global_device_ids=true, to_apply=%region_3.5 | all-reduce | flops 4352 | bytes 34816 | tf_op jit(solution)/shard_map/psum | solution.py:43
  18.7 1.5 cholesky.74
  21.5 1.2 custom-call.14
  23.2 6.6 %fusion.5 = (f32[]{:T(128)}, f32[256,4096]{1,0:T(8,128)}) fusion(f32[256]{0:T(256)S(1)} %convert_element_type.10, s32[4096]{0:T(1024)S(1)} %add_select_fusion, s32[256]{0:T(256)S(1)} %copy-done.5, f32[16,256]{1,0:T(8,128)S(1)} %fusion.50, f32[16,4096]{1,0:T(8,128)S(1)} %copy-done.2, f32[4096]{0:T(1024)S(1)} %copy-done.4, bf16[256,4096]{1,0:T(8,128)(2,1)S(1)} %copy-done.6), kind=kOutput, calls=%fused_computation.15 | convolution fusion | flops 209715200 | bytes 6604804 | tf_op jit(solution)/shard_map/dot_general | solution.py:46
  29.8 41.8 %psum.73 = f32[]{:T(128)} all-reduce(f32[]{:T(128)} %get-tuple-element.16), channel_id=1, replica_groups=mesh['tiles'=16,'pix'=2] {'tiles','pix'}, use_global_device_ids=true, to_apply=%region_6.9 | all-reduce | flops 1 | bytes 8 | tf_op jit(solution)/shard_map/psum | solution.py:51
  72.3 3.4 multiply_reduce_fusion.1
  75.8 2.2 fusion.10
  78.0 0.8 pad_maximum_fusion
  79.0 41.6 %psum.72 = f32[16,16]{0,1:T(8,128)S(1)} all-reduce(f32[16,16]{0,1:T(8,128)S(1)} %fusion.24), channel_id=1, replica_groups=mesh['tiles'=16,'pix'=2] {'tiles'}, use_global_device_ids=true, to_apply=%region_4.7 | all-reduce | flops 256 | bytes 2048 | tf_op jit(solution)/shard_map/psum | solution.py:52
  120.7 1.5 cholesky.85
  123.5 1.2 custom-call.15
  124.7 62.3 %all-reduce.5.cloned.1.call-done = f32[18,4096]{1,0:T(8,128)} async-done(((f32[18,4096]{1,0:T(8,128)}), f32[18,4096]{1,0:T(8,128)}) %all-reduce.5.cloned.1.call-update) | async-done | bytes 294928 | tf_op jit(solution)/shard_map/psum | solution.py:65
  187.1 1.4 fusion.13
  188.8 1.0 fusion.28
  190.3 3.4 fusion.3
  193.7 3.7 %all-reduce = (f32[256,16]{1,0:T(8,128)S(1)}, f32[16,16]{0,1:T(8,128)S(1)}) all-reduce(f32[256,16]{1,0:T(8,128)S(1)} %fusion.3, f32[16,16]{0,1:T(8,128)S(1)} %fusion.63), channel_id=1, replica_groups=mesh['tiles'=16,'pix'=2] {'pix'}, use_global_device_ids=true, to_apply=%region_11.15 | all-reduce | flops 4352 | bytes 34816 | tf_op jit(solution)/shard_map/psum | solution.py:43
  197.5 1.5 cholesky.96
  200.3 1.2 custom-call.16
  202.0 6.6 %fusion.4 = (f32[]{:T(128)}, f32[256,4096]{1,0:T(8,128)}) fusion(f32[256]{0:T(256)S(1)} %convert_element_type.10, s32[4096]{0:T(1024)S(1)} %add_select_fusion, s32[256]{0:T(256)S(1)} %copy-done.5, f32[16,256]{1,0:T(8,128)S(1)} %fusion.43, f32[16,4096]{1,0:T(8,128)S(1)} %convolution_add_fusion.1, f32[4096]{0:T(1024)S(1)} %add.102, ...), kind=kOutput, calls=%fused_computation.14 | convolution fusion | flops 209715200 | bytes 6604804 | tf_op jit(solution)/shard_map/dot_general | solution.py:46
  208.6 39.7 %psum.78 = f32[]{:T(128)} all-reduce(f32[]{:T(128)} %get-tuple-element.18), channel_id=1, replica_groups=mesh['tiles'=16,'pix'=2] {'tiles','pix'}, use_global_device_ids=true, to_apply=%region_14.18 | all-reduce | flops 1 | bytes 8 | tf_op jit(solution)/shard_map/psum | solution.py:51
  248.9 3.4 multiply_reduce_fusion
  252.4 2.2 fusion.8
  255.5 41.2 %psum.77 = f32[16,16]{0,1:T(8,128)S(1)} all-reduce(f32[16,16]{0,1:T(8,128)S(1)} %fusion.29), channel_id=1, replica_groups=mesh['tiles'=16,'pix'=2] {'tiles'}, use_global_device_ids=true, to_apply=%region_12.16 | all-reduce | flops 256 | bytes 2048 | tf_op jit(solution)/shard_map/psum | solution.py:52
  296.8 1.5 cholesky.107
  299.6 1.2 custom-call.17
  300.8 62.7 %all-reduce.7.cloned.1.call-done = f32[18,4096]{1,0:T(8,128)} async-done(((f32[18,4096]{1,0:T(8,128)}), f32[18,4096]{1,0:T(8,128)}) %all-reduce.7.cloned.1.call-update) | async-done | bytes 294928 | tf_op jit(solution)/shard_map/psum | solution.py:65
  363.5 1.4 fusion.12
  364.9 1.1 convolution_add_fusion
  365.9 1.0 fusion.27
  (54 shorter events, 9.2 us)
Async XLA Ops:
  7.2 16.0 %copy-start.2 = (f32[16,4096]{1,0:T(8,128)S(1)}, f32[16,4096]{1,0:T(8,128)}, u32[]{:S(2)}) copy-start(f32[16,4096]{1,0:T(8,128)} %param.13) | copy-start | bytes 786436
  7.2 16.0 %copy-start.6 = (bf16[256,4096]{1,0:T(8,128)(2,1)S(1)}, bf16[256,4096]{1,0:T(8,128)(2,1)}, u32[]{:S(2)}) copy-start(bf16[256,4096]{1,0:T(8,128)(2,1)} %param.10) | copy-start | bytes 6291460
  7.2 16.0 %copy-start.4 = (f32[4096]{0:T(1024)S(1)}, f32[4096]{0:T(1024)}, u32[]{:S(2)}) copy-start(f32[4096]{0:T(1024)} %param.14) | copy-start | bytes 49156
  7.2 16.0 %copy-start.5 = (s32[256]{0:T(256)S(1)}, s32[256]{0:T(256)}, u32[]{:S(2)}) copy-start(s32[256]{0:T(256)} %param.12) | copy-start | bytes 3076
  7.2 179.8 %all-reduce.5.cloned.1.call-start = ((), (), s32[]{:S(2)}) async-start(), calls=%async_computation | async-start | bytes 786432 | tf_op jit(solution)/shard_map/psum | solution.py:65
  72.3 3.5 copy-start.1
  78.8 284.7 %all-reduce.7.cloned.1.call-start = ((), (), s32[]{:S(2)}) async-start(), calls=%async_computation.1 | async-start | bytes 786432 | tf_op jit(solution)/shard_map/psum | solution.py:65
  201.9 53.4 %copy-start.3 = (f32[16,256]{1,0:T(8,128)}, f32[16,256]{1,0:T(8,128)S(1)}, u32[]{:S(2)}) copy-start(f32[16,256]{1,0:T(8,128)S(1)} %fusion.43) | copy-start | bytes 49156
  248.9 3.5 copy-start
Sparse Core Ops, SparseCore 0:
  78.9 108.0 all-reduce.4
  255.5 107.9 all-reduce.6
where the time goes:
time: 375 us; the launch traced here: 374 us
  blocking collectives  172 us (46%)
  waiting for transfers between devices  125 us (33%)
  matrix products  33.2 us (9%)
  other arithmetic  27.9 us (7%)
  between operations  15.6 us (4%)
    psum x2, waiting for transfers between devices, local(): totals = lax.psum(column_terms, 'tiles')  125 us
    psum x2, blocking collectives, local(): coef_total = lax.psum(local_coef_gram, 'tiles')  82.8 us
    psum x2, blocking collectives, local(): square_total = lax.psum(local_square, ('tiles', 'pix'))  81.5 us
    dot_general x2, matrix products, local(): residual = shifted - jnp.dot(coefficients, basis, precision=precise)  13.2 us
    another operation x12, other arithmetic, solve_gram(): factor = jnp.linalg.cholesky(gram_matrix)  8.52 us
    dot_general x2, matrix products, local(): local_proj = jnp.dot(shifted, basis.T, precision=precise)  8.4 us
    psum x2, blocking collectives, local(): gram_total, proj_total = lax.psum((local_gram, local_proj), 'pix')  7.79 us
    another operation x8, other arithmetic, solve_gram(): return jax.scipy.linalg.cho_solve((factor, True), right_rows)  7.51 us
  transfers between devices with their start and end apart: 2, of which 2 were waited for; matrix products, arithmetic and copies ran while one was open for 2% of the time, Pallas kernels for 0%

commit v1 on v0

v1 whole, which is shorter than its diff:
```python
import functools

import jax
import jax.numpy as jnp
from jax import lax
from jax.experimental import pallas as pl
from jax.experimental.pallas import tpu as pltpu
from jax.sharding import PartitionSpec as P

ROW_PX = 2048
BLOCK = 128
ITERS = 2
RIDGE = 0.01
VMEM_LIMIT = 48 * 1024 * 1024

F32 = jnp.float32
BF16 = jnp.bfloat16
NT = (((1,), (1,)), ((), ()))


def params():
    return pltpu.CompilerParams(vmem_limit_bytes=VMEM_LIMIT)


def vmem(n):
    return [pl.BlockSpec(memory_space=pltpu.VMEM)] * n


SMEM = pl.BlockSpec(memory_space=pltpu.SMEM)


def split3(x):
    hi = x.astype(BF16)
    rest = x - hi.astype(F32)
    mid = rest.astype(BF16)
    low = (rest - mid.astype(F32)).astype(BF16)
    return hi, mid, low


def eliminate(a, first, count):
    rows = lax.broadcasted_iota(jnp.int32, a.shape, 0)
    for k in range(count):
        column = a[:, first + k : first + k + 1]
        pivot = a[k : k + 1, first + k : first + k + 1]
        scaled = a[k : k + 1, :] * (1.0 / pivot)
        a = jnp.where(rows == k, scaled, a - column * scaled)
    return a


def eye_at(shape, first):
    row = lax.broadcasted_iota(jnp.int32, shape, 0)
    col = lax.broadcasted_iota(jnp.int32, shape, 1)
    return (col == row + first).astype(F32)


class Sizes:
    def __init__(self, tile_dev, pix_dev, rank, n_tiles, n_pix):
        self.tile_dev, self.pix_dev, self.rank = tile_dev, pix_dev, rank
        self.n_tiles, self.n_pix = n_tiles, n_pix
        self.tiles_all, self.pixels_all = tile_dev * n_tiles, pix_dev * n_pix
        self.tile_levels = levels(n_tiles)
        self.group = len(self.tile_levels[0]) + 1 if self.tile_levels else 1
        self.chunk = pix_dev // self.group
        self.blocks = self.chunk // BLOCK
        self.extra = BLOCK * (-(-2 * self.blocks // rank))
        self.stack = 6 * rank + 16


def levels(n):
    if n & (n - 1):
        return None
    out, bit = [], 1
    while bit < n:
        out.append((bit, 2 * bit, 3 * bit) if 4 * bit <= n else (bit,))
        bit *= 4
    return out


def partner(x, axis, mask):
    n = lax.axis_size(axis)
    return lax.ppermute(x, axis, [(i, i ^ mask) for i in range(n)])


def tree(parts):
    while len(parts) > 1:
        parts = [a + b for a, b in zip(parts[::2], parts[1::2])]
    return parts[0]


def sum_level(x, axis, masks):
    return tree([x] + [partner(x, axis, m) for m in masks])


def stack_block(sz, stack_ref, offset, b, d_rows):
    r = sz.rank
    hi, mid, low = split3(b)
    span = pl.ds(offset, b.shape[1])
    for at, part in enumerate((hi, mid, low, hi, mid, hi)):
        stack_ref[at * r : (at + 1) * r, span] = part
    for j, d in enumerate(d_rows):
        at = pl.ds(offset + j * BLOCK, BLOCK)
        d_hi, d_mid, d_low = split3(d)
        row = lax.broadcasted_iota(jnp.int32, (16, BLOCK), 0)
        tile = jnp.where(
            row == 0,
            d_hi.astype(F32),
            jnp.where(row == 1, d_mid.astype(F32), jnp.where(row == 2, d_low.astype(F32), 0.0)),
        )
        stack_ref[6 * r : 6 * r + 16, at] = tile.astype(BF16)


def project_chunk(sz, f_ref, stack_ref, offset, b, d_rows, totals):
    r = sz.rank
    stack_block(sz, stack_ref, offset, b, d_rows)
    span = pl.ds(offset, b.shape[1])
    parts = stack_ref[0 : 3 * r, span]
    proj = lax.dot_general(parts, f_ref[:, span], NT, preferred_element_type=F32)
    gram = lax.dot_general(parts, parts, NT, preferred_element_type=F32)
    dark = None
    for j, d in enumerate(d_rows):
        term = b[:, j * BLOCK : (j + 1) * BLOCK] * d
        dark = term if dark is None else dark + term
    new = (proj, gram, dark)
    return new if totals is None else tuple(a + b for a, b in zip(totals, new))


def pack_projections(sz, totals, packed_ref):
    r, td = sz.rank, sz.tile_dev
    proj, gram, dark = totals
    proj = proj[0:r] + proj[r : 2 * r] + proj[2 * r : 3 * r]
    gram = gram[0:r] + gram[r : 2 * r] + gram[2 * r : 3 * r]
    gram = gram[:, 0:r] + gram[:, r : 2 * r] + gram[:, 2 * r : 3 * r]
    packed_ref[:, 0:td] = proj - jnp.sum(dark, axis=1, keepdims=True)
    packed_ref[:, td : td + BLOCK] = jnp.zeros((r, BLOCK), F32)
    packed_ref[:, td : td + r] = gram


def first_projection(sz, me_ref, f_ref, b_ref, d_ref, valid_ref, fore_ref, packed_ref, stack_ref, own_ref, least_ref):
    totals = None
    for c in range(sz.group):
        at = c * sz.chunk
        d_rows = [d_ref[c * sz.blocks + j : c * sz.blocks + j + 1, :] for j in range(sz.blocks)]
        totals = project_chunk(sz, f_ref, stack_ref, at, b_ref[:, at : at + sz.chunk], d_rows, totals)
    pack_projections(sz, totals, packed_ref)
    me = me_ref[0]
    own_ref[:, 0 : sz.chunk] = b_ref[:, pl.ds(pl.multiple_of(me * sz.chunk, BLOCK), sz.chunk)]
    own_ref[:, sz.chunk :] = jnp.zeros((sz.rank, sz.extra), F32)
    for j in range(sz.blocks):
        own_ref[j % sz.rank, pl.ds(sz.chunk + j // sz.rank * BLOCK, BLOCK)] = d_ref[me * sz.blocks + j, :]
    least = jnp.where(valid_ref[...] != 0, fore_ref[...], ROW_PX)
    least_ref[...] = jnp.broadcast_to(least, (BLOCK, sz.tile_dev)).T


def later_projection(sz, me_ref, f_ref, *refs):
    chunks, (packed_ref, stack_ref) = refs[: sz.group], refs[sz.group :]
    me = me_ref[0]
    totals = None
    for k, ref in enumerate(chunks):
        at = pl.multiple_of((me ^ k) * sz.chunk, BLOCK)
        d_rows = [
            ref[j % sz.rank : j % sz.rank + 1, sz.chunk + j // sz.rank * BLOCK : sz.chunk + (j // sz.rank + 1) * BLOCK]
            for j in range(sz.blocks)
        ]
        totals = project_chunk(sz, f_ref, stack_ref, at, ref[:, 0 : sz.chunk], d_rows, totals)
    pack_projections(sz, totals, packed_ref)


def residual(sz, f_ref, stack_ref, parts, offset, width):
    span = pl.ds(offset, width)
    model = lax.dot_general(
        parts, stack_ref[:, span], (((1,), (0,)), ((), ())), preferred_element_type=F32
    )
    return f_ref[:, span].astype(F32) - model


def solve_tiles(sz, width, *refs):
    packed = refs[: sz.n_pix]
    f_ref, stack_ref, least_ref, valid_ref, coef_ref, parts_ref, note_ref = refs[sz.n_pix :]
    r, td = sz.rank, sz.tile_dev
    a = tree([ref[...] for ref in packed]) / sz.pixels_all
    a = a + RIDGE * eye_at(a.shape, td)
    coef = eliminate(a, td, r)[:, 0:td]
    coef_ref[...] = coef
    hi, mid, low = split3(coef)
    row = lax.broadcasted_iota(jnp.int32, (BLOCK - 6 * r, td), 0)
    ones = (row < 3).astype(F32)
    hi, mid, low = hi.astype(F32), mid.astype(F32), low.astype(F32)
    parts = jnp.concatenate([hi, hi, hi, mid, mid, low, ones], axis=0).T.astype(BF16)
    parts_ref[...] = parts
    parts = parts[:, 0 : sz.stack]
    least = least_ref[...]

    def body(step, total):
        offset = pl.multiple_of(step * width, BLOCK)
        res = residual(sz, f_ref, stack_ref, parts, offset, width)
        square = res * res
        for j in range(width // BLOCK):
            block = (step * (width // BLOCK) + j) % (ROW_PX // BLOCK)
            term = jnp.where(least <= block, square[:, j * BLOCK : (j + 1) * BLOCK], 0.0)
            total = total + jnp.sum(term.reshape(td // 8, 8, BLOCK), axis=0)
        return total

    total = lax.fori_loop(0, sz.pix_dev // width, body, jnp.zeros((8, BLOCK), F32))
    total = jnp.sum(jnp.sum(total, axis=0, keepdims=True), axis=1, keepdims=True)
    held = coef * (valid_ref[...] != 0).astype(F32)
    gram = lax.dot_general(held, coef, NT, precision=lax.Precision.HIGHEST, preferred_element_type=F32)
    note_ref[...] = jnp.zeros((r, BLOCK), F32)
    note_ref[:, 0:r] = gram
    note_ref[0:1, r : r + 1] = total


def invert_gram(sz, note_ref, inverse_ref):
    r = sz.rank
    gram = note_ref[:, 0:r] / sz.tiles_all + RIDGE * eye_at((r, r), 0)
    a = jnp.concatenate([gram, eye_at((r, BLOCK - r), 0)], axis=1)
    inverse_ref[...] = eliminate(a, 0, r)


def update_terms(sz, width, me_ref, *refs):
    notes = refs[: sz.n_pix]
    f_ref, stack_ref, least_ref, coef_ref, parts_ref = refs[sz.n_pix : sz.n_pix + 5]
    outs = refs[sz.n_pix + 5 :]
    r, td = sz.rank, sz.tile_dev
    me = me_ref[0]
    total = tree([ref[0:1, r : r + 1] for ref in notes])
    spread = total / (sz.tiles_all * sz.pixels_all) + 1e-05
    scale = jnp.broadcast_to(1.0 / (4.0 * spread), (8, BLOCK))[0:1, :]
    parts = parts_ref[:, 0 : sz.stack]
    hi, mid, low = split3(coef_ref[...])
    three = jnp.concatenate([hi, mid, low], axis=0)
    least = least_ref[...]
    steps = sz.chunk // width
    for k, out_ref in enumerate(outs):
        start = (me ^ k) * sz.chunk
        for step in range(steps):
            offset = pl.multiple_of(start + step * width, BLOCK)
            res = residual(sz, f_ref, stack_ref, parts, offset, width)
            hi_parts, mid_parts = [], []
            for j in range(width // BLOCK):
                block = (offset // BLOCK + j) % (ROW_PX // BLOCK)
                x = res[:, j * BLOCK : (j + 1) * BLOCK]
                t = x * x * scale + 1.0
                g = pl.reciprocal(t, approx=True)
                g = g * (2.0 - t * g)
                g = jnp.where(least <= block, g, 0.0)
                w = g * x
                w_hi = w.astype(BF16)
                hi_parts.append(w_hi)
                mid_parts.append((w - w_hi.astype(F32)).astype(BF16))
                at = step * (width // BLOCK) + j
                for flat, value in ((at, w), (sz.blocks + at, g)):
                    lane = sz.chunk + flat // r * BLOCK
                    out_ref[flat % r : flat % r + 1, lane : lane + BLOCK] = jnp.sum(value, axis=0, keepdims=True)
            nn = (((1,), (0,)), ((), ()))
            terms = lax.dot_general(three, jnp.concatenate(hi_parts, axis=1), nn, preferred_element_type=F32)
            more = lax.dot_general(three[0 : 2 * r], jnp.concatenate(mid_parts, axis=1), nn, preferred_element_type=F32)
            out_ref[:, step * width : (step + 1) * width] = (
                terms[0:r] + (terms[r : 2 * r] + terms[2 * r : 3 * r] + more[0:r] + more[r : 2 * r])
            )
    used = 2 * sz.blocks
    if used % r:
        for out_ref in outs:
            out_ref[used % r :, sz.chunk + used // r * BLOCK :] = jnp.zeros((r - used % r, BLOCK), F32)


def update_chunk(sz, inverse_ref, old_ref, *refs):
    total_refs, new_ref = refs[:-1], refs[-1]
    r = sz.rank
    totals = tree([ref[...] for ref in total_refs])
    inverse = inverse_ref[:, r : 2 * r]
    change = jnp.dot(inverse, totals[:, 0 : sz.chunk] / sz.tiles_all, precision=lax.Precision.HIGHEST, preferred_element_type=F32)
    new_ref[:, 0 : sz.chunk] = old_ref[:, 0 : sz.chunk] + change
    new_ref[:, sz.chunk :] = jnp.zeros((r, sz.extra), F32)

    def place(flat):
        return flat % r, sz.chunk + flat // r * BLOCK

    many = 8 if sz.blocks % 8 == 0 else 1
    for j in range(0, sz.blocks, many):
        (row, lane), (row_g, lane_g) = place(j), place(sz.blocks + j)
        w = totals[row : row + many, lane : lane + BLOCK]
        g = totals[row_g : row_g + many, lane_g : lane_g + BLOCK]
        new_ref[row : row + many, lane : lane + BLOCK] = (
            old_ref[row : row + many, lane : lane + BLOCK] + w / (g + 1.0)
        )


def assemble(sz, me_ref, *refs):
    chunks, (b_ref, d_ref) = refs[: sz.group], refs[sz.group :]
    me = me_ref[0]
    for k, ref in enumerate(chunks):
        c = me ^ k
        b_ref[:, pl.ds(pl.multiple_of(c * sz.chunk, BLOCK), sz.chunk)] = ref[:, 0 : sz.chunk]
        for j in range(sz.blocks):
            lane = sz.chunk + j // sz.rank * BLOCK
            d_ref[c * sz.blocks + j, :] = ref[j % sz.rank, lane : lane + BLOCK]


def call(body, outs, ins, smem=0, cost=None):
    return pl.pallas_call(
        body,
        out_shape=[jax.ShapeDtypeStruct(s, t) for s, t in outs],
        in_specs=[SMEM] * smem + vmem(len(ins) - smem),
        out_specs=vmem(len(outs)),
        compiler_params=params(),
    )(*ins)


def local(frames, tile_valid, foreground_blocks, basis_start, dark_start):
    td, pd = frames.shape
    r = basis_start.shape[0]
    sz = Sizes(td, pd, r, lax.axis_size("tiles"), lax.axis_size("pix"))
    pix_masks = [m for m in range(1, sz.n_pix)]
    me = (lax.axis_index("tiles") & (sz.group - 1)).astype(jnp.int32).reshape(1)
    valid = tile_valid.reshape(1, td)
    fore = foreground_blocks.reshape(1, td)
    width = min(512, sz.chunk)
    chunk_shape = (r, sz.chunk + sz.extra)
    packed_out = ((r, td + BLOCK), F32)
    stack_out = ((sz.stack, pd), BF16)
    masks = sz.tile_levels[0]
    for iteration in range(ITERS):
        if iteration == 0:
            packed, stack, old, least = call(
                functools.partial(first_projection, sz),
                [packed_out, stack_out, (chunk_shape, F32), ((td, BLOCK), jnp.int32)],
                [me, frames, basis_start, dark_start.reshape(pd // BLOCK, BLOCK), valid, fore],
                smem=1,
            )
        else:
            packed, stack = call(
                functools.partial(later_projection, sz), [packed_out, stack_out], [me, frames] + chunks, smem=1
            )
        both = [packed] + [partner(packed, "pix", m) for m in pix_masks]
        coef, parts, note = call(
            functools.partial(solve_tiles, sz, width),
            [((r, td), F32), ((td, BLOCK), BF16), ((r, BLOCK), F32)],
            both + [frames, stack, least, valid],
        )
        for level in sz.tile_levels:
            note = sum_level(note, "tiles", level)
        (inverse,) = call(functools.partial(invert_gram, sz), [((r, BLOCK), F32)], [note])
        notes = [note] + [partner(note, "pix", m) for m in pix_masks]
        terms = call(
            functools.partial(update_terms, sz, width),
            [(chunk_shape, F32)] * sz.group,
            [me] + notes + [frames, stack, least, coef, parts],
            smem=1,
        )
        total = tree([terms[0]] + [partner(terms[k], "tiles", m) for k, m in enumerate(masks, 1)])
        later = sz.tile_levels[1:]
        for level in later[:-1]:
            total = sum_level(total, "tiles", level)
        totals = [total] + [partner(total, "tiles", m) for m in (later[-1] if later else ())]
        (old,) = call(functools.partial(update_chunk, sz), [(chunk_shape, F32)], [inverse, old] + totals)
        chunks = [old] + [partner(old, "tiles", m) for m in masks]
    basis, dark = call(
        functools.partial(assemble, sz), [((r, pd), F32), ((pd // BLOCK, BLOCK), F32)], [me] + chunks, smem=1
    )
    return basis, dark.reshape(pd), coef.T


def solution(mesh):
    return jax.shard_map(
        local,
        mesh=mesh,
        in_specs=(P("tiles", "pix"), P("tiles"), P("tiles"), P(None, "pix"), P("pix")),
        out_specs=(P(None, "pix"), P("pix"), P("tiles", None)),
        check_vma=False,
    )
```

time: 375 us -> 109 us (0.29)
  blocking collectives: 172 us -> 0 us
  waiting for transfers between devices: 125 us -> 41.4 us
  starting transfers between devices: 0.08 us -> 40.2 us
  matrix products: 33.2 us -> 0 us
  other arithmetic: 27.9 us -> 0.06 us
  Pallas kernels: 0 us -> 20.8 us
  between operations: 15.6 us -> 0.79 us
  local copies, waits for them, and re-layouts: 0.41 us -> 5.33 us
    psum x6 -> x0, blocking collectives: 172 us -> none  [the longest x2 82.8 us: local(): coef_total = lax.psum(local_coef_gram, 'tiles')]
    psum x2 -> x0, waiting for transfers between devices: 125 us -> none  [local(): totals = lax.psum(column_terms, 'tiles')]
    ppermute x0 -> x34, waiting for transfers between devices: none -> 41.4 us  [partner(): return lax.ppermute(x, axis, [(i, i ^ mask) for i in range(n)])]
    ppermute x0 -> x34, starting transfers between devices: none -> 40.2 us  [partner(): return lax.ppermute(x, axis, [(i, i ^ mask) for i in range(n)])]
    dot_general x10 -> x0, matrix products: 28.3 us -> none  [the longest x2 13.2 us: local(): residual = shifted - jnp.dot(coefficients, basis, precision=precise)]
    pallas_call x0 -> x11, Pallas kernels: none -> 20.8 us  [call(): pl.pallas_call(body, out_shape=[jax.ShapeDtypeStruct(s, t) for s, t in ou...]
    another operation x20 -> x0, other arithmetic: 16 us -> none  [the longest x12 8.52 us: solve_gram(): factor = jnp.linalg.cholesky(gram_matrix)]
    reduce_sum x2 -> x0, other arithmetic: 6.79 us -> none  [local(): jnp.sum(weighted, axis=0, keepdims=True)]
  transfers between devices with their start and end apart: 2 -> 34, of which waited for: 2 -> 28; matrix products, arithmetic and copies ran while one was open for 2% -> 0% of each run, Pallas kernels for 0% -> 2%
where the time goes in v1:
time: 109 us
  waiting for transfers between devices  41.4 us (38%)
  starting transfers between devices  40.2 us (37%)
  Pallas kernels  20.8 us (19%)
  local copies, waits for them, and re-layouts  5.33 us (5%)
    ppermute x34, waiting for transfers between devices, partner(): return lax.ppermute(x, axis, [(i, i ^ mask) for i in range(n)])  41.4 us
    ppermute x34, starting transfers between devices, partner(): return lax.ppermute(x, axis, [(i, i ^ mask) for i in range(n)])  40.2 us
    pallas_call x11, Pallas kernels, call(): pl.pallas_call(body, out_shape=[jax.ShapeDtypeStruct(s, t) for s, t in ou...  20.8 us
    unnamed x14, local copies, waits for them, and re-layouts  5.33 us
  transfers between devices with their start and end apart: 34, of which 28 were waited for; matrix products, arithmetic and copies ran while one was open for 0% of the time, Pallas kernels for 2%

profile of v1, /device:TPU:0, one launch (start us, length us, event | category | flops | bytes accessed | tf_op | source)
XLA Modules:
  0.0 108.6 jit_solution(17603038804078028580)
XLA Ops:
  0.6 1.6 %copy-done = bf16[256,4096]{1,0:T(8,128)(2,1)S(1)} copy-done((bf16[256,4096]{1,0:T(8,128)(2,1)S(1)}, bf16[256,4096]{1,0:T(8,128)(2,1)}, u32[]{:S(2)}) %copy-start) | copy-done | bytes 2097176
  7.7 3.4 %shard_map.77 = (f32[16,256]{1,0:T(8,128)S(1)}, bf16[256,128]{1,0:T(8,128)(2,1)S(1)}, f32[16,128]{1,0:T(8,128)S(1)}) custom-call(f32[16,384]{1,0:T(8,128)S(1)} %get-tuple-element.25.refs_0_, f32[16,384]{1,0:T(8,128)S(1)} %collective-permute-done.refs_1_, bf16[256,4096]{1,0:T(8,128)(2,1)S(1)} %copy-done.1, bf16[112,4096]{1,0:T(8,128)(2,1)S(1)} %get-tuple-element.26.refs_3_, ...), custom_call_target="tpu_custom_call" | custom-call | tf_op jit(solution)/shard_map/pallas_call | solution.py:300
  11.1 2.9 %collective-permute-start.1 = (f32[16,128]{1,0:T(8,128)S(1)}, f32[16,128]{1,0:T(8,128)S(1)}, u32[]{:S(2)}, u32[]{:S(2)}) collective-permute-start(f32[16,128]{1,0:T(8,128)S(1)} %get-tuple-element.28), channel_id=1, source_target_pairs={{0,2},{2,0},{4,6},{6,4},{8,10},{10,8},{12,14},{14,12},{16,18},{18,... | collective-permute-start | bytes 24584 | tf_op jit(solution)/shard_map/ppermute | solution.py:81
  14.0 1.5 %collective-permute-start.2 = (f32[16,128]{1,0:T(8,128)S(1)}, f32[16,128]{1,0:T(8,128)S(1)}, u32[]{:S(2)}, u32[]{:S(2)}) collective-permute-start(f32[16,128]{1,0:T(8,128)S(1)} %get-tuple-element.28), channel_id=1, source_target_pairs={{0,4},{2,6},{4,0},{6,2},{8,12},{10,14},{12,8},{14,10},{16,20},{18,... | collective-permute-start | bytes 24584 | tf_op jit(solution)/shard_map/ppermute | solution.py:81
  15.6 2.0 %collective-permute-done.2 = f32[16,128]{1,0:T(8,128)S(1)} collective-permute-done((f32[16,128]{1,0:T(8,128)S(1)}, f32[16,128]{1,0:T(8,128)S(1)}, u32[]{:S(2)}, u32[]{:S(2)}) %collective-permute-start.2) | collective-permute-done | bytes 8224 | tf_op jit(solution)/shard_map/ppermute | solution.py:81
  17.7 2.4 %collective-permute-done.3 = f32[16,128]{1,0:T(8,128)S(1)} collective-permute-done((f32[16,128]{1,0:T(8,128)S(1)}, f32[16,128]{1,0:T(8,128)S(1)}, u32[]{:S(2)}, u32[]{:S(2)}) %collective-permute-start.3) | collective-permute-done | bytes 8224 | tf_op jit(solution)/shard_map/ppermute | solution.py:81
  20.1 1.6 %collective-permute-start.4 = (f32[16,128]{1,0:T(8,128)S(1)}, f32[16,128]{1,0:T(8,128)S(1)}, u32[]{:S(2)}, u32[]{:S(2)}) collective-permute-start(f32[16,128]{1,0:T(8,128)S(1)} %add_add_fusion.5), channel_id=1, source_target_pairs={{0,8},{2,10},{4,12},{6,14},{8,0},{10,2},{12,4},{14,6},{16,24},{18,... | collective-permute-start | bytes 24584 | tf_op jit(solution)/shard_map/ppermute | solution.py:81
  21.7 2.6 %collective-permute-start.5 = (f32[16,128]{1,0:T(8,128)S(1)}, f32[16,128]{1,0:T(8,128)S(1)}, u32[]{:S(2)}, u32[]{:S(2)}) collective-permute-start(f32[16,128]{1,0:T(8,128)S(1)} %add_add_fusion.5), channel_id=1, source_target_pairs={{0,16},{2,18},{4,20},{6,22},{8,24},{10,26},{12,28},{14,30},{16,0},... | collective-permute-start | bytes 24584 | tf_op jit(solution)/shard_map/ppermute | solution.py:81
  24.5 1.7 %collective-permute-done.5 = f32[16,128]{1,0:T(8,128)S(1)} collective-permute-done((f32[16,128]{1,0:T(8,128)S(1)}, f32[16,128]{1,0:T(8,128)S(1)}, u32[]{:S(2)}, u32[]{:S(2)}) %collective-permute-start.5) | collective-permute-done | bytes 8224 | tf_op jit(solution)/shard_map/ppermute | solution.py:81
  26.2 3.5 %collective-permute-done.6 = f32[16,128]{1,0:T(8,128)S(1)} collective-permute-done((f32[16,128]{1,0:T(8,128)S(1)}, f32[16,128]{1,0:T(8,128)S(1)}, u32[]{:S(2)}, u32[]{:S(2)}) %collective-permute-start.6) | collective-permute-done | bytes 8224 | tf_op jit(solution)/shard_map/ppermute | solution.py:81
  30.9 3.8 %shard_map.79 = (f32[16,1152]{1,0:T(8,128)S(1)}, f32[16,1152]{1,0:T(8,128)S(1)}, f32[16,1152]{1,0:T(8,128)S(1)}, f32[16,1152]{1,0:T(8,128)S(1)}) custom-call(s32[1]{0:T(128)} %bitcast.me_ref, f32[16,128]{1,0:T(8,128)S(1)} %add_add_fusion.4.note_ref.refs_0_, f32[16,128]{1,0:T(8,128)S(1)} %collective-permute-done.7.refs_1_, bf16[256,4096]{1,0:T(8,128)(2,1)S(1)} %copy-done.1, ...), custom_call_target="tpu_custom_call" | custom-call | tf_op jit(solution)/shard_map/pallas_call | solution.py:300
  35.2 1.5 %collective-permute-start.8 = (f32[16,1152]{1,0:T(8,128)S(1)}, f32[16,1152]{1,0:T(8,128)S(1)}, u32[]{:S(2)}, u32[]{:S(2)}) collective-permute-start(f32[16,1152]{1,0:T(8,128)S(1)} %get-tuple-element.33), channel_id=1, source_target_pairs={{0,2},{2,0},{4,6},{6,4},{8,10},{10,8},{12,14},{14,12},{16,18},{18,... | collective-permute-start | bytes 221192 | tf_op jit(solution)/shard_map/ppermute | solution.py:81
  36.7 1.5 %collective-permute-start.9 = (f32[16,1152]{1,0:T(8,128)S(1)}, f32[16,1152]{1,0:T(8,128)S(1)}, u32[]{:S(2)}, u32[]{:S(2)}) collective-permute-start(f32[16,1152]{1,0:T(8,128)S(1)} %get-tuple-element.34), channel_id=1, source_target_pairs={{0,4},{2,6},{4,0},{6,2},{8,12},{10,14},{12,8},{14,10},{16,20},{18,... | collective-permute-start | bytes 221192 | tf_op jit(solution)/shard_map/ppermute | solution.py:81
  38.2 2.5 %collective-permute-done.10 = f32[16,1152]{1,0:T(8,128)S(1)} collective-permute-done((f32[16,1152]{1,0:T(8,128)S(1)}, f32[16,1152]{1,0:T(8,128)S(1)}, u32[]{:S(2)}, u32[]{:S(2)}) %collective-permute-start.10) | collective-permute-done | bytes 73760 | tf_op jit(solution)/shard_map/ppermute | solution.py:81
  42.4 3.6 %collective-permute-start.13 = (f32[16,1152]{1,0:T(8,128)S(1)}, f32[16,1152]{1,0:T(8,128)S(1)}, u32[]{:S(2)}, u32[]{:S(2)}) collective-permute-start(f32[16,1152]{1,0:T(8,128)S(1)} %add_add_fusion.1.refs_0_), channel_id=1, source_target_pairs={{0,24},{2,26},{4,28},{6,30},{8,16},{10,18},{12,20},{14,22},{16,8},... | collective-permute-start | bytes 221192 | tf_op jit(solution)/shard_map/ppermute | solution.py:81
  47.3 2.9 %collective-permute-done.12.refs_2_ = f32[16,1152]{1,0:T(8,128)S(1)} collective-permute-done((f32[16,1152]{1,0:T(8,128)S(1)}, f32[16,1152]{1,0:T(8,128)S(1)}, u32[]{:S(2)}, u32[]{:S(2)}) %collective-permute-start.12) | collective-permute-done | bytes 73760 | tf_op jit(solution)/shard_map/ppermute | solution.py:81
  51.6 2.4 %collective-permute-start.16 = (f32[16,1152]{1,0:T(8,128)S(1)}, f32[16,1152]{1,0:T(8,128)S(1)}, u32[]{:S(2)}, u32[]{:S(2)}) collective-permute-start(f32[16,1152]{1,0:T(8,128)S(1)} %shard_map.80.refs_0_.old_ref), channel_id=1, source_target_pairs={{0,6},{2,4},{4,2},{6,0},{8,14},{10,12},{12,10},{14,8},{16,22},{18,... | collective-permute-start | bytes 221192 | tf_op jit(solution)/shard_map/ppermute | solution.py:81
  59.0 4.0 %shard_map.82 = (f32[16,256]{1,0:T(8,128)}, bf16[256,128]{1,0:T(8,128)(2,1)S(1)}, f32[16,128]{1,0:T(8,128)S(1)}) custom-call(f32[16,384]{1,0:T(8,128)S(1)} %get-tuple-element.36.refs_0_, f32[16,384]{1,0:T(8,128)S(1)} %collective-permute-done.17.refs_1_, bf16[256,4096]{1,0:T(8,128)(2,1)S(1)} %copy-done.1, bf16[112,4096]{1,0:T(8,128)(2,1)S(1)} %get-tuple-element.37.refs_3_, ...), custom_call_target="tpu_custom_call" | custom-call | tf_op jit(solution)/shard_map/pallas_call | solution.py:300
  63.0 1.6 %collective-permute-start.18 = (f32[16,128]{1,0:T(8,128)S(1)}, f32[16,128]{1,0:T(8,128)S(1)}, u32[]{:S(2)}, u32[]{:S(2)}) collective-permute-start(f32[16,128]{1,0:T(8,128)S(1)} %get-tuple-element.38), channel_id=1, source_target_pairs={{0,2},{2,0},{4,6},{6,4},{8,10},{10,8},{12,14},{14,12},{16,18},{18,... | collective-permute-start | bytes 24584 | tf_op jit(solution)/shard_map/ppermute | solution.py:81
  66.7 1.6 %collective-permute-done.19 = f32[16,128]{1,0:T(8,128)S(1)} collective-permute-done((f32[16,128]{1,0:T(8,128)S(1)}, f32[16,128]{1,0:T(8,128)S(1)}, u32[]{:S(2)}, u32[]{:S(2)}) %collective-permute-start.19) | collective-permute-done | bytes 8224 | tf_op jit(solution)/shard_map/ppermute | solution.py:81
  68.3 2.3 %collective-permute-done.20 = f32[16,128]{1,0:T(8,128)S(1)} collective-permute-done((f32[16,128]{1,0:T(8,128)S(1)}, f32[16,128]{1,0:T(8,128)S(1)}, u32[]{:S(2)}, u32[]{:S(2)}) %collective-permute-start.20) | collective-permute-done | bytes 8224 | tf_op jit(solution)/shard_map/ppermute | solution.py:81
  73.1 1.8 %collective-permute-start.23 = (f32[16,128]{1,0:T(8,128)S(1)}, f32[16,128]{1,0:T(8,128)S(1)}, u32[]{:S(2)}, u32[]{:S(2)}) collective-permute-start(f32[16,128]{1,0:T(8,128)S(1)} %add_add_fusion.3), channel_id=1, source_target_pairs={{0,24},{2,26},{4,28},{6,30},{8,16},{10,18},{12,20},{14,22},{16,8},... | collective-permute-start | bytes 24584 | tf_op jit(solution)/shard_map/ppermute | solution.py:81
  75.0 1.5 %collective-permute-done.22 = f32[16,128]{1,0:T(8,128)S(1)} collective-permute-done((f32[16,128]{1,0:T(8,128)S(1)}, f32[16,128]{1,0:T(8,128)S(1)}, u32[]{:S(2)}, u32[]{:S(2)}) %collective-permute-start.22) | collective-permute-done | bytes 8224 | tf_op jit(solution)/shard_map/ppermute | solution.py:81
  76.5 2.1 %collective-permute-done.23 = f32[16,128]{1,0:T(8,128)S(1)} collective-permute-done((f32[16,128]{1,0:T(8,128)S(1)}, f32[16,128]{1,0:T(8,128)S(1)}, u32[]{:S(2)}, u32[]{:S(2)}) %collective-permute-start.23) | collective-permute-done | bytes 8224 | tf_op jit(solution)/shard_map/ppermute | solution.py:81
  80.5 3.8 %shard_map.84 = (f32[16,1152]{1,0:T(8,128)S(1)}, f32[16,1152]{1,0:T(8,128)S(1)}, f32[16,1152]{1,0:T(8,128)S(1)}, f32[16,1152]{1,0:T(8,128)S(1)}) custom-call(s32[1]{0:T(128)} %bitcast.me_ref, f32[16,128]{1,0:T(8,128)S(1)} %add_add_fusion.2.note_ref.refs_0_, f32[16,128]{1,0:T(8,128)S(1)} %collective-permute-done.24.refs_1_, bf16[256,4096]{1,0:T(8,128)(2,1)S(1)} %copy-done.1, ...), custom_call_target="tpu_custom_call" | custom-call | tf_op jit(solution)/shard_map/pallas_call | solution.py:300
  85.8 2.0 %collective-permute-start.27 = (f32[16,1152]{1,0:T(8,128)S(1)}, f32[16,1152]{1,0:T(8,128)S(1)}, u32[]{:S(2)}, u32[]{:S(2)}) collective-permute-start(f32[16,1152]{1,0:T(8,128)S(1)} %get-tuple-element.44), channel_id=1, source_target_pairs={{0,6},{2,4},{4,2},{6,0},{8,14},{10,12},{12,10},{14,8},{16,22},{18,... | collective-permute-start | bytes 221192 | tf_op jit(solution)/shard_map/ppermute | solution.py:81
  91.1 2.2 %collective-permute-start.29 = (f32[16,1152]{1,0:T(8,128)S(1)}, f32[16,1152]{1,0:T(8,128)S(1)}, u32[]{:S(2)}, u32[]{:S(2)}) collective-permute-start(f32[16,1152]{1,0:T(8,128)S(1)} %add_add_fusion.refs_0_), channel_id=1, source_target_pairs={{0,16},{2,18},{4,20},{6,22},{8,24},{10,26},{12,28},{14,30},{16,0},... | collective-permute-start | bytes 221192 | tf_op jit(solution)/shard_map/ppermute | solution.py:81
  93.3 2.2 %collective-permute-start.30 = (f32[16,1152]{1,0:T(8,128)S(1)}, f32[16,1152]{1,0:T(8,128)S(1)}, u32[]{:S(2)}, u32[]{:S(2)}) collective-permute-start(f32[16,1152]{1,0:T(8,128)S(1)} %add_add_fusion.refs_0_), channel_id=1, source_target_pairs={{0,24},{2,26},{4,28},{6,30},{8,16},{10,18},{12,20},{14,22},{16,8},... | collective-permute-start | bytes 221192 | tf_op jit(solution)/shard_map/ppermute | solution.py:81
  96.8 1.4 %collective-permute-done.29.refs_2_ = f32[16,1152]{1,0:T(8,128)S(1)} collective-permute-done((f32[16,1152]{1,0:T(8,128)S(1)}, f32[16,1152]{1,0:T(8,128)S(1)}, u32[]{:S(2)}, u32[]{:S(2)}) %collective-permute-start.29) | collective-permute-done | bytes 73760 | tf_op jit(solution)/shard_map/ppermute | solution.py:81
  99.8 1.5 %collective-permute-start.31 = (f32[16,1152]{1,0:T(8,128)S(1)}, f32[16,1152]{1,0:T(8,128)S(1)}, u32[]{:S(2)}, u32[]{:S(2)}) collective-permute-start(f32[16,1152]{1,0:T(8,128)S(1)} %shard_map.85.refs_0_), channel_id=1, source_target_pairs={{0,2},{2,0},{4,6},{6,4},{8,10},{10,8},{12,14},{14,12},{16,18},{18,... | collective-permute-start | bytes 221192 | tf_op jit(solution)/shard_map/ppermute | solution.py:81
  104.2 1.4 %collective-permute-done.32.refs_2_ = f32[16,1152]{1,0:T(8,128)S(1)} collective-permute-done((f32[16,1152]{1,0:T(8,128)S(1)}, f32[16,1152]{1,0:T(8,128)S(1)}, u32[]{:S(2)}, u32[]{:S(2)}) %collective-permute-start.32) | collective-permute-done | bytes 73760 | tf_op jit(solution)/shard_map/ppermute | solution.py:81
  105.6 2.2 %collective-permute-done.33.refs_3_ = f32[16,1152]{1,0:T(8,128)S(1)} collective-permute-done((f32[16,1152]{1,0:T(8,128)S(1)}, f32[16,1152]{1,0:T(8,128)S(1)}, u32[]{:S(2)}, u32[]{:S(2)}) %collective-permute-start.33) | collective-permute-done | bytes 73760 | tf_op jit(solution)/shard_map/ppermute | solution.py:81
  (67 shorter events, 34.5 us)
Async XLA Ops:
  6.3 1.4 %collective-permute-start = (f32[16,384]{1,0:T(8,128)S(1)}, f32[16,384]{1,0:T(8,128)S(1)}, u32[]{:S(2)}, u32[]{:S(2)}) collective-permute-start(f32[16,384]{1,0:T(8,128)S(1)} %get-tuple-element.25.refs_0_), channel_id=1, source_target_pairs={{0,1},{1,0},{2,3},{3,2},{4,5},{5,4},{6,7},{7,6},{8,9},{9,8},{10,11... | collective-permute-start | bytes 73736 | tf_op jit(solution)/shard_map/ppermute | solution.py:81
  11.1 4.5 %collective-permute-start.1 = (f32[16,128]{1,0:T(8,128)S(1)}, f32[16,128]{1,0:T(8,128)S(1)}, u32[]{:S(2)}, u32[]{:S(2)}) collective-permute-start(f32[16,128]{1,0:T(8,128)S(1)} %get-tuple-element.28), channel_id=1, source_target_pairs={{0,2},{2,0},{4,6},{6,4},{8,10},{10,8},{12,14},{14,12},{16,18},{18,... | collective-permute-start | bytes 24584 | tf_op jit(solution)/shard_map/ppermute | solution.py:81
  14.0 3.7 %collective-permute-start.2 = (f32[16,128]{1,0:T(8,128)S(1)}, f32[16,128]{1,0:T(8,128)S(1)}, u32[]{:S(2)}, u32[]{:S(2)}) collective-permute-start(f32[16,128]{1,0:T(8,128)S(1)} %get-tuple-element.28), channel_id=1, source_target_pairs={{0,4},{2,6},{4,0},{6,2},{8,12},{10,14},{12,8},{14,10},{16,20},{18,... | collective-permute-start | bytes 24584 | tf_op jit(solution)/shard_map/ppermute | solution.py:81
  15.5 4.5 %collective-permute-start.3 = (f32[16,128]{1,0:T(8,128)S(1)}, f32[16,128]{1,0:T(8,128)S(1)}, u32[]{:S(2)}, u32[]{:S(2)}) collective-permute-start(f32[16,128]{1,0:T(8,128)S(1)} %get-tuple-element.28), channel_id=1, source_target_pairs={{0,6},{2,4},{4,2},{6,0},{8,14},{10,12},{12,10},{14,8},{16,22},{18,... | collective-permute-start | bytes 24584 | tf_op jit(solution)/shard_map/ppermute | solution.py:81
  20.1 4.4 %collective-permute-start.4 = (f32[16,128]{1,0:T(8,128)S(1)}, f32[16,128]{1,0:T(8,128)S(1)}, u32[]{:S(2)}, u32[]{:S(2)}) collective-permute-start(f32[16,128]{1,0:T(8,128)S(1)} %add_add_fusion.5), channel_id=1, source_target_pairs={{0,8},{2,10},{4,12},{6,14},{8,0},{10,2},{12,4},{14,6},{16,24},{18,... | collective-permute-start | bytes 24584 | tf_op jit(solution)/shard_map/ppermute | solution.py:81
  21.7 4.5 %collective-permute-start.5 = (f32[16,128]{1,0:T(8,128)S(1)}, f32[16,128]{1,0:T(8,128)S(1)}, u32[]{:S(2)}, u32[]{:S(2)}) collective-permute-start(f32[16,128]{1,0:T(8,128)S(1)} %add_add_fusion.5), channel_id=1, source_target_pairs={{0,16},{2,18},{4,20},{6,22},{8,24},{10,26},{12,28},{14,30},{16,0},... | collective-permute-start | bytes 24584 | tf_op jit(solution)/shard_map/ppermute | solution.py:81
  24.2 5.4 %collective-permute-start.6 = (f32[16,128]{1,0:T(8,128)S(1)}, f32[16,128]{1,0:T(8,128)S(1)}, u32[]{:S(2)}, u32[]{:S(2)}) collective-permute-start(f32[16,128]{1,0:T(8,128)S(1)} %add_add_fusion.5), channel_id=1, source_target_pairs={{0,24},{2,26},{4,28},{6,30},{8,16},{10,18},{12,20},{14,22},{16,8},... | collective-permute-start | bytes 24584 | tf_op jit(solution)/shard_map/ppermute | solution.py:81
  34.7 6.0 %collective-permute-start.10 = (f32[16,1152]{1,0:T(8,128)S(1)}, f32[16,1152]{1,0:T(8,128)S(1)}, u32[]{:S(2)}, u32[]{:S(2)}) collective-permute-start(f32[16,1152]{1,0:T(8,128)S(1)} %get-tuple-element.35), channel_id=1, source_target_pairs={{0,6},{2,4},{4,2},{6,0},{8,14},{10,12},{12,10},{14,8},{16,22},{18,... | collective-permute-start | bytes 221192 | tf_op jit(solution)/shard_map/ppermute | solution.py:81
  35.2 5.5 %collective-permute-start.8 = (f32[16,1152]{1,0:T(8,128)S(1)}, f32[16,1152]{1,0:T(8,128)S(1)}, u32[]{:S(2)}, u32[]{:S(2)}) collective-permute-start(f32[16,1152]{1,0:T(8,128)S(1)} %get-tuple-element.33), channel_id=1, source_target_pairs={{0,2},{2,0},{4,6},{6,4},{8,10},{10,8},{12,14},{14,12},{16,18},{18,... | collective-permute-start | bytes 221192 | tf_op jit(solution)/shard_map/ppermute | solution.py:81
  36.7 4.8 %collective-permute-start.9 = (f32[16,1152]{1,0:T(8,128)S(1)}, f32[16,1152]{1,0:T(8,128)S(1)}, u32[]{:S(2)}, u32[]{:S(2)}) collective-permute-start(f32[16,1152]{1,0:T(8,128)S(1)} %get-tuple-element.34), channel_id=1, source_target_pairs={{0,4},{2,6},{4,0},{6,2},{8,12},{10,14},{12,8},{14,10},{16,20},{18,... | collective-permute-start | bytes 221192 | tf_op jit(solution)/shard_map/ppermute | solution.py:81
  41.5 5.8 %collective-permute-start.11 = (f32[16,1152]{1,0:T(8,128)S(1)}, f32[16,1152]{1,0:T(8,128)S(1)}, u32[]{:S(2)}, u32[]{:S(2)}) collective-permute-start(f32[16,1152]{1,0:T(8,128)S(1)} %add_add_fusion.1.refs_0_), channel_id=1, source_target_pairs={{0,8},{2,10},{4,12},{6,14},{8,0},{10,2},{12,4},{14,6},{16,24},{18,... | collective-permute-start | bytes 221192 | tf_op jit(solution)/shard_map/ppermute | solution.py:81
  41.6 8.6 %collective-permute-start.12 = (f32[16,1152]{1,0:T(8,128)S(1)}, f32[16,1152]{1,0:T(8,128)S(1)}, u32[]{:S(2)}, u32[]{:S(2)}) collective-permute-start(f32[16,1152]{1,0:T(8,128)S(1)} %add_add_fusion.1.refs_0_), channel_id=1, source_target_pairs={{0,16},{2,18},{4,20},{6,22},{8,24},{10,26},{12,28},{14,30},{16,0},... | collective-permute-start | bytes 221192 | tf_op jit(solution)/shard_map/ppermute | solution.py:81
  42.4 7.9 %collective-permute-start.13 = (f32[16,1152]{1,0:T(8,128)S(1)}, f32[16,1152]{1,0:T(8,128)S(1)}, u32[]{:S(2)}, u32[]{:S(2)}) collective-permute-start(f32[16,1152]{1,0:T(8,128)S(1)} %add_add_fusion.1.refs_0_), channel_id=1, source_target_pairs={{0,24},{2,26},{4,28},{6,30},{8,16},{10,18},{12,20},{14,22},{16,8},... | collective-permute-start | bytes 221192 | tf_op jit(solution)/shard_map/ppermute | solution.py:81
  50.5 4.4 %collective-permute-start.14 = (f32[16,1152]{1,0:T(8,128)S(1)}, f32[16,1152]{1,0:T(8,128)S(1)}, u32[]{:S(2)}, u32[]{:S(2)}) collective-permute-start(f32[16,1152]{1,0:T(8,128)S(1)} %shard_map.80.refs_0_.old_ref), channel_id=1, source_target_pairs={{0,2},{2,0},{4,6},{6,4},{8,10},{10,8},{12,14},{14,12},{16,18},{18,... | collective-permute-start | bytes 221192 | tf_op jit(solution)/shard_map/ppermute | solution.py:81
  51.2 4.4 %collective-permute-start.15 = (f32[16,1152]{1,0:T(8,128)S(1)}, f32[16,1152]{1,0:T(8,128)S(1)}, u32[]{:S(2)}, u32[]{:S(2)}) collective-permute-start(f32[16,1152]{1,0:T(8,128)S(1)} %shard_map.80.refs_0_.old_ref), channel_id=1, source_target_pairs={{0,4},{2,6},{4,0},{6,2},{8,12},{10,14},{12,8},{14,10},{16,20},{18,... | collective-permute-start | bytes 221192 | tf_op jit(solution)/shard_map/ppermute | solution.py:81
  51.6 5.3 %collective-permute-start.16 = (f32[16,1152]{1,0:T(8,128)S(1)}, f32[16,1152]{1,0:T(8,128)S(1)}, u32[]{:S(2)}, u32[]{:S(2)}) collective-permute-start(f32[16,1152]{1,0:T(8,128)S(1)} %shard_map.80.refs_0_.old_ref), channel_id=1, source_target_pairs={{0,6},{2,4},{4,2},{6,0},{8,14},{10,12},{12,10},{14,8},{16,22},{18,... | collective-permute-start | bytes 221192 | tf_op jit(solution)/shard_map/ppermute | solution.py:81
  57.8 1.2 %collective-permute-start.17 = (f32[16,384]{1,0:T(8,128)S(1)}, f32[16,384]{1,0:T(8,128)S(1)}, u32[]{:S(2)}, u32[]{:S(2)}) collective-permute-start(f32[16,384]{1,0:T(8,128)S(1)} %get-tuple-element.36.refs_0_), channel_id=1, source_target_pairs={{0,1},{1,0},{2,3},{3,2},{4,5},{5,4},{6,7},{7,6},{8,9},{9,8},{10,11... | collective-permute-start | bytes 73736 | tf_op jit(solution)/shard_map/ppermute | solution.py:81
  63.0 3.7 %collective-permute-start.18 = (f32[16,128]{1,0:T(8,128)S(1)}, f32[16,128]{1,0:T(8,128)S(1)}, u32[]{:S(2)}, u32[]{:S(2)}) collective-permute-start(f32[16,128]{1,0:T(8,128)S(1)} %get-tuple-element.38), channel_id=1, source_target_pairs={{0,2},{2,0},{4,6},{6,4},{8,10},{10,8},{12,14},{14,12},{16,18},{18,... | collective-permute-start | bytes 24584 | tf_op jit(solution)/shard_map/ppermute | solution.py:81
  64.6 3.7 %collective-permute-start.19 = (f32[16,128]{1,0:T(8,128)S(1)}, f32[16,128]{1,0:T(8,128)S(1)}, u32[]{:S(2)}, u32[]{:S(2)}) collective-permute-start(f32[16,128]{1,0:T(8,128)S(1)} %get-tuple-element.38), channel_id=1, source_target_pairs={{0,4},{2,6},{4,0},{6,2},{8,12},{10,14},{12,8},{14,10},{16,20},{18,... | collective-permute-start | bytes 24584 | tf_op jit(solution)/shard_map/ppermute | solution.py:81
  66.0 4.5 %collective-permute-start.20 = (f32[16,128]{1,0:T(8,128)S(1)}, f32[16,128]{1,0:T(8,128)S(1)}, u32[]{:S(2)}, u32[]{:S(2)}) collective-permute-start(f32[16,128]{1,0:T(8,128)S(1)} %get-tuple-element.38), channel_id=1, source_target_pairs={{0,6},{2,4},{4,2},{6,0},{8,14},{10,12},{12,10},{14,8},{16,22},{18,... | collective-permute-start | bytes 24584 | tf_op jit(solution)/shard_map/ppermute | solution.py:81
  70.6 4.4 %collective-permute-start.21 = (f32[16,128]{1,0:T(8,128)S(1)}, f32[16,128]{1,0:T(8,128)S(1)}, u32[]{:S(2)}, u32[]{:S(2)}) collective-permute-start(f32[16,128]{1,0:T(8,128)S(1)} %add_add_fusion.3), channel_id=1, source_target_pairs={{0,8},{2,10},{4,12},{6,14},{8,0},{10,2},{12,4},{14,6},{16,24},{18,... | collective-permute-start | bytes 24584 | tf_op jit(solution)/shard_map/ppermute | solution.py:81
  71.9 4.5 %collective-permute-start.22 = (f32[16,128]{1,0:T(8,128)S(1)}, f32[16,128]{1,0:T(8,128)S(1)}, u32[]{:S(2)}, u32[]{:S(2)}) collective-permute-start(f32[16,128]{1,0:T(8,128)S(1)} %add_add_fusion.3), channel_id=1, source_target_pairs={{0,16},{2,18},{4,20},{6,22},{8,24},{10,26},{12,28},{14,30},{16,0},... | collective-permute-start | bytes 24584 | tf_op jit(solution)/shard_map/ppermute | solution.py:81
  73.1 5.4 %collective-permute-start.23 = (f32[16,128]{1,0:T(8,128)S(1)}, f32[16,128]{1,0:T(8,128)S(1)}, u32[]{:S(2)}, u32[]{:S(2)}) collective-permute-start(f32[16,128]{1,0:T(8,128)S(1)} %add_add_fusion.3), channel_id=1, source_target_pairs={{0,24},{2,26},{4,28},{6,30},{8,16},{10,18},{12,20},{14,22},{16,8},... | collective-permute-start | bytes 24584 | tf_op jit(solution)/shard_map/ppermute | solution.py:81
  84.3 4.6 %collective-permute-start.25 = (f32[16,1152]{1,0:T(8,128)S(1)}, f32[16,1152]{1,0:T(8,128)S(1)}, u32[]{:S(2)}, u32[]{:S(2)}) collective-permute-start(f32[16,1152]{1,0:T(8,128)S(1)} %get-tuple-element.42), channel_id=1, source_target_pairs={{0,2},{2,0},{4,6},{6,4},{8,10},{10,8},{12,14},{14,12},{16,18},{18,... | collective-permute-start | bytes 221192 | tf_op jit(solution)/shard_map/ppermute | solution.py:81
  84.8 5.1 %collective-permute-start.26 = (f32[16,1152]{1,0:T(8,128)S(1)}, f32[16,1152]{1,0:T(8,128)S(1)}, u32[]{:S(2)}, u32[]{:S(2)}) collective-permute-start(f32[16,1152]{1,0:T(8,128)S(1)} %get-tuple-element.43), channel_id=1, source_target_pairs={{0,4},{2,6},{4,0},{6,2},{8,12},{10,14},{12,8},{14,10},{16,20},{18,... | collective-permute-start | bytes 221192 | tf_op jit(solution)/shard_map/ppermute | solution.py:81
  85.8 5.3 %collective-permute-start.27 = (f32[16,1152]{1,0:T(8,128)S(1)}, f32[16,1152]{1,0:T(8,128)S(1)}, u32[]{:S(2)}, u32[]{:S(2)}) collective-permute-start(f32[16,1152]{1,0:T(8,128)S(1)} %get-tuple-element.44), channel_id=1, source_target_pairs={{0,6},{2,4},{4,2},{6,0},{8,14},{10,12},{12,10},{14,8},{16,22},{18,... | collective-permute-start | bytes 221192 | tf_op jit(solution)/shard_map/ppermute | solution.py:81
  91.0 5.8 %collective-permute-start.28 = (f32[16,1152]{1,0:T(8,128)S(1)}, f32[16,1152]{1,0:T(8,128)S(1)}, u32[]{:S(2)}, u32[]{:S(2)}) collective-permute-start(f32[16,1152]{1,0:T(8,128)S(1)} %add_add_fusion.refs_0_), channel_id=1, source_target_pairs={{0,8},{2,10},{4,12},{6,14},{8,0},{10,2},{12,4},{14,6},{16,24},{18,... | collective-permute-start | bytes 221192 | tf_op jit(solution)/shard_map/ppermute | solution.py:81
  91.1 7.1 %collective-permute-start.29 = (f32[16,1152]{1,0:T(8,128)S(1)}, f32[16,1152]{1,0:T(8,128)S(1)}, u32[]{:S(2)}, u32[]{:S(2)}) collective-permute-start(f32[16,1152]{1,0:T(8,128)S(1)} %add_add_fusion.refs_0_), channel_id=1, source_target_pairs={{0,16},{2,18},{4,20},{6,22},{8,24},{10,26},{12,28},{14,30},{16,0},... | collective-permute-start | bytes 221192 | tf_op jit(solution)/shard_map/ppermute | solution.py:81
  93.3 6.3 %collective-permute-start.30 = (f32[16,1152]{1,0:T(8,128)S(1)}, f32[16,1152]{1,0:T(8,128)S(1)}, u32[]{:S(2)}, u32[]{:S(2)}) collective-permute-start(f32[16,1152]{1,0:T(8,128)S(1)} %add_add_fusion.refs_0_), channel_id=1, source_target_pairs={{0,24},{2,26},{4,28},{6,30},{8,16},{10,18},{12,20},{14,22},{16,8},... | collective-permute-start | bytes 221192 | tf_op jit(solution)/shard_map/ppermute | solution.py:81
  99.8 4.4 %collective-permute-start.31 = (f32[16,1152]{1,0:T(8,128)S(1)}, f32[16,1152]{1,0:T(8,128)S(1)}, u32[]{:S(2)}, u32[]{:S(2)}) collective-permute-start(f32[16,1152]{1,0:T(8,128)S(1)} %shard_map.85.refs_0_), channel_id=1, source_target_pairs={{0,2},{2,0},{4,6},{6,4},{8,10},{10,8},{12,14},{14,12},{16,18},{18,... | collective-permute-start | bytes 221192 | tf_op jit(solution)/shard_map/ppermute | solution.py:81
  101.3 4.4 %collective-permute-start.32 = (f32[16,1152]{1,0:T(8,128)S(1)}, f32[16,1152]{1,0:T(8,128)S(1)}, u32[]{:S(2)}, u32[]{:S(2)}) collective-permute-start(f32[16,1152]{1,0:T(8,128)S(1)} %shard_map.85.refs_0_), channel_id=1, source_target_pairs={{0,4},{2,6},{4,0},{6,2},{8,12},{10,14},{12,8},{14,10},{16,20},{18,... | collective-permute-start | bytes 221192 | tf_op jit(solution)/shard_map/ppermute | solution.py:81
  102.6 5.3 %collective-permute-start.33 = (f32[16,1152]{1,0:T(8,128)S(1)}, f32[16,1152]{1,0:T(8,128)S(1)}, u32[]{:S(2)}, u32[]{:S(2)}) collective-permute-start(f32[16,1152]{1,0:T(8,128)S(1)} %shard_map.85.refs_0_), channel_id=1, source_target_pairs={{0,6},{2,4},{4,2},{6,0},{8,14},{10,12},{12,10},{14,8},{16,22},{18,... | collective-permute-start | bytes 221192 | tf_op jit(solution)/shard_map/ppermute | solution.py:81
  (9 other events, 10.1 us)

commit v2 on v1

--- a/solution.py
+++ b/solution.py
@@ -37,14 +37,21 @@
     return hi, mid, low
 
 
-def eliminate(a, first, count):
-    rows = lax.broadcasted_iota(jnp.int32, a.shape, 0)
-    for k in range(count):
-        column = a[:, first + k : first + k + 1]
-        pivot = a[k : k + 1, first + k : first + k + 1]
-        scaled = a[k : k + 1, :] * (1.0 / pivot)
-        a = jnp.where(rows == k, scaled, a - column * scaled)
-    return a
+def solve_spd(gram, sides):
+    r = gram.shape[0]
+    columns = [jnp.broadcast_to(gram[:, j : j + 1], (r, BLOCK)) for j in range(r)]
+    rows = lax.broadcasted_iota(jnp.int32, (r, BLOCK), 0)
+    for k in range(r):
+        pivot = columns[k]
+        inverse = 1.0 / pivot[k : k + 1, :]
+
+        def step(x):
+            scaled = x[k : k + 1, :] * inverse
+            return jnp.where(rows == k, scaled, x - pivot * scaled)
+
+        columns = columns[: k + 1] + [step(c) for c in columns[k + 1 :]]
+        sides = [step(x) for x in sides]
+    return sides
 
 
 def eye_at(shape, first):
@@ -64,6 +71,7 @@
         self.blocks = self.chunk // BLOCK
         self.extra = BLOCK * (-(-2 * self.blocks // rank))
         self.stack = 6 * rank + 16
+        self.spot, self.twin = rank * rank - 2, rank * rank - rank - 1
 
 
 def levels(n):
@@ -135,25 +143,39 @@
     packed_ref[:, td : td + r] = gram
 
 
-def first_projection(sz, me_ref, f_ref, b_ref, d_ref, valid_ref, fore_ref, packed_ref, stack_ref, own_ref, least_ref):
-    totals = None
-    for c in range(sz.group):
-        at = c * sz.chunk
-        d_rows = [d_ref[c * sz.blocks + j : c * sz.blocks + j + 1, :] for j in range(sz.blocks)]
-        totals = project_chunk(sz, f_ref, stack_ref, at, b_ref[:, at : at + sz.chunk], d_rows, totals)
-    pack_projections(sz, totals, packed_ref)
-    me = me_ref[0]
+def first_projection(sz, f_hbm, b_hbm, d_hbm, valid_hbm, fore_hbm, f_ref, packed_ref, stack_ref, own_ref, least_ref, valid_ref, b_ref, d_ref, flags_ref, sems):
+    small = [
+        pltpu.make_async_copy(d_hbm, d_ref, sems.at[0]),
+        pltpu.make_async_copy(b_hbm, b_ref, sems.at[1]),
+        pltpu.make_async_copy(valid_hbm, flags_ref.at[0:1], sems.at[2]),
+        pltpu.make_async_copy(fore_hbm, flags_ref.at[8:9], sems.at[3]),
+    ]
+    spans = [pl.ds(c * sz.chunk, sz.chunk) for c in range(sz.group)]
+    large = [pltpu.make_async_copy(f_hbm.at[:, s], f_ref.at[:, s], sems.at[4 + c]) for c, s in enumerate(spans)]
+    for copy in small + large:
+        copy.start()
+    for copy in small:
+        copy.wait()
+    valid = flags_ref[0:1, :] != 0
+    valid_ref[...] = jnp.broadcast_to(valid.astype(F32), valid_ref.shape)
+    least_ref[...] = jnp.broadcast_to(jnp.where(valid, flags_ref[8:9, :], ROW_PX), (BLOCK, sz.tile_dev)).T
+    me = lax.axis_index("tiles") & (sz.group - 1)
     own_ref[:, 0 : sz.chunk] = b_ref[:, pl.ds(pl.multiple_of(me * sz.chunk, BLOCK), sz.chunk)]
     own_ref[:, sz.chunk :] = jnp.zeros((sz.rank, sz.extra), F32)
     for j in range(sz.blocks):
         own_ref[j % sz.rank, pl.ds(sz.chunk + j // sz.rank * BLOCK, BLOCK)] = d_ref[me * sz.blocks + j, :]
-    least = jnp.where(valid_ref[...] != 0, fore_ref[...], ROW_PX)
-    least_ref[...] = jnp.broadcast_to(least, (BLOCK, sz.tile_dev)).T
-
-
-def later_projection(sz, me_ref, f_ref, *refs):
+    totals = None
+    for c in range(sz.group):
+        at = c * sz.chunk
+        large[c].wait()
+        d_rows = [d_ref[c * sz.blocks + j : c * sz.blocks + j + 1, :] for j in range(sz.blocks)]
+        totals = project_chunk(sz, f_ref, stack_ref, at, b_ref[:, at : at + sz.chunk], d_rows, totals)
+    pack_projections(sz, totals, packed_ref)
+
+
+def later_projection(sz, f_ref, *refs):
     chunks, (packed_ref, stack_ref) = refs[: sz.group], refs[sz.group :]
-    me = me_ref[0]
+    me = lax.axis_index("tiles") & (sz.group - 1)
     totals = None
     for k, ref in enumerate(chunks):
         at = pl.multiple_of((me ^ k) * sz.chunk, BLOCK)
@@ -178,8 +200,9 @@
     f_ref, stack_ref, least_ref, valid_ref, coef_ref, parts_ref, note_ref = refs[sz.n_pix :]
     r, td = sz.rank, sz.tile_dev
     a = tree([ref[...] for ref in packed]) / sz.pixels_all
-    a = a + RIDGE * eye_at(a.shape, td)
-    coef = eliminate(a, td, r)[:, 0:td]
+    gram = a[:, td : td + r] + RIDGE * eye_at((r, r), 0)
+    sides = [a[:, at : at + BLOCK] for at in range(0, td, BLOCK)]
+    coef = jnp.concatenate(solve_spd(gram, sides), axis=1)
     coef_ref[...] = coef
     hi, mid, low = split3(coef)
     row = lax.broadcasted_iota(jnp.int32, (BLOCK - 6 * r, td), 0)
@@ -190,39 +213,40 @@
     parts = parts[:, 0 : sz.stack]
     least = least_ref[...]
 
-    def body(step, total):
-        offset = pl.multiple_of(step * width, BLOCK)
+    total = jnp.zeros((8, BLOCK), F32)
+    for offset in range(0, sz.pix_dev, width):
         res = residual(sz, f_ref, stack_ref, parts, offset, width)
         square = res * res
         for j in range(width // BLOCK):
-            block = (step * (width // BLOCK) + j) % (ROW_PX // BLOCK)
+            block = (offset // BLOCK + j) % (ROW_PX // BLOCK)
             term = jnp.where(least <= block, square[:, j * BLOCK : (j + 1) * BLOCK], 0.0)
             total = total + jnp.sum(term.reshape(td // 8, 8, BLOCK), axis=0)
-        return total
-
-    total = lax.fori_loop(0, sz.pix_dev // width, body, jnp.zeros((8, BLOCK), F32))
     total = jnp.sum(jnp.sum(total, axis=0, keepdims=True), axis=1, keepdims=True)
-    held = coef * (valid_ref[...] != 0).astype(F32)
-    gram = lax.dot_general(held, coef, NT, precision=lax.Precision.HIGHEST, preferred_element_type=F32)
-    note_ref[...] = jnp.zeros((r, BLOCK), F32)
-    note_ref[:, 0:r] = gram
-    note_ref[0:1, r : r + 1] = total
+    products = jnp.concatenate([coef[i : i + 1] * coef for i in range(r)], axis=0)
+    ones = valid_ref[...].astype(BF16)
+    flat = sum(lax.dot_general(ones, part, NT, preferred_element_type=F32) for part in split3(products))
+    lane = lax.broadcasted_iota(jnp.int32, flat.shape, 1)
+    flat = jnp.where(lane == sz.spot, total, flat)
+    for at in range(0, note_ref.shape[0], 8):
+        note_ref[at : at + 8, :] = flat
 
 
 def invert_gram(sz, note_ref, inverse_ref):
     r = sz.rank
-    gram = note_ref[:, 0:r] / sz.tiles_all + RIDGE * eye_at((r, r), 0)
-    a = jnp.concatenate([gram, eye_at((r, BLOCK - r), 0)], axis=1)
-    inverse_ref[...] = eliminate(a, 0, r)
-
-
-def update_terms(sz, width, me_ref, *refs):
-    notes = refs[: sz.n_pix]
-    f_ref, stack_ref, least_ref, coef_ref, parts_ref = refs[sz.n_pix : sz.n_pix + 5]
-    outs = refs[sz.n_pix + 5 :]
+    flat = jnp.sum(note_ref[...], axis=0, keepdims=True)
+    gram = jnp.concatenate([flat[:, i * r : (i + 1) * r] for i in range(r)], axis=0)
+    row = lax.broadcasted_iota(jnp.int32, (r, r), 0)
+    col = lax.broadcasted_iota(jnp.int32, (r, r), 1)
+    twin = flat[:, sz.twin : sz.twin + 1]
+    gram = jnp.where((row == r - 1) & (col == r - 2), twin, gram)
+    gram = gram / (sz.n_pix * sz.tiles_all) + RIDGE * eye_at((r, r), 0)
+    (inverse_ref[...],) = solve_spd(gram, [eye_at((r, BLOCK), 0)])
+
+
+def update_terms(sz, width, note_ref, f_ref, stack_ref, least_ref, coef_ref, parts_ref, *outs):
     r, td = sz.rank, sz.tile_dev
-    me = me_ref[0]
-    total = tree([ref[0:1, r : r + 1] for ref in notes])
+    me = lax.axis_index("tiles") & (sz.group - 1)
+    total = jnp.sum(note_ref[:, sz.spot : sz.spot + 1], axis=0, keepdims=True)
     spread = total / (sz.tiles_all * sz.pixels_all) + 1e-05
     scale = jnp.broadcast_to(1.0 / (4.0 * spread), (8, BLOCK))[0:1, :]
     parts = parts_ref[:, 0 : sz.stack]
@@ -267,7 +291,7 @@
     total_refs, new_ref = refs[:-1], refs[-1]
     r = sz.rank
     totals = tree([ref[...] for ref in total_refs])
-    inverse = inverse_ref[:, r : 2 * r]
+    inverse = inverse_ref[:, 0:r]
     change = jnp.dot(inverse, totals[:, 0 : sz.chunk] / sz.tiles_all, precision=lax.Precision.HIGHEST, preferred_element_type=F32)
     new_ref[:, 0 : sz.chunk] = old_ref[:, 0 : sz.chunk] + change
     new_ref[:, sz.chunk :] = jnp.zeros((r, sz.extra), F32)
@@ -285,9 +309,9 @@
         )
 
 
-def assemble(sz, me_ref, *refs):
+def assemble(sz, *refs):
     chunks, (b_ref, d_ref) = refs[: sz.group], refs[sz.group :]
-    me = me_ref[0]
+    me = lax.axis_index("tiles") & (sz.group - 1)
     for k, ref in enumerate(chunks):
         c = me ^ k
         b_ref[:, pl.ds(pl.multiple_of(c * sz.chunk, BLOCK), sz.chunk)] = ref[:, 0 : sz.chunk]
@@ -296,24 +320,24 @@
             d_ref[c * sz.blocks + j, :] = ref[j % sz.rank, lane : lane + BLOCK]
 
 
-def call(body, outs, ins, smem=0, cost=None):
+def call(body, outs, ins, in_hbm=False, scratch=()):
     return pl.pallas_call(
         body,
         out_shape=[jax.ShapeDtypeStruct(s, t) for s, t in outs],
-        in_specs=[SMEM] * smem + vmem(len(ins) - smem),
+        in_specs=[pl.BlockSpec(memory_space=pltpu.HBM)] * len(ins) if in_hbm else vmem(len(ins)),
         out_specs=vmem(len(outs)),
+        scratch_shapes=scratch,
         compiler_params=params(),
-    )(*ins)
+    )(*([pltpu.with_memory_space_constraint(x, pltpu.HBM) for x in ins] if in_hbm else ins))
 
 
 def local(frames, tile_valid, foreground_blocks, basis_start, dark_start):
     td, pd = frames.shape
     r = basis_start.shape[0]
     sz = Sizes(td, pd, r, lax.axis_size("tiles"), lax.axis_size("pix"))
-    pix_masks = [m for m in range(1, sz.n_pix)]
-    me = (lax.axis_index("tiles") & (sz.group - 1)).astype(jnp.int32).reshape(1)
-    valid = tile_valid.reshape(1, td)
-    fore = foreground_blocks.reshape(1, td)
+    everyone = ("tiles", "pix")
+    devices = sz.n_tiles * sz.n_pix
+    pix_masks = range(1, sz.n_pix)
     width = min(512, sz.chunk)
     chunk_shape = (r, sz.chunk + sz.extra)
     packed_out = ((r, td + BLOCK), F32)
@@ -321,31 +345,32 @@
     masks = sz.tile_levels[0]
     for iteration in range(ITERS):
         if iteration == 0:
-            packed, stack, old, least = call(
+            frames, packed, stack, old, least, valid = call(
                 functools.partial(first_projection, sz),
-                [packed_out, stack_out, (chunk_shape, F32), ((td, BLOCK), jnp.int32)],
-                [me, frames, basis_start, dark_start.reshape(pd // BLOCK, BLOCK), valid, fore],
-                smem=1,
+                [((td, pd), BF16), packed_out, stack_out, (chunk_shape, F32), ((td, BLOCK), jnp.int32), ((8, td), F32)],
+                [frames, basis_start, dark_start.reshape(pd // BLOCK, BLOCK), tile_valid.reshape(1, td), foreground_blocks.reshape(1, td)],
+                in_hbm=True,
+                scratch=[
+                    pltpu.VMEM((r, pd), F32),
+                    pltpu.VMEM((pd // BLOCK, BLOCK), F32),
+                    pltpu.VMEM((16, td), jnp.int32),
+                    pltpu.SemaphoreType.DMA((4 + sz.group,)),
+                ],
             )
         else:
-            packed, stack = call(
-                functools.partial(later_projection, sz), [packed_out, stack_out], [me, frames] + chunks, smem=1
-            )
+            packed, stack = call(functools.partial(later_projection, sz), [packed_out, stack_out], [frames] + chunks)
         both = [packed] + [partner(packed, "pix", m) for m in pix_masks]
         coef, parts, note = call(
             functools.partial(solve_tiles, sz, width),
-            [((r, td), F32), ((td, BLOCK), BF16), ((r, BLOCK), F32)],
+            [((r, td), F32), ((td, BLOCK), BF16), ((devices, r * r), F32)],
             both + [frames, stack, least, valid],
         )
-        for level in sz.tile_levels:
-            note = sum_level(note, "tiles", level)
-        (inverse,) = call(functools.partial(invert_gram, sz), [((r, BLOCK), F32)], [note])
-        notes = [note] + [partner(note, "pix", m) for m in pix_masks]
+        notes = lax.all_to_all(note, everyone, 0, 0, tiled=True)
+        (inverse,) = call(functools.partial(invert_gram, sz), [((r, BLOCK), F32)], [notes])
         terms = call(
             functools.partial(update_terms, sz, width),
             [(chunk_shape, F32)] * sz.group,
-            [me] + notes + [frames, stack, least, coef, parts],
-            smem=1,
+            [notes, frames, stack, least, coef, parts],
         )
         total = tree([terms[0]] + [partner(terms[k], "tiles", m) for k, m in enumerate(masks, 1)])
         later = sz.tile_levels[1:]
@@ -354,9 +379,7 @@
         totals = [total] + [partner(total, "tiles", m) for m in (later[-1] if later else ())]
         (old,) = call(functools.partial(update_chunk, sz), [(chunk_shape, F32)], [inverse, old] + totals)
         chunks = [old] + [partner(old, "tiles", m) for m in masks]
-    basis, dark = call(
-        functools.partial(assemble, sz), [((r, pd), F32), ((pd // BLOCK, BLOCK), F32)], [me] + chunks, smem=1
-    )
+    basis, dark = call(functools.partial(assemble, sz), [((r, pd), F32), ((pd // BLOCK, BLOCK), F32)], chunks)
     return basis, dark.reshape(pd), coef.T
 
 

time: 109 us -> 87.6 us (0.80)
  blocking collectives: 0 us -> 24.2 us
  waiting for transfers between devices: 41.4 us -> 21.7 us
  starting transfers between devices: 40.2 us -> 23.5 us
  local copies, waits for them, and re-layouts: 5.33 us -> 0.79 us
  Pallas kernels: 20.8 us -> 16.3 us
    all_to_all x0 -> x2, blocking collectives: none -> 24.2 us  [local(): notes = lax.all_to_all(note, everyone, 0, 0, tiled=True)]
    ppermute x34 -> x20, waiting for transfers between devices: 41.4 us -> 21.7 us  [partner(): return lax.ppermute(x, axis, [(i, i ^ mask) for i in range(n)])]
    ppermute x34 -> x20, starting transfers between devices: 40.2 us -> 23.5 us  [partner(): return lax.ppermute(x, axis, [(i, i ^ mask) for i in range(n)])]
    unnamed x14 -> x4, local copies, waits for them, and re-layouts: 5.33 us -> 0.72 us
    pallas_call x11, Pallas kernels: 20.8 us -> 16.3 us  [call(): pl.pallas_call(body, out_shape=[jax.ShapeDtypeStruct(s, t) for s, t in ou...]
  transfers between devices with their start and end apart: 34 -> 20, of which waited for: 28 -> 18; matrix products, arithmetic and copies ran while one was open for 0% -> 0% of each run, Pallas kernels for 2% -> 1%
where the time goes in v2:
time: 87.6 us; the launch traced here: 87.2 us
  blocking collectives  24.2 us (28%)
  starting transfers between devices  23.5 us (27%)
  waiting for transfers between devices  21.7 us (25%)
  Pallas kernels  16.3 us (19%)
    all_to_all x2, blocking collectives, local(): notes = lax.all_to_all(note, everyone, 0, 0, tiled=True)  24.2 us
    ppermute x20, starting transfers between devices, partner(): return lax.ppermute(x, axis, [(i, i ^ mask) for i in range(n)])  23.5 us
    ppermute x20, waiting for transfers between devices, partner(): return lax.ppermute(x, axis, [(i, i ^ mask) for i in range(n)])  21.7 us
    pallas_call x11, Pallas kernels, call(): pl.pallas_call(body, out_shape=[jax.ShapeDtypeStruct(s, t) for s, t in ou...  16.3 us
  transfers between devices with their start and end apart: 20, of which 18 were waited for; matrix products, arithmetic and copies ran while one was open for 0% of the time, Pallas kernels for 1%

profile of v2, /device:TPU:0, one launch (start us, length us, event | category | flops | bytes accessed | tf_op | source)
XLA Modules:
  0.0 87.2 jit_solution(4427202808307125010)
XLA Ops:
  0.6 2.7 %shard_map.76 = (bf16[256,4096]{1,0:T(8,128)(2,1)S(1)}, f32[16,384]{1,0:T(8,128)S(1)}, bf16[112,4096]{1,0:T(8,128)(2,1)S(1)}, f32[16,1152]{1,0:T(8,128)S(1)}, s3...) custom-call(bf16[256,4096]{1,0:T(8,128)(2,1)} %f_hbm.1, f32[16,4096]{1,0:T(8,128)} %b_hbm.1, f32[32,128]{1,0:T(8,128)} %bitcast.20, ...), custom_call_target="tpu_custom_call" | custom-call | tf_op jit(solution)/shard_map/pallas_call | solution.py:324
  3.9 0.8 collective-permute-done.refs_1_
  4.7 1.5 %shard_map.77 = (f32[16,256]{1,0:T(8,128)S(1)}, bf16[256,128]{1,0:T(8,128)(2,1)S(1)}, f32[32,256]{1,0:T(8,128)S(1)}) custom-call(f32[16,384]{1,0:T(8,128)S(1)} %get-tuple-element.28.refs_0_, f32[16,384]{1,0:T(8,128)S(1)} %collective-permute-done.refs_1_, bf16[256,4096]{1,0:T(8,128)(2,1)S(1)} %get-tuple-element.27.refs_2_.f_ref, ...), custom_call_target="tpu_custom_call" | custom-call | tf_op jit(solution)/shard_map/pallas_call | solution.py:324
  6.2 14.2 %all_to_all.22 = f32[32,1,256]{2,1,0:T(1,128)S(1)} all-to-all(f32[32,1,256]{2,1,0:T(1,128)S(1)} %copy.8), channel_id=1, replica_groups=mesh['tiles'=16,'pix'=2] {'tiles','pix'}, dimensions={0} | all-to-all | bytes 65536 | tf_op jit(solution)/shard_map/all_to_all | solution.py:368
  20.5 3.8 %shard_map.79 = (f32[16,1152]{1,0:T(8,128)S(1)}, f32[16,1152]{1,0:T(8,128)S(1)}, f32[16,1152]{1,0:T(8,128)S(1)}, f32[16,1152]{1,0:T(8,128)S(1)}) custom-call(f32[32,256]{1,0:T(8,128)S(1)} %bitcast.15, bf16[256,4096]{1,0:T(8,128)(2,1)S(1)} %get-tuple-element.27.refs_2_.f_ref, bf16[112,4096]{1,0:T(8,128)(2,1)S(1)} %get-tuple-element.29.refs_3_.stack_ref, ...), custom_call_target="tpu_custom_call" | custom-call | tf_op jit(solution)/shard_map/pallas_call | solution.py:324
  25.5 2.3 %collective-permute-start.3 = (f32[16,1152]{1,0:T(8,128)S(1)}, f32[16,1152]{1,0:T(8,128)S(1)}, u32[]{:S(2)}, u32[]{:S(2)}) collective-permute-start(f32[16,1152]{1,0:T(8,128)S(1)} %get-tuple-element.39), channel_id=1, source_target_pairs={{0,6},{2,4},{4,2},{6,0},{8,14},{10,12},{12,10},{14,8},{16,22},{18,... | collective-permute-start | bytes 221192 | tf_op jit(solution)/shard_map/ppermute | solution.py:89
  27.8 1.2 %collective-permute-done.1 = f32[16,1152]{1,0:T(8,128)S(1)} collective-permute-done((f32[16,1152]{1,0:T(8,128)S(1)}, f32[16,1152]{1,0:T(8,128)S(1)}, u32[]{:S(2)}, u32[]{:S(2)}) %collective-permute-start.1) | collective-permute-done | bytes 73760 | tf_op jit(solution)/shard_map/ppermute | solution.py:89
  28.9 1.0 %collective-permute-done.2 = f32[16,1152]{1,0:T(8,128)S(1)} collective-permute-done((f32[16,1152]{1,0:T(8,128)S(1)}, f32[16,1152]{1,0:T(8,128)S(1)}, u32[]{:S(2)}, u32[]{:S(2)}) %collective-permute-start.2) | collective-permute-done | bytes 73760 | tf_op jit(solution)/shard_map/ppermute | solution.py:89
  29.9 0.8 collective-permute-done.3
  31.4 1.5 %collective-permute-start.5 = (f32[16,1152]{1,0:T(8,128)S(1)}, f32[16,1152]{1,0:T(8,128)S(1)}, u32[]{:S(2)}, u32[]{:S(2)}) collective-permute-start(f32[16,1152]{1,0:T(8,128)S(1)} %add_add_fusion.1.refs_0_), channel_id=1, source_target_pairs={{0,16},{2,18},{4,20},{6,22},{8,24},{10,26},{12,28},{14,30},{16,0},... | collective-permute-start | bytes 221192 | tf_op jit(solution)/shard_map/ppermute | solution.py:89
  32.9 2.3 %collective-permute-start.4 = (f32[16,1152]{1,0:T(8,128)S(1)}, f32[16,1152]{1,0:T(8,128)S(1)}, u32[]{:S(2)}, u32[]{:S(2)}) collective-permute-start(f32[16,1152]{1,0:T(8,128)S(1)} %add_add_fusion.1.refs_0_), channel_id=1, source_target_pairs={{0,8},{2,10},{4,12},{6,14},{8,0},{10,2},{12,4},{14,6},{16,24},{18,... | collective-permute-start | bytes 221192 | tf_op jit(solution)/shard_map/ppermute | solution.py:89
  35.6 1.5 %collective-permute-done.6.refs_3_ = f32[16,1152]{1,0:T(8,128)S(1)} collective-permute-done((f32[16,1152]{1,0:T(8,128)S(1)}, f32[16,1152]{1,0:T(8,128)S(1)}, u32[]{:S(2)}, u32[]{:S(2)}) %collective-permute-start.6) | collective-permute-done | bytes 73760 | tf_op jit(solution)/shard_map/ppermute | solution.py:89
  37.1 1.6 %collective-permute-done.5.refs_2_ = f32[16,1152]{1,0:T(8,128)S(1)} collective-permute-done((f32[16,1152]{1,0:T(8,128)S(1)}, f32[16,1152]{1,0:T(8,128)S(1)}, u32[]{:S(2)}, u32[]{:S(2)}) %collective-permute-start.5) | collective-permute-done | bytes 73760 | tf_op jit(solution)/shard_map/ppermute | solution.py:89
  38.9 2.1 %collective-permute-start.9 = (f32[16,1152]{1,0:T(8,128)S(1)}, f32[16,1152]{1,0:T(8,128)S(1)}, u32[]{:S(2)}, u32[]{:S(2)}) collective-permute-start(f32[16,1152]{1,0:T(8,128)S(1)} %shard_map.80.refs_0_.old_ref), channel_id=1, source_target_pairs={{0,6},{2,4},{4,2},{6,0},{8,14},{10,12},{12,10},{14,8},{16,22},{18,... | collective-permute-start | bytes 221192 | tf_op jit(solution)/shard_map/ppermute | solution.py:89
  42.5 1.8 %collective-permute-done.9.refs_3_ = f32[16,1152]{1,0:T(8,128)S(1)} collective-permute-done((f32[16,1152]{1,0:T(8,128)S(1)}, f32[16,1152]{1,0:T(8,128)S(1)}, u32[]{:S(2)}, u32[]{:S(2)}) %collective-permute-start.9) | collective-permute-done | bytes 73760 | tf_op jit(solution)/shard_map/ppermute | solution.py:89
  44.2 1.1 %collective-permute-done.8.refs_2_ = f32[16,1152]{1,0:T(8,128)S(1)} collective-permute-done((f32[16,1152]{1,0:T(8,128)S(1)}, f32[16,1152]{1,0:T(8,128)S(1)}, u32[]{:S(2)}, u32[]{:S(2)}) %collective-permute-start.8) | collective-permute-done | bytes 73760 | tf_op jit(solution)/shard_map/ppermute | solution.py:89
  46.1 1.0 %shard_map.81 = (f32[16,384]{1,0:T(8,128)S(1)}, bf16[112,4096]{1,0:T(8,128)(2,1)S(1)}) custom-call(bf16[256,4096]{1,0:T(8,128)(2,1)S(1)} %get-tuple-element.27.refs_2_.f_ref, f32[16,1152]{1,0:T(8,128)S(1)} %shard_map.80.refs_0_.old_ref, f32[16,1152]{1,0:T(8,128)S(1)} %collective-permute-done.7.refs_1_, f32[16,1152]{1,0:T(8,128)S(1)} %collective-permute-done.8.refs_2_, ...), custom_call_target="tpu_custom_call" | custom-call | tf_op jit(solution)/shard_map/pallas_call | solution.py:324
  47.1 1.2 %collective-permute-done.10.refs_1_ = f32[16,384]{1,0:T(8,128)S(1)} collective-permute-done((f32[16,384]{1,0:T(8,128)S(1)}, f32[16,384]{1,0:T(8,128)S(1)}, u32[]{:S(2)}, u32[]{:S(2)}) %collective-permute-start.10) | collective-permute-done | bytes 24608 | tf_op jit(solution)/shard_map/ppermute | solution.py:89
  48.3 1.8 %shard_map.82 = (f32[16,256]{1,0:T(8,128)}, bf16[256,128]{1,0:T(8,128)(2,1)S(1)}, f32[32,256]{1,0:T(8,128)S(1)}) custom-call(f32[16,384]{1,0:T(8,128)S(1)} %get-tuple-element.40.refs_0_, f32[16,384]{1,0:T(8,128)S(1)} %collective-permute-done.10.refs_1_, bf16[256,4096]{1,0:T(8,128)(2,1)S(1)} %get-tuple-element.27.refs_2_.f_ref, ...), custom_call_target="tpu_custom_call" | custom-call | tf_op jit(solution)/shard_map/pallas_call | solution.py:324
  50.1 10.0 %all_to_all.23 = f32[32,1,256]{2,1,0:T(1,128)S(1)} all-to-all(f32[32,1,256]{2,1,0:T(1,128)S(1)} %copy.9), channel_id=1, replica_groups=mesh['tiles'=16,'pix'=2] {'tiles','pix'}, dimensions={0} | all-to-all | bytes 65536 | tf_op jit(solution)/shard_map/all_to_all | solution.py:368
  60.8 3.8 %shard_map.84 = (f32[16,1152]{1,0:T(8,128)S(1)}, f32[16,1152]{1,0:T(8,128)S(1)}, f32[16,1152]{1,0:T(8,128)S(1)}, f32[16,1152]{1,0:T(8,128)S(1)}) custom-call(f32[32,256]{1,0:T(8,128)S(1)} %bitcast.13, bf16[256,4096]{1,0:T(8,128)(2,1)S(1)} %get-tuple-element.27.refs_2_.f_ref, bf16[112,4096]{1,0:T(8,128)(2,1)S(1)} %get-tuple-element.41.refs_3_.stack_ref, ...), custom_call_target="tpu_custom_call" | custom-call | tf_op jit(solution)/shard_map/pallas_call | solution.py:324
  65.8 2.3 %collective-permute-start.13 = (f32[16,1152]{1,0:T(8,128)S(1)}, f32[16,1152]{1,0:T(8,128)S(1)}, u32[]{:S(2)}, u32[]{:S(2)}) collective-permute-start(f32[16,1152]{1,0:T(8,128)S(1)} %get-tuple-element.48), channel_id=1, source_target_pairs={{0,6},{2,4},{4,2},{6,0},{8,14},{10,12},{12,10},{14,8},{16,22},{18,... | collective-permute-start | bytes 221192 | tf_op jit(solution)/shard_map/ppermute | solution.py:89
  68.1 1.2 %collective-permute-done.11 = f32[16,1152]{1,0:T(8,128)S(1)} collective-permute-done((f32[16,1152]{1,0:T(8,128)S(1)}, f32[16,1152]{1,0:T(8,128)S(1)}, u32[]{:S(2)}, u32[]{:S(2)}) %collective-permute-start.11) | collective-permute-done | bytes 73760 | tf_op jit(solution)/shard_map/ppermute | solution.py:89
  69.3 1.0 %collective-permute-done.12 = f32[16,1152]{1,0:T(8,128)S(1)} collective-permute-done((f32[16,1152]{1,0:T(8,128)S(1)}, f32[16,1152]{1,0:T(8,128)S(1)}, u32[]{:S(2)}, u32[]{:S(2)}) %collective-permute-start.12) | collective-permute-done | bytes 73760 | tf_op jit(solution)/shard_map/ppermute | solution.py:89
  70.2 0.8 collective-permute-done.13
  71.7 1.5 %collective-permute-start.15 = (f32[16,1152]{1,0:T(8,128)S(1)}, f32[16,1152]{1,0:T(8,128)S(1)}, u32[]{:S(2)}, u32[]{:S(2)}) collective-permute-start(f32[16,1152]{1,0:T(8,128)S(1)} %add_add_fusion.refs_0_), channel_id=1, source_target_pairs={{0,16},{2,18},{4,20},{6,22},{8,24},{10,26},{12,28},{14,30},{16,0},... | collective-permute-start | bytes 221192 | tf_op jit(solution)/shard_map/ppermute | solution.py:89
  73.2 2.3 %collective-permute-start.14 = (f32[16,1152]{1,0:T(8,128)S(1)}, f32[16,1152]{1,0:T(8,128)S(1)}, u32[]{:S(2)}, u32[]{:S(2)}) collective-permute-start(f32[16,1152]{1,0:T(8,128)S(1)} %add_add_fusion.refs_0_), channel_id=1, source_target_pairs={{0,8},{2,10},{4,12},{6,14},{8,0},{10,2},{12,4},{14,6},{16,24},{18,... | collective-permute-start | bytes 221192 | tf_op jit(solution)/shard_map/ppermute | solution.py:89
  75.9 1.5 %collective-permute-done.16.refs_3_ = f32[16,1152]{1,0:T(8,128)S(1)} collective-permute-done((f32[16,1152]{1,0:T(8,128)S(1)}, f32[16,1152]{1,0:T(8,128)S(1)}, u32[]{:S(2)}, u32[]{:S(2)}) %collective-permute-start.16) | collective-permute-done | bytes 73760 | tf_op jit(solution)/shard_map/ppermute | solution.py:89
  77.4 1.6 %collective-permute-done.15.refs_2_ = f32[16,1152]{1,0:T(8,128)S(1)} collective-permute-done((f32[16,1152]{1,0:T(8,128)S(1)}, f32[16,1152]{1,0:T(8,128)S(1)}, u32[]{:S(2)}, u32[]{:S(2)}) %collective-permute-start.15) | collective-permute-done | bytes 73760 | tf_op jit(solution)/shard_map/ppermute | solution.py:89
  79.3 2.1 %collective-permute-start.19 = (f32[16,1152]{1,0:T(8,128)S(1)}, f32[16,1152]{1,0:T(8,128)S(1)}, u32[]{:S(2)}, u32[]{:S(2)}) collective-permute-start(f32[16,1152]{1,0:T(8,128)S(1)} %shard_map.85.refs_0_), channel_id=1, source_target_pairs={{0,6},{2,4},{4,2},{6,0},{8,14},{10,12},{12,10},{14,8},{16,22},{18,... | collective-permute-start | bytes 221192 | tf_op jit(solution)/shard_map/ppermute | solution.py:89
  82.8 1.8 %collective-permute-done.19.refs_3_ = f32[16,1152]{1,0:T(8,128)S(1)} collective-permute-done((f32[16,1152]{1,0:T(8,128)S(1)}, f32[16,1152]{1,0:T(8,128)S(1)}, u32[]{:S(2)}, u32[]{:S(2)}) %collective-permute-start.19) | collective-permute-done | bytes 73760 | tf_op jit(solution)/shard_map/ppermute | solution.py:89
  84.6 1.1 %collective-permute-done.18.refs_2_ = f32[16,1152]{1,0:T(8,128)S(1)} collective-permute-done((f32[16,1152]{1,0:T(8,128)S(1)}, f32[16,1152]{1,0:T(8,128)S(1)}, u32[]{:S(2)}, u32[]{:S(2)}) %collective-permute-start.18) | collective-permute-done | bytes 73760 | tf_op jit(solution)/shard_map/ppermute | solution.py:89
  (29 shorter events, 11.3 us)
Async XLA Ops:
  3.3 1.4 %collective-permute-start = (f32[16,384]{1,0:T(8,128)S(1)}, f32[16,384]{1,0:T(8,128)S(1)}, u32[]{:S(2)}, u32[]{:S(2)}) collective-permute-start(f32[16,384]{1,0:T(8,128)S(1)} %get-tuple-element.28.refs_0_), channel_id=1, source_target_pairs={{0,1},{1,0},{2,3},{3,2},{4,5},{5,4},{6,7},{7,6},{8,9},{9,8},{10,11... | collective-permute-start | bytes 73736 | tf_op jit(solution)/shard_map/ppermute | solution.py:89
  24.3 4.7 %collective-permute-start.1 = (f32[16,1152]{1,0:T(8,128)S(1)}, f32[16,1152]{1,0:T(8,128)S(1)}, u32[]{:S(2)}, u32[]{:S(2)}) collective-permute-start(f32[16,1152]{1,0:T(8,128)S(1)} %get-tuple-element.37), channel_id=1, source_target_pairs={{0,2},{2,0},{4,6},{6,4},{8,10},{10,8},{12,14},{14,12},{16,18},{18,... | collective-permute-start | bytes 221192 | tf_op jit(solution)/shard_map/ppermute | solution.py:89
  24.8 5.1 %collective-permute-start.2 = (f32[16,1152]{1,0:T(8,128)S(1)}, f32[16,1152]{1,0:T(8,128)S(1)}, u32[]{:S(2)}, u32[]{:S(2)}) collective-permute-start(f32[16,1152]{1,0:T(8,128)S(1)} %get-tuple-element.38), channel_id=1, source_target_pairs={{0,4},{2,6},{4,0},{6,2},{8,12},{10,14},{12,8},{14,10},{16,20},{18,... | collective-permute-start | bytes 221192 | tf_op jit(solution)/shard_map/ppermute | solution.py:89
  25.5 5.3 %collective-permute-start.3 = (f32[16,1152]{1,0:T(8,128)S(1)}, f32[16,1152]{1,0:T(8,128)S(1)}, u32[]{:S(2)}, u32[]{:S(2)}) collective-permute-start(f32[16,1152]{1,0:T(8,128)S(1)} %get-tuple-element.39), channel_id=1, source_target_pairs={{0,6},{2,4},{4,2},{6,0},{8,14},{10,12},{12,10},{14,8},{16,22},{18,... | collective-permute-start | bytes 221192 | tf_op jit(solution)/shard_map/ppermute | solution.py:89
  30.8 6.4 %collective-permute-start.6 = (f32[16,1152]{1,0:T(8,128)S(1)}, f32[16,1152]{1,0:T(8,128)S(1)}, u32[]{:S(2)}, u32[]{:S(2)}) collective-permute-start(f32[16,1152]{1,0:T(8,128)S(1)} %add_add_fusion.1.refs_0_), channel_id=1, source_target_pairs={{0,24},{2,26},{4,28},{6,30},{8,16},{10,18},{12,20},{14,22},{16,8},... | collective-permute-start | bytes 221192 | tf_op jit(solution)/shard_map/ppermute | solution.py:89
  31.4 7.3 %collective-permute-start.5 = (f32[16,1152]{1,0:T(8,128)S(1)}, f32[16,1152]{1,0:T(8,128)S(1)}, u32[]{:S(2)}, u32[]{:S(2)}) collective-permute-start(f32[16,1152]{1,0:T(8,128)S(1)} %add_add_fusion.1.refs_0_), channel_id=1, source_target_pairs={{0,16},{2,18},{4,20},{6,22},{8,24},{10,26},{12,28},{14,30},{16,0},... | collective-permute-start | bytes 221192 | tf_op jit(solution)/shard_map/ppermute | solution.py:89
  32.9 5.9 %collective-permute-start.4 = (f32[16,1152]{1,0:T(8,128)S(1)}, f32[16,1152]{1,0:T(8,128)S(1)}, u32[]{:S(2)}, u32[]{:S(2)}) collective-permute-start(f32[16,1152]{1,0:T(8,128)S(1)} %add_add_fusion.1.refs_0_), channel_id=1, source_target_pairs={{0,8},{2,10},{4,12},{6,14},{8,0},{10,2},{12,4},{14,6},{16,24},{18,... | collective-permute-start | bytes 221192 | tf_op jit(solution)/shard_map/ppermute | solution.py:89
  38.9 5.3 %collective-permute-start.9 = (f32[16,1152]{1,0:T(8,128)S(1)}, f32[16,1152]{1,0:T(8,128)S(1)}, u32[]{:S(2)}, u32[]{:S(2)}) collective-permute-start(f32[16,1152]{1,0:T(8,128)S(1)} %shard_map.80.refs_0_.old_ref), channel_id=1, source_target_pairs={{0,6},{2,4},{4,2},{6,0},{8,14},{10,12},{12,10},{14,8},{16,22},{18,... | collective-permute-start | bytes 221192 | tf_op jit(solution)/shard_map/ppermute | solution.py:89
  41.0 4.4 %collective-permute-start.8 = (f32[16,1152]{1,0:T(8,128)S(1)}, f32[16,1152]{1,0:T(8,128)S(1)}, u32[]{:S(2)}, u32[]{:S(2)}) collective-permute-start(f32[16,1152]{1,0:T(8,128)S(1)} %shard_map.80.refs_0_.old_ref), channel_id=1, source_target_pairs={{0,4},{2,6},{4,0},{6,2},{8,12},{10,14},{12,8},{14,10},{16,20},{18,... | collective-permute-start | bytes 221192 | tf_op jit(solution)/shard_map/ppermute | solution.py:89
  41.8 4.4 %collective-permute-start.7 = (f32[16,1152]{1,0:T(8,128)S(1)}, f32[16,1152]{1,0:T(8,128)S(1)}, u32[]{:S(2)}, u32[]{:S(2)}) collective-permute-start(f32[16,1152]{1,0:T(8,128)S(1)} %shard_map.80.refs_0_.old_ref), channel_id=1, source_target_pairs={{0,2},{2,0},{4,6},{6,4},{8,10},{10,8},{12,14},{14,12},{16,18},{18,... | collective-permute-start | bytes 221192 | tf_op jit(solution)/shard_map/ppermute | solution.py:89
  47.1 1.2 %collective-permute-start.10 = (f32[16,384]{1,0:T(8,128)S(1)}, f32[16,384]{1,0:T(8,128)S(1)}, u32[]{:S(2)}, u32[]{:S(2)}) collective-permute-start(f32[16,384]{1,0:T(8,128)S(1)} %get-tuple-element.40.refs_0_), channel_id=1, source_target_pairs={{0,1},{1,0},{2,3},{3,2},{4,5},{5,4},{6,7},{7,6},{8,9},{9,8},{10,11... | collective-permute-start | bytes 73736 | tf_op jit(solution)/shard_map/ppermute | solution.py:89
  60.1 0.7 copy-start
  64.6 4.7 %collective-permute-start.11 = (f32[16,1152]{1,0:T(8,128)S(1)}, f32[16,1152]{1,0:T(8,128)S(1)}, u32[]{:S(2)}, u32[]{:S(2)}) collective-permute-start(f32[16,1152]{1,0:T(8,128)S(1)} %get-tuple-element.46), channel_id=1, source_target_pairs={{0,2},{2,0},{4,6},{6,4},{8,10},{10,8},{12,14},{14,12},{16,18},{18,... | collective-permute-start | bytes 221192 | tf_op jit(solution)/shard_map/ppermute | solution.py:89
  65.1 5.1 %collective-permute-start.12 = (f32[16,1152]{1,0:T(8,128)S(1)}, f32[16,1152]{1,0:T(8,128)S(1)}, u32[]{:S(2)}, u32[]{:S(2)}) collective-permute-start(f32[16,1152]{1,0:T(8,128)S(1)} %get-tuple-element.47), channel_id=1, source_target_pairs={{0,4},{2,6},{4,0},{6,2},{8,12},{10,14},{12,8},{14,10},{16,20},{18,... | collective-permute-start | bytes 221192 | tf_op jit(solution)/shard_map/ppermute | solution.py:89
  65.8 5.3 %collective-permute-start.13 = (f32[16,1152]{1,0:T(8,128)S(1)}, f32[16,1152]{1,0:T(8,128)S(1)}, u32[]{:S(2)}, u32[]{:S(2)}) collective-permute-start(f32[16,1152]{1,0:T(8,128)S(1)} %get-tuple-element.48), channel_id=1, source_target_pairs={{0,6},{2,4},{4,2},{6,0},{8,14},{10,12},{12,10},{14,8},{16,22},{18,... | collective-permute-start | bytes 221192 | tf_op jit(solution)/shard_map/ppermute | solution.py:89
  71.1 6.4 %collective-permute-start.16 = (f32[16,1152]{1,0:T(8,128)S(1)}, f32[16,1152]{1,0:T(8,128)S(1)}, u32[]{:S(2)}, u32[]{:S(2)}) collective-permute-start(f32[16,1152]{1,0:T(8,128)S(1)} %add_add_fusion.refs_0_), channel_id=1, source_target_pairs={{0,24},{2,26},{4,28},{6,30},{8,16},{10,18},{12,20},{14,22},{16,8},... | collective-permute-start | bytes 221192 | tf_op jit(solution)/shard_map/ppermute | solution.py:89
  71.7 7.3 %collective-permute-start.15 = (f32[16,1152]{1,0:T(8,128)S(1)}, f32[16,1152]{1,0:T(8,128)S(1)}, u32[]{:S(2)}, u32[]{:S(2)}) collective-permute-start(f32[16,1152]{1,0:T(8,128)S(1)} %add_add_fusion.refs_0_), channel_id=1, source_target_pairs={{0,16},{2,18},{4,20},{6,22},{8,24},{10,26},{12,28},{14,30},{16,0},... | collective-permute-start | bytes 221192 | tf_op jit(solution)/shard_map/ppermute | solution.py:89
  73.2 5.9 %collective-permute-start.14 = (f32[16,1152]{1,0:T(8,128)S(1)}, f32[16,1152]{1,0:T(8,128)S(1)}, u32[]{:S(2)}, u32[]{:S(2)}) collective-permute-start(f32[16,1152]{1,0:T(8,128)S(1)} %add_add_fusion.refs_0_), channel_id=1, source_target_pairs={{0,8},{2,10},{4,12},{6,14},{8,0},{10,2},{12,4},{14,6},{16,24},{18,... | collective-permute-start | bytes 221192 | tf_op jit(solution)/shard_map/ppermute | solution.py:89
  79.3 5.3 %collective-permute-start.19 = (f32[16,1152]{1,0:T(8,128)S(1)}, f32[16,1152]{1,0:T(8,128)S(1)}, u32[]{:S(2)}, u32[]{:S(2)}) collective-permute-start(f32[16,1152]{1,0:T(8,128)S(1)} %shard_map.85.refs_0_), channel_id=1, source_target_pairs={{0,6},{2,4},{4,2},{6,0},{8,14},{10,12},{12,10},{14,8},{16,22},{18,... | collective-permute-start | bytes 221192 | tf_op jit(solution)/shard_map/ppermute | solution.py:89
  81.4 4.4 %collective-permute-start.18 = (f32[16,1152]{1,0:T(8,128)S(1)}, f32[16,1152]{1,0:T(8,128)S(1)}, u32[]{:S(2)}, u32[]{:S(2)}) collective-permute-start(f32[16,1152]{1,0:T(8,128)S(1)} %shard_map.85.refs_0_), channel_id=1, source_target_pairs={{0,4},{2,6},{4,0},{6,2},{8,12},{10,14},{12,8},{14,10},{16,20},{18,... | collective-permute-start | bytes 221192 | tf_op jit(solution)/shard_map/ppermute | solution.py:89
  82.1 4.4 %collective-permute-start.17 = (f32[16,1152]{1,0:T(8,128)S(1)}, f32[16,1152]{1,0:T(8,128)S(1)}, u32[]{:S(2)}, u32[]{:S(2)}) collective-permute-start(f32[16,1152]{1,0:T(8,128)S(1)} %shard_map.85.refs_0_), channel_id=1, source_target_pairs={{0,2},{2,0},{4,6},{6,4},{8,10},{10,8},{12,14},{14,12},{16,18},{18,... | collective-permute-start | bytes 221192 | tf_op jit(solution)/shard_map/ppermute | solution.py:89

commit v3 on v2

v3 whole, which is shorter than its diff:
```python
import functools

import jax
import jax.numpy as jnp
from jax import lax
from jax.experimental import pallas as pl
from jax.experimental.pallas import tpu as pltpu
from jax.sharding import PartitionSpec as P

ROW_PX = 2048
BLOCK = 128
ITERS = 2
RIDGE = 0.01
VMEM_LIMIT = 48 * 1024 * 1024

F32 = jnp.float32
BF16 = jnp.bfloat16
NN = (((1,), (0,)), ((), ()))
NT = (((1,), (1,)), ((), ()))


def params():
    return pltpu.CompilerParams(vmem_limit_bytes=VMEM_LIMIT)


def vmem(n):
    return [pl.BlockSpec(memory_space=pltpu.VMEM)] * n


SMEM = pl.BlockSpec(memory_space=pltpu.SMEM)


def split3(x):
    hi = x.astype(BF16)
    rest = x - hi.astype(F32)
    mid = rest.astype(BF16)
    low = (rest - mid.astype(F32)).astype(BF16)
    return hi, mid, low


def solve_spd(gram, sides):
    r = gram.shape[0]
    columns = [jnp.broadcast_to(gram[:, j : j + 1], (r, BLOCK)) for j in range(r)]
    rows = lax.broadcasted_iota(jnp.int32, (r, BLOCK), 0)
    for k in range(r):
        pivot = columns[k]
        inverse = 1.0 / pivot[k : k + 1, :]

        def step(x):
            scaled = x[k : k + 1, :] * inverse
            return jnp.where(rows == k, scaled, x - pivot * scaled)

        columns = columns[: k + 1] + [step(c) for c in columns[k + 1 :]]
        sides = [step(x) for x in sides]
    return sides


def eye_at(shape, first):
    row = lax.broadcasted_iota(jnp.int32, shape, 0)
    col = lax.broadcasted_iota(jnp.int32, shape, 1)
    return (col == row + first).astype(F32)


class Sizes:
    def __init__(self, tile_dev, pix_dev, rank, n_tiles, n_pix):
        self.tile_dev, self.pix_dev, self.rank = tile_dev, pix_dev, rank
        self.n_tiles, self.n_pix = n_tiles, n_pix
        self.tiles_all, self.pixels_all = tile_dev * n_tiles, pix_dev * n_pix
        self.tile_levels = levels(n_tiles)
        self.group = len(self.tile_levels[0]) + 1 if self.tile_levels else 1
        self.chunk = pix_dev // self.group
        self.blocks = self.chunk // BLOCK
        self.extra = BLOCK * (-(-2 * self.blocks // rank))
        self.stack = 6 * rank + 16
        self.spot, self.twin = rank * rank - 2, rank * rank - rank - 1


def levels(n):
    if n & (n - 1):
        return None
    out, bit = [], 1
    while bit < n:
        out.append((bit, 2 * bit, 3 * bit) if 4 * bit <= n else (bit,))
        bit *= 4
    return out


def partner(x, axis, mask):
    n = lax.axis_size(axis)
    return lax.ppermute(x, axis, [(i, i ^ mask) for i in range(n)])


def tree(parts):
    while len(parts) > 1:
        parts = [a + b for a, b in zip(parts[::2], parts[1::2])]
    return parts[0]


def sum_level(x, axis, masks):
    return tree([x] + [partner(x, axis, m) for m in masks])


def stack_block(sz, stack_ref, b, d_rows):
    r = sz.rank
    hi, mid, low = split3(b)
    for at, part in enumerate((hi, mid, low, hi, mid, hi)):
        stack_ref[at * r : (at + 1) * r, :] = part
    row = lax.broadcasted_iota(jnp.int32, (16, BLOCK), 0)
    for j, d in enumerate(d_rows):
        d_hi, d_mid, d_low = (part.astype(F32) for part in split3(d))
        tile = jnp.where(row == 0, d_hi, jnp.where(row == 1, d_mid, jnp.where(row == 2, d_low, 0.0)))
        stack_ref[6 * r : 6 * r + 16, j * BLOCK : (j + 1) * BLOCK] = tile.astype(BF16)


def project_chunk(sz, frames, stack_ref, b, d_rows, totals):
    r = sz.rank
    stack_block(sz, stack_ref, b, d_rows)
    parts = stack_ref[0 : 3 * r, :]
    proj = lax.dot_general(parts, frames, NT, preferred_element_type=F32)
    gram = lax.dot_general(parts, parts, NT, preferred_element_type=F32)
    dark = tree([b[:, j * BLOCK : (j + 1) * BLOCK] * d for j, d in enumerate(d_rows)])
    new = (proj, gram, dark)
    return new if totals is None else tuple(a + b for a, b in zip(totals, new))


def pack_projections(sz, totals, packed_ref, before_ref=None):
    r, td = sz.rank, sz.tile_dev
    proj, gram, dark = totals
    proj = proj[0:r] + proj[r : 2 * r] + proj[2 * r : 3 * r] - jnp.sum(dark, axis=1, keepdims=True)
    gram = gram[0:r] + gram[r : 2 * r] + gram[2 * r : 3 * r]
    gram = gram[:, 0:r] + gram[:, r : 2 * r] + gram[:, 2 * r : 3 * r]
    if before_ref is None:
        packed_ref[:, td : td + BLOCK] = jnp.zeros((r, BLOCK), F32)
    else:
        proj = proj + before_ref[:, 0:td]
        packed_ref[:, td : td + BLOCK] = before_ref[:, td : td + BLOCK]
        gram = gram + before_ref[:, td : td + r]
    packed_ref[:, 0:td] = proj
    packed_ref[:, td : td + r] = gram


def start_of(sz, k):
    me = lax.axis_index("tiles") & (sz.group - 1)
    return pl.multiple_of((me ^ k) * sz.chunk, BLOCK)


def first_projection(sz, f_hbm, b_hbm, d_hbm, valid_hbm, fore_hbm, f_ref, packed_ref, own_ref, least_ref, valid_ref, *refs):
    stack_refs, (b_ref, d_ref, flags_ref, sems) = refs[: sz.group], refs[sz.group :]
    small = [
        pltpu.make_async_copy(d_hbm, d_ref, sems.at[0]),
        pltpu.make_async_copy(b_hbm, b_ref, sems.at[1]),
        pltpu.make_async_copy(valid_hbm, flags_ref.at[0:1], sems.at[2]),
        pltpu.make_async_copy(fore_hbm, flags_ref.at[8:9], sems.at[3]),
    ]
    spans = [pl.ds(start_of(sz, k), sz.chunk) for k in range(sz.group)]
    large = [pltpu.make_async_copy(f_hbm.at[:, s], f_ref.at[:, s], sems.at[4 + k]) for k, s in enumerate(spans)]
    for copy in small + large:
        copy.start()
    for copy in small:
        copy.wait()
    valid = flags_ref[0:1, :] != 0
    valid_ref[...] = jnp.broadcast_to(valid.astype(F32), valid_ref.shape)
    least_ref[...] = jnp.broadcast_to(jnp.where(valid, flags_ref[8:9, :], ROW_PX), (BLOCK, sz.tile_dev)).T
    me = lax.axis_index("tiles") & (sz.group - 1)
    own_ref[:, 0 : sz.chunk] = b_ref[:, spans[0]]
    own_ref[:, sz.chunk :] = jnp.zeros((sz.rank, sz.extra), F32)
    for j in range(sz.blocks):
        own_ref[j % sz.rank, pl.ds(sz.chunk + j // sz.rank * BLOCK, BLOCK)] = d_ref[me * sz.blocks + j, :]
    totals = None
    for k in range(sz.group):
        d_rows = [d_ref[pl.ds((me ^ k) * sz.blocks + j, 1), :] for j in range(sz.blocks)]
        b = b_ref[:, spans[k]]
        large[k].wait()
        totals = project_chunk(sz, f_ref[:, spans[k]], stack_refs[k], b, d_rows, totals)
    pack_projections(sz, totals, packed_ref)


def later_projection(sz, k, f_ref, chunk_ref, *refs):
    before_ref, packed_ref, stack_ref = refs if len(refs) == 3 else (None,) + refs
    d_rows = []
    for j in range(sz.blocks):
        lane = sz.chunk + j // sz.rank * BLOCK
        d_rows.append(chunk_ref[j % sz.rank : j % sz.rank + 1, lane : lane + BLOCK])
    frames = f_ref[:, pl.ds(start_of(sz, k), sz.chunk)]
    totals = project_chunk(sz, frames, stack_ref, chunk_ref[:, 0 : sz.chunk], d_rows, None)
    pack_projections(sz, totals, packed_ref, before_ref)


def residual(sz, f_ref, stack_ref, parts, start, step, width):
    model = lax.dot_general(
        parts, stack_ref[:, step * width : (step + 1) * width], NN, preferred_element_type=F32
    )
    return f_ref[:, pl.ds(pl.multiple_of(start + step * width, BLOCK), width)].astype(F32) - model


def solve_tiles(sz, width, *refs):
    packed = refs[: sz.n_pix]
    stack_refs, refs = refs[sz.n_pix : sz.n_pix + sz.group], refs[sz.n_pix + sz.group :]
    f_ref, least_ref, valid_ref, coef_ref, three_ref, parts_ref, note_ref = refs
    r, td = sz.rank, sz.tile_dev
    a = tree([ref[...] for ref in packed]) / sz.pixels_all
    gram = a[:, td : td + r] + RIDGE * eye_at((r, r), 0)
    sides = [a[:, at : at + BLOCK] for at in range(0, td, BLOCK)]
    coef = jnp.concatenate(solve_spd(gram, sides), axis=1)
    coef_ref[...] = coef
    hi, mid, low = split3(coef)
    three_ref[...] = jnp.concatenate([hi, mid, jnp.ones((16, td), BF16), low], axis=0)
    row = lax.broadcasted_iota(jnp.int32, (BLOCK - 6 * r, td), 0)
    ones = (row < 3).astype(F32)
    hi, mid, low = hi.astype(F32), mid.astype(F32), low.astype(F32)
    parts = jnp.concatenate([hi, hi, hi, mid, mid, low, ones], axis=0).T.astype(BF16)
    parts_ref[...] = parts
    parts = parts[:, 0 : sz.stack]
    least = least_ref[...]

    total = jnp.zeros((8, BLOCK), F32)
    for k, stack_ref in enumerate(stack_refs):
        start = start_of(sz, k)
        for step in range(sz.chunk // width):
            res = residual(sz, f_ref, stack_ref, parts, start, step, width)
            square = res * res
            for j in range(width // BLOCK):
                block = (start // BLOCK + step * (width // BLOCK) + j) % (ROW_PX // BLOCK)
                term = jnp.where(least <= block, square[:, j * BLOCK : (j + 1) * BLOCK], 0.0)
                total = total + jnp.sum(term.reshape(td // 8, 8, BLOCK), axis=0)
    total = jnp.sum(jnp.sum(total, axis=0, keepdims=True), axis=1, keepdims=True)
    products = jnp.concatenate([coef[i : i + 1] * coef for i in range(r)], axis=0)
    ones = valid_ref[...].astype(BF16)
    flat = sum(lax.dot_general(ones, part, NT, preferred_element_type=F32) for part in split3(products))
    lane = lax.broadcasted_iota(jnp.int32, flat.shape, 1)
    flat = jnp.where(lane == sz.spot, total, flat)
    for at in range(0, note_ref.shape[0], 8):
        note_ref[at : at + 8, :] = flat


def invert_gram(sz, note_ref, inverse_ref):
    r = sz.rank
    flat = jnp.sum(note_ref[...], axis=0, keepdims=True)
    gram = jnp.concatenate([flat[:, i * r : (i + 1) * r] for i in range(r)], axis=0)
    row = lax.broadcasted_iota(jnp.int32, (r, r), 0)
    col = lax.broadcasted_iota(jnp.int32, (r, r), 1)
    twin = flat[:, sz.twin : sz.twin + 1]
    gram = jnp.where((row == r - 1) & (col == r - 2), twin, gram)
    gram = gram / (sz.n_pix * sz.tiles_all) + RIDGE * eye_at((r, r), 0)
    (inverse_ref[...],) = solve_spd(gram, [eye_at((r, BLOCK), 0)])


def update_terms(sz, width, k, note_ref, f_ref, stack_ref, least_ref, three_ref, parts_ref, out_ref):
    r = sz.rank
    start = start_of(sz, k)
    total = jnp.sum(note_ref[:, sz.spot : sz.spot + 1], axis=0, keepdims=True)
    spread = total / (sz.tiles_all * sz.pixels_all) + 1e-05
    scale = jnp.broadcast_to(1.0 / (4.0 * spread), (8, BLOCK))[0:1, :]
    parts = parts_ref[:, 0 : sz.stack]
    three = three_ref[...]
    two = three[0 : 2 * r + 16]
    least = least_ref[...]
    each = width // BLOCK

    def place(flat):
        lane = sz.chunk + flat // r * BLOCK
        return slice(flat % r, flat % r + 1), slice(lane, lane + BLOCK)

    for step in range(sz.chunk // width):
        res = residual(sz, f_ref, stack_ref, parts, start, step, width)
        hi_parts, mid_parts = [], []
        for j in range(each):
            block = (start // BLOCK + step * each + j) % (ROW_PX // BLOCK)
            x = res[:, j * BLOCK : (j + 1) * BLOCK]
            g = jnp.where(least <= block, pl.reciprocal(x * x * scale + 1.0, approx=True), 0.0)
            out_ref[place(sz.blocks + step * each + j)] = jnp.sum(g, axis=0, keepdims=True)
            w = g * x
            w_hi = w.astype(BF16)
            hi_parts.append(w_hi)
            mid_parts.append((w - w_hi.astype(F32)).astype(BF16))
        terms = lax.dot_general(three, jnp.concatenate(hi_parts, axis=1), NN, preferred_element_type=F32)
        more = lax.dot_general(two, jnp.concatenate(mid_parts, axis=1), NN, preferred_element_type=F32)
        out_ref[:, step * width : (step + 1) * width] = terms[0:r] + (
            terms[r : 2 * r] + terms[2 * r + 16 :] + more[0:r] + more[r : 2 * r]
        )
        sums = terms[2 * r : 2 * r + 1] + more[2 * r : 2 * r + 1]
        for j in range(each):
            out_ref[place(step * each + j)] = sums[:, j * BLOCK : (j + 1) * BLOCK]
    used = 2 * sz.blocks
    if used % r:
        out_ref[used % r :, sz.chunk + used // r * BLOCK :] = jnp.zeros((r - used % r, BLOCK), F32)


def update_chunk(sz, inverse_ref, old_ref, *refs):
    total_refs, new_ref = refs[:-1], refs[-1]
    r = sz.rank
    totals = tree([ref[...] for ref in total_refs])
    inverse = inverse_ref[:, 0:r]
    change = jnp.dot(inverse, totals[:, 0 : sz.chunk] / sz.tiles_all, precision=lax.Precision.HIGHEST, preferred_element_type=F32)
    new_ref[:, 0 : sz.chunk] = old_ref[:, 0 : sz.chunk] + change
    new_ref[:, sz.chunk :] = jnp.zeros((r, sz.extra), F32)

    def place(flat):
        return flat % r, sz.chunk + flat // r * BLOCK

    many = 8 if sz.blocks % 8 == 0 else 1
    for j in range(0, sz.blocks, many):
        (row, lane), (row_g, lane_g) = place(j), place(sz.blocks + j)
        w = totals[row : row + many, lane : lane + BLOCK]
        g = totals[row_g : row_g + many, lane_g : lane_g + BLOCK]
        new_ref[row : row + many, lane : lane + BLOCK] = (
            old_ref[row : row + many, lane : lane + BLOCK] + w / (g + 1.0)
        )


def assemble(sz, coef_ref, *refs):
    chunks, (b_ref, d_ref, coef_out_ref) = refs[: sz.group], refs[sz.group :]
    coef_out_ref[...] = coef_ref[...]
    me = lax.axis_index("tiles") & (sz.group - 1)
    for k, ref in enumerate(chunks):
        c = me ^ k
        b_ref[:, pl.ds(pl.multiple_of(c * sz.chunk, BLOCK), sz.chunk)] = ref[:, 0 : sz.chunk]
        for j in range(sz.blocks):
            lane = sz.chunk + j // sz.rank * BLOCK
            d_ref[c * sz.blocks + j, :] = ref[j % sz.rank, lane : lane + BLOCK]


def call(body, outs, ins, in_hbm=False, scratch=()):
    return pl.pallas_call(
        body,
        out_shape=[jax.ShapeDtypeStruct(s, t) for s, t in outs],
        in_specs=[pl.BlockSpec(memory_space=pltpu.HBM)] * len(ins) if in_hbm else vmem(len(ins)),
        out_specs=vmem(len(outs)),
        scratch_shapes=scratch,
        compiler_params=params(),
    )(*([pltpu.with_memory_space_constraint(x, pltpu.HBM) for x in ins] if in_hbm else ins))


def local(frames, tile_valid, foreground_blocks, basis_start, dark_start):
    td, pd = frames.shape
    r = basis_start.shape[0]
    sz = Sizes(td, pd, r, lax.axis_size("tiles"), lax.axis_size("pix"))
    everyone = ("tiles", "pix")
    devices = sz.n_tiles * sz.n_pix
    pix_masks = range(1, sz.n_pix)
    width = min(256, sz.chunk)
    chunk_shape = (r, sz.chunk + sz.extra)
    packed_out = ((r, td + BLOCK), F32)
    stack_out = ((sz.stack, sz.chunk), BF16)
    masks = sz.tile_levels[0]
    for iteration in range(ITERS):
        if iteration == 0:
            frames, packed, old, least, valid, *stacks = call(
                functools.partial(first_projection, sz),
                [((td, pd), BF16), packed_out, (chunk_shape, F32), ((td, BLOCK), jnp.int32), ((8, td), F32)]
                + [stack_out] * sz.group,
                [frames, basis_start, dark_start.reshape(pd // BLOCK, BLOCK), tile_valid.reshape(1, td), foreground_blocks.reshape(1, td)],
                in_hbm=True,
                scratch=[
                    pltpu.VMEM((r, pd), F32),
                    pltpu.VMEM((pd // BLOCK, BLOCK), F32),
                    pltpu.VMEM((16, td), jnp.int32),
                    pltpu.SemaphoreType.DMA((4 + sz.group,)),
                ],
            )
        else:
            before, stacks = [], [None] * sz.group
            for k in [0] + list(masks)[::-1]:
                packed, stacks[k] = call(
                    functools.partial(later_projection, sz, k), [packed_out, stack_out], [frames, chunks[k]] + before
                )
                before = [packed]
        both = [packed] + [partner(packed, "pix", m) for m in pix_masks]
        coef, three, parts, note = call(
            functools.partial(solve_tiles, sz, width),
            [((r, td), F32), ((3 * r + 16, td), BF16), ((td, BLOCK), BF16), ((devices, r * r), F32)],
            both + stacks + [frames, least, valid],
        )
        notes = lax.all_to_all(note, everyone, 0, 0, tiled=True)
        (inverse,) = call(functools.partial(invert_gram, sz), [((r, BLOCK), F32)], [notes])
        terms = {}
        for k in list(masks) + [0]:
            (terms[k],) = call(
                functools.partial(update_terms, sz, width, k),
                [(chunk_shape, F32)],
                [notes, frames, stacks[k], least, three, parts],
            )
        total = tree([terms[0]] + [partner(terms[m], "tiles", m) for m in masks])
        later = sz.tile_levels[1:]
        for level in later[:-1]:
            total = sum_level(total, "tiles", level)
        totals = [total] + [partner(total, "tiles", m) for m in (later[-1] if later else ())]
        (old,) = call(functools.partial(update_chunk, sz), [(chunk_shape, F32)], [inverse, old] + totals)
        chunks = [old] + [partner(old, "tiles", m) for m in masks]
    basis, dark, coef = call(
        functools.partial(assemble, sz),
        [((r, pd), F32), ((pd // BLOCK, BLOCK), F32), ((r, td), F32)],
        [coef] + chunks,
    )
    return basis, dark.reshape(pd), coef.T


def solution(mesh):
    return jax.shard_map(
        local,
        mesh=mesh,
        in_specs=(P("tiles", "pix"), P("tiles"), P("tiles"), P(None, "pix"), P("pix")),
        out_specs=(P(None, "pix"), P("pix"), P("tiles", None)),
        check_vma=False,
    )
```

time: 87.6 us -> 83.5 us (0.953)
  waiting for transfers between devices: 21.7 us -> 19.1 us
    ppermute x20, waiting for transfers between devices: 21.7 us -> 19.1 us  [partner(): return lax.ppermute(x, axis, [(i, i ^ mask) for i in range(n)])]
    pallas_call x11 -> x20, Pallas kernels: 16.3 us -> 15.6 us  [call(): pl.pallas_call(body, out_shape=[jax.ShapeDtypeStruct(s, t) for s, t in ou...]
  transfers between devices with their start and end apart: 20 -> 20, of which waited for: 18 -> 18; matrix products, arithmetic and copies ran while one was open for 0% -> 0% of each run, Pallas kernels for 1% -> 4%
where the time goes in v3:
time: 83.5 us; the launch traced here: 83.3 us
  blocking collectives  24.2 us (29%)
  starting transfers between devices  23.5 us (28%)
  waiting for transfers between devices  19.1 us (23%)
  Pallas kernels  15.6 us (19%)
    all_to_all x2, blocking collectives, local(): notes = lax.all_to_all(note, everyone, 0, 0, tiled=True)  24.2 us
    ppermute x20, starting transfers between devices, partner(): return lax.ppermute(x, axis, [(i, i ^ mask) for i in range(n)])  23.5 us
    ppermute x20, waiting for transfers between devices, partner(): return lax.ppermute(x, axis, [(i, i ^ mask) for i in range(n)])  19.1 us
    pallas_call x20, Pallas kernels, call(): pl.pallas_call(body, out_shape=[jax.ShapeDtypeStruct(s, t) for s, t in ou...  15.6 us
  transfers between devices with their start and end apart: 20, of which 18 were waited for; matrix products, arithmetic and copies ran while one was open for 0% of the time, Pallas kernels for 4%

profile of v3, /device:TPU:0, one launch (start us, length us, event | category | flops | bytes accessed | tf_op | source)
XLA Modules:
  0.0 83.3 jit_solution(7804266524025026092)
XLA Ops:
  0.6 2.8 %shard_map.76 = (bf16[256,4096]{1,0:T(8,128)(2,1)S(1)}, f32[16,384]{1,0:T(8,128)S(1)}, f32[16,1152]{1,0:T(8,128)S(1)}, s32[256,128]{1,0:T(8,128)S(1)}, f32[8,256...) custom-call(bf16[256,4096]{1,0:T(8,128)(2,1)} %f_hbm.1, ...), custom_call_target="tpu_custom_call" | custom-call | tf_op jit(solution)/shard_map/pallas_call | solution.py:324
  3.9 0.8 %collective-permute-done.refs_1_ = f32[16,384]{1,0:T(8,128)S(1)} collective-permute-done((f32[16,384]{1,0:T(8,128)S(1)}, f32[16,384]{1,0:T(8,128)S(1)}, u32[]{:S(2)}, u32[]{:S(2)}) %collective-permute-start) | collective-permute-done | bytes 24608 | tf_op jit(solution)/shard_map/ppermute | solution.py:90
  4.8 2.0 %shard_map.77 = (f32[16,256]{1,0:T(8,128)}, bf16[64,256]{1,0:T(8,128)(2,1)S(1)}, bf16[256,128]{1,0:T(8,128)(2,1)S(1)}, f32[32,256]{1,0:T(8,128)S(1)}) custom-call(f32[16,384]{1,0:T(8,128)S(1)} %get-tuple-element.31.refs_0_, f32[16,384]{1,0:T(8,128)S(1)} %collective-permute-done.refs_1_, bf16[112,1024]{1,0:T(8,128)(2,1)S(1)} %get-tuple-element.32.refs_2_.stack_ref, ...), custom_call_target="tpu_custom_call" | custom-call | tf_op jit(solution)/shard_map/pallas_call | solution.py:324
  6.8 14.2 %all_to_all.22 = f32[32,1,256]{2,1,0:T(1,128)S(1)} all-to-all(f32[32,1,256]{2,1,0:T(1,128)S(1)} %copy.8), channel_id=1, replica_groups=mesh['tiles'=16,'pix'=2] {'tiles','pix'}, dimensions={0} | all-to-all | bytes 65536 | tf_op jit(solution)/shard_map/all_to_all | solution.py:374
  21.8 0.8 shard_map.81
  22.6 0.8 shard_map.80
  24.6 2.3 %collective-permute-start.3 = (f32[16,1152]{1,0:T(8,128)S(1)}, f32[16,1152]{1,0:T(8,128)S(1)}, u32[]{:S(2)}, u32[]{:S(2)}) collective-permute-start(f32[16,1152]{1,0:T(8,128)S(1)} %shard_map.82), channel_id=1, source_target_pairs={{0,6},{2,4},{4,2},{6,0},{8,14},{10,12},{12,10},{14,8},{16,22},{18,... | collective-permute-start | bytes 221192 | tf_op jit(solution)/shard_map/ppermute | solution.py:90
  28.0 1.0 %collective-permute-done.2 = f32[16,1152]{1,0:T(8,128)S(1)} collective-permute-done((f32[16,1152]{1,0:T(8,128)S(1)}, f32[16,1152]{1,0:T(8,128)S(1)}, u32[]{:S(2)}, u32[]{:S(2)}) %collective-permute-start.2) | collective-permute-done | bytes 73760 | tf_op jit(solution)/shard_map/ppermute | solution.py:90
  29.0 0.8 collective-permute-done.3
  30.5 1.5 %collective-permute-start.5 = (f32[16,1152]{1,0:T(8,128)S(1)}, f32[16,1152]{1,0:T(8,128)S(1)}, u32[]{:S(2)}, u32[]{:S(2)}) collective-permute-start(f32[16,1152]{1,0:T(8,128)S(1)} %add_add_fusion.1.refs_0_), channel_id=1, source_target_pairs={{0,16},{2,18},{4,20},{6,22},{8,24},{10,26},{12,28},{14,30},{16,0},... | collective-permute-start | bytes 221192 | tf_op jit(solution)/shard_map/ppermute | solution.py:90
  32.0 2.3 %collective-permute-start.4 = (f32[16,1152]{1,0:T(8,128)S(1)}, f32[16,1152]{1,0:T(8,128)S(1)}, u32[]{:S(2)}, u32[]{:S(2)}) collective-permute-start(f32[16,1152]{1,0:T(8,128)S(1)} %add_add_fusion.1.refs_0_), channel_id=1, source_target_pairs={{0,8},{2,10},{4,12},{6,14},{8,0},{10,2},{12,4},{14,6},{16,24},{18,... | collective-permute-start | bytes 221192 | tf_op jit(solution)/shard_map/ppermute | solution.py:90
  34.7 1.6 %collective-permute-done.6.refs_3_ = f32[16,1152]{1,0:T(8,128)S(1)} collective-permute-done((f32[16,1152]{1,0:T(8,128)S(1)}, f32[16,1152]{1,0:T(8,128)S(1)}, u32[]{:S(2)}, u32[]{:S(2)}) %collective-permute-start.6) | collective-permute-done | bytes 73760 | tf_op jit(solution)/shard_map/ppermute | solution.py:90
  36.2 1.6 %collective-permute-done.5.refs_2_ = f32[16,1152]{1,0:T(8,128)S(1)} collective-permute-done((f32[16,1152]{1,0:T(8,128)S(1)}, f32[16,1152]{1,0:T(8,128)S(1)}, u32[]{:S(2)}, u32[]{:S(2)}) %collective-permute-start.5) | collective-permute-done | bytes 73760 | tf_op jit(solution)/shard_map/ppermute | solution.py:90
  38.0 2.1 %collective-permute-start.9 = (f32[16,1152]{1,0:T(8,128)S(1)}, f32[16,1152]{1,0:T(8,128)S(1)}, u32[]{:S(2)}, u32[]{:S(2)}) collective-permute-start(f32[16,1152]{1,0:T(8,128)S(1)} %shard_map.83.chunk_ref.old_ref), channel_id=1, source_target_pairs={{0,6},{2,4},{4,2},{6,0},{8,14},{10,12},{12,10},{14,8},{16,22},{18,... | collective-permute-start | bytes 221192 | tf_op jit(solution)/shard_map/ppermute | solution.py:90
  41.9 1.4 %collective-permute-done.9.chunk_ref = f32[16,1152]{1,0:T(8,128)S(1)} collective-permute-done((f32[16,1152]{1,0:T(8,128)S(1)}, f32[16,1152]{1,0:T(8,128)S(1)}, u32[]{:S(2)}, u32[]{:S(2)}) %collective-permute-start.9) | collective-permute-done | bytes 73760 | tf_op jit(solution)/shard_map/ppermute | solution.py:90
  43.7 0.8 collective-permute-done.8.chunk_ref
  45.6 1.2 %collective-permute-done.10.refs_1_ = f32[16,384]{1,0:T(8,128)S(1)} collective-permute-done((f32[16,384]{1,0:T(8,128)S(1)}, f32[16,384]{1,0:T(8,128)S(1)}, u32[]{:S(2)}, u32[]{:S(2)}) %collective-permute-start.10) | collective-permute-done | bytes 24608 | tf_op jit(solution)/shard_map/ppermute | solution.py:90
  46.8 1.5 %shard_map.88 = (f32[16,256]{1,0:T(8,128)S(1)}, bf16[64,256]{1,0:T(8,128)(2,1)S(1)}, bf16[256,128]{1,0:T(8,128)(2,1)S(1)}, f32[32,256]{1,0:T(8,128)S(1)}) custom-call(f32[16,384]{1,0:T(8,128)S(1)} %get-tuple-element.45.refs_0_, f32[16,384]{1,0:T(8,128)S(1)} %collective-permute-done.10.refs_1_, bf16[112,1024]{1,0:T(8,128)(2,1)S(1)} %get-tuple-element.46.refs_2_.stack_ref, ...), custom_call_target="tpu_custom_call" | custom-call | tf_op jit(solution)/shard_map/pallas_call | solution.py:324
  48.4 10.0 %all_to_all.23 = f32[32,1,256]{2,1,0:T(1,128)S(1)} all-to-all(f32[32,1,256]{2,1,0:T(1,128)S(1)} %copy.9), channel_id=1, replica_groups=mesh['tiles'=16,'pix'=2] {'tiles','pix'}, dimensions={0} | all-to-all | bytes 65536 | tf_op jit(solution)/shard_map/all_to_all | solution.py:374
  59.1 0.8 shard_map.92
  59.9 0.8 shard_map.91
  61.9 2.3 %collective-permute-start.13 = (f32[16,1152]{1,0:T(8,128)S(1)}, f32[16,1152]{1,0:T(8,128)S(1)}, u32[]{:S(2)}, u32[]{:S(2)}) collective-permute-start(f32[16,1152]{1,0:T(8,128)S(1)} %shard_map.93), channel_id=1, source_target_pairs={{0,6},{2,4},{4,2},{6,0},{8,14},{10,12},{12,10},{14,8},{16,22},{18,... | collective-permute-start | bytes 221192 | tf_op jit(solution)/shard_map/ppermute | solution.py:90
  65.3 1.0 %collective-permute-done.12 = f32[16,1152]{1,0:T(8,128)S(1)} collective-permute-done((f32[16,1152]{1,0:T(8,128)S(1)}, f32[16,1152]{1,0:T(8,128)S(1)}, u32[]{:S(2)}, u32[]{:S(2)}) %collective-permute-start.12) | collective-permute-done | bytes 73760 | tf_op jit(solution)/shard_map/ppermute | solution.py:90
  66.3 0.8 collective-permute-done.13
  67.8 1.5 %collective-permute-start.15 = (f32[16,1152]{1,0:T(8,128)S(1)}, f32[16,1152]{1,0:T(8,128)S(1)}, u32[]{:S(2)}, u32[]{:S(2)}) collective-permute-start(f32[16,1152]{1,0:T(8,128)S(1)} %add_add_fusion.refs_0_), channel_id=1, source_target_pairs={{0,16},{2,18},{4,20},{6,22},{8,24},{10,26},{12,28},{14,30},{16,0},... | collective-permute-start | bytes 221192 | tf_op jit(solution)/shard_map/ppermute | solution.py:90
  69.3 2.3 %collective-permute-start.14 = (f32[16,1152]{1,0:T(8,128)S(1)}, f32[16,1152]{1,0:T(8,128)S(1)}, u32[]{:S(2)}, u32[]{:S(2)}) collective-permute-start(f32[16,1152]{1,0:T(8,128)S(1)} %add_add_fusion.refs_0_), channel_id=1, source_target_pairs={{0,8},{2,10},{4,12},{6,14},{8,0},{10,2},{12,4},{14,6},{16,24},{18,... | collective-permute-start | bytes 221192 | tf_op jit(solution)/shard_map/ppermute | solution.py:90
  71.9 1.5 %collective-permute-done.16.refs_3_ = f32[16,1152]{1,0:T(8,128)S(1)} collective-permute-done((f32[16,1152]{1,0:T(8,128)S(1)}, f32[16,1152]{1,0:T(8,128)S(1)}, u32[]{:S(2)}, u32[]{:S(2)}) %collective-permute-start.16) | collective-permute-done | bytes 73760 | tf_op jit(solution)/shard_map/ppermute | solution.py:90
  73.5 1.6 %collective-permute-done.15.refs_2_ = f32[16,1152]{1,0:T(8,128)S(1)} collective-permute-done((f32[16,1152]{1,0:T(8,128)S(1)}, f32[16,1152]{1,0:T(8,128)S(1)}, u32[]{:S(2)}, u32[]{:S(2)}) %collective-permute-start.15) | collective-permute-done | bytes 73760 | tf_op jit(solution)/shard_map/ppermute | solution.py:90
  75.3 2.1 %collective-permute-start.19 = (f32[16,1152]{1,0:T(8,128)S(1)}, f32[16,1152]{1,0:T(8,128)S(1)}, u32[]{:S(2)}, u32[]{:S(2)}) collective-permute-start(f32[16,1152]{1,0:T(8,128)S(1)} %shard_map.94.refs_0_), channel_id=1, source_target_pairs={{0,6},{2,4},{4,2},{6,0},{8,14},{10,12},{12,10},{14,8},{16,22},{18,... | collective-permute-start | bytes 221192 | tf_op jit(solution)/shard_map/ppermute | solution.py:90
  78.9 1.8 %collective-permute-done.19.refs_3_ = f32[16,1152]{1,0:T(8,128)S(1)} collective-permute-done((f32[16,1152]{1,0:T(8,128)S(1)}, f32[16,1152]{1,0:T(8,128)S(1)}, u32[]{:S(2)}, u32[]{:S(2)}) %collective-permute-start.19) | collective-permute-done | bytes 73760 | tf_op jit(solution)/shard_map/ppermute | solution.py:90
  80.6 1.1 %collective-permute-done.18.refs_2_ = f32[16,1152]{1,0:T(8,128)S(1)} collective-permute-done((f32[16,1152]{1,0:T(8,128)S(1)}, f32[16,1152]{1,0:T(8,128)S(1)}, u32[]{:S(2)}, u32[]{:S(2)}) %collective-permute-start.18) | collective-permute-done | bytes 73760 | tf_op jit(solution)/shard_map/ppermute | solution.py:90
  82.5 0.8 shard_map.95
  (36 shorter events, 14.8 us)
Async XLA Ops:
  3.4 1.4 %collective-permute-start = (f32[16,384]{1,0:T(8,128)S(1)}, f32[16,384]{1,0:T(8,128)S(1)}, u32[]{:S(2)}, u32[]{:S(2)}) collective-permute-start(f32[16,384]{1,0:T(8,128)S(1)} %get-tuple-element.31.refs_0_), channel_id=1, source_target_pairs={{0,1},{1,0},{2,3},{3,2},{4,5},{5,4},{6,7},{7,6},{8,9},{9,8},{10,11... | collective-permute-start | bytes 73736 | tf_op jit(solution)/shard_map/ppermute | solution.py:90
  23.3 4.7 %collective-permute-start.1 = (f32[16,1152]{1,0:T(8,128)S(1)}, f32[16,1152]{1,0:T(8,128)S(1)}, u32[]{:S(2)}, u32[]{:S(2)}) collective-permute-start(f32[16,1152]{1,0:T(8,128)S(1)} %shard_map.80), channel_id=1, source_target_pairs={{0,2},{2,0},{4,6},{6,4},{8,10},{10,8},{12,14},{14,12},{16,18},{18,... | collective-permute-start | bytes 221192 | tf_op jit(solution)/shard_map/ppermute | solution.py:90
  23.9 5.1 %collective-permute-start.2 = (f32[16,1152]{1,0:T(8,128)S(1)}, f32[16,1152]{1,0:T(8,128)S(1)}, u32[]{:S(2)}, u32[]{:S(2)}) collective-permute-start(f32[16,1152]{1,0:T(8,128)S(1)} %shard_map.81), channel_id=1, source_target_pairs={{0,4},{2,6},{4,0},{6,2},{8,12},{10,14},{12,8},{14,10},{16,20},{18,... | collective-permute-start | bytes 221192 | tf_op jit(solution)/shard_map/ppermute | solution.py:90
  24.6 5.3 %collective-permute-start.3 = (f32[16,1152]{1,0:T(8,128)S(1)}, f32[16,1152]{1,0:T(8,128)S(1)}, u32[]{:S(2)}, u32[]{:S(2)}) collective-permute-start(f32[16,1152]{1,0:T(8,128)S(1)} %shard_map.82), channel_id=1, source_target_pairs={{0,6},{2,4},{4,2},{6,0},{8,14},{10,12},{12,10},{14,8},{16,22},{18,... | collective-permute-start | bytes 221192 | tf_op jit(solution)/shard_map/ppermute | solution.py:90
  29.8 6.4 %collective-permute-start.6 = (f32[16,1152]{1,0:T(8,128)S(1)}, f32[16,1152]{1,0:T(8,128)S(1)}, u32[]{:S(2)}, u32[]{:S(2)}) collective-permute-start(f32[16,1152]{1,0:T(8,128)S(1)} %add_add_fusion.1.refs_0_), channel_id=1, source_target_pairs={{0,24},{2,26},{4,28},{6,30},{8,16},{10,18},{12,20},{14,22},{16,8},... | collective-permute-start | bytes 221192 | tf_op jit(solution)/shard_map/ppermute | solution.py:90
  30.5 7.3 %collective-permute-start.5 = (f32[16,1152]{1,0:T(8,128)S(1)}, f32[16,1152]{1,0:T(8,128)S(1)}, u32[]{:S(2)}, u32[]{:S(2)}) collective-permute-start(f32[16,1152]{1,0:T(8,128)S(1)} %add_add_fusion.1.refs_0_), channel_id=1, source_target_pairs={{0,16},{2,18},{4,20},{6,22},{8,24},{10,26},{12,28},{14,30},{16,0},... | collective-permute-start | bytes 221192 | tf_op jit(solution)/shard_map/ppermute | solution.py:90
  32.0 5.9 %collective-permute-start.4 = (f32[16,1152]{1,0:T(8,128)S(1)}, f32[16,1152]{1,0:T(8,128)S(1)}, u32[]{:S(2)}, u32[]{:S(2)}) collective-permute-start(f32[16,1152]{1,0:T(8,128)S(1)} %add_add_fusion.1.refs_0_), channel_id=1, source_target_pairs={{0,8},{2,10},{4,12},{6,14},{8,0},{10,2},{12,4},{14,6},{16,24},{18,... | collective-permute-start | bytes 221192 | tf_op jit(solution)/shard_map/ppermute | solution.py:90
  38.0 5.3 %collective-permute-start.9 = (f32[16,1152]{1,0:T(8,128)S(1)}, f32[16,1152]{1,0:T(8,128)S(1)}, u32[]{:S(2)}, u32[]{:S(2)}) collective-permute-start(f32[16,1152]{1,0:T(8,128)S(1)} %shard_map.83.chunk_ref.old_ref), channel_id=1, source_target_pairs={{0,6},{2,4},{4,2},{6,0},{8,14},{10,12},{12,10},{14,8},{16,22},{18,... | collective-permute-start | bytes 221192 | tf_op jit(solution)/shard_map/ppermute | solution.py:90
  40.1 4.4 %collective-permute-start.8 = (f32[16,1152]{1,0:T(8,128)S(1)}, f32[16,1152]{1,0:T(8,128)S(1)}, u32[]{:S(2)}, u32[]{:S(2)}) collective-permute-start(f32[16,1152]{1,0:T(8,128)S(1)} %shard_map.83.chunk_ref.old_ref), channel_id=1, source_target_pairs={{0,4},{2,6},{4,0},{6,2},{8,12},{10,14},{12,8},{14,10},{16,20},{18,... | collective-permute-start | bytes 221192 | tf_op jit(solution)/shard_map/ppermute | solution.py:90
  40.9 4.4 %collective-permute-start.7 = (f32[16,1152]{1,0:T(8,128)S(1)}, f32[16,1152]{1,0:T(8,128)S(1)}, u32[]{:S(2)}, u32[]{:S(2)}) collective-permute-start(f32[16,1152]{1,0:T(8,128)S(1)} %shard_map.83.chunk_ref.old_ref), channel_id=1, source_target_pairs={{0,2},{2,0},{4,6},{6,4},{8,10},{10,8},{12,14},{14,12},{16,18},{18,... | collective-permute-start | bytes 221192 | tf_op jit(solution)/shard_map/ppermute | solution.py:90
  45.6 1.2 %collective-permute-start.10 = (f32[16,384]{1,0:T(8,128)S(1)}, f32[16,384]{1,0:T(8,128)S(1)}, u32[]{:S(2)}, u32[]{:S(2)}) collective-permute-start(f32[16,384]{1,0:T(8,128)S(1)} %get-tuple-element.45.refs_0_), channel_id=1, source_target_pairs={{0,1},{1,0},{2,3},{3,2},{4,5},{5,4},{6,7},{7,6},{8,9},{9,8},{10,11... | collective-permute-start | bytes 73736 | tf_op jit(solution)/shard_map/ppermute | solution.py:90
  60.6 4.7 %collective-permute-start.11 = (f32[16,1152]{1,0:T(8,128)S(1)}, f32[16,1152]{1,0:T(8,128)S(1)}, u32[]{:S(2)}, u32[]{:S(2)}) collective-permute-start(f32[16,1152]{1,0:T(8,128)S(1)} %shard_map.91), channel_id=1, source_target_pairs={{0,2},{2,0},{4,6},{6,4},{8,10},{10,8},{12,14},{14,12},{16,18},{18,... | collective-permute-start | bytes 221192 | tf_op jit(solution)/shard_map/ppermute | solution.py:90
  61.2 5.1 %collective-permute-start.12 = (f32[16,1152]{1,0:T(8,128)S(1)}, f32[16,1152]{1,0:T(8,128)S(1)}, u32[]{:S(2)}, u32[]{:S(2)}) collective-permute-start(f32[16,1152]{1,0:T(8,128)S(1)} %shard_map.92), channel_id=1, source_target_pairs={{0,4},{2,6},{4,0},{6,2},{8,12},{10,14},{12,8},{14,10},{16,20},{18,... | collective-permute-start | bytes 221192 | tf_op jit(solution)/shard_map/ppermute | solution.py:90
  61.9 5.3 %collective-permute-start.13 = (f32[16,1152]{1,0:T(8,128)S(1)}, f32[16,1152]{1,0:T(8,128)S(1)}, u32[]{:S(2)}, u32[]{:S(2)}) collective-permute-start(f32[16,1152]{1,0:T(8,128)S(1)} %shard_map.93), channel_id=1, source_target_pairs={{0,6},{2,4},{4,2},{6,0},{8,14},{10,12},{12,10},{14,8},{16,22},{18,... | collective-permute-start | bytes 221192 | tf_op jit(solution)/shard_map/ppermute | solution.py:90
  67.1 6.4 %collective-permute-start.16 = (f32[16,1152]{1,0:T(8,128)S(1)}, f32[16,1152]{1,0:T(8,128)S(1)}, u32[]{:S(2)}, u32[]{:S(2)}) collective-permute-start(f32[16,1152]{1,0:T(8,128)S(1)} %add_add_fusion.refs_0_), channel_id=1, source_target_pairs={{0,24},{2,26},{4,28},{6,30},{8,16},{10,18},{12,20},{14,22},{16,8},... | collective-permute-start | bytes 221192 | tf_op jit(solution)/shard_map/ppermute | solution.py:90
  67.8 7.3 %collective-permute-start.15 = (f32[16,1152]{1,0:T(8,128)S(1)}, f32[16,1152]{1,0:T(8,128)S(1)}, u32[]{:S(2)}, u32[]{:S(2)}) collective-permute-start(f32[16,1152]{1,0:T(8,128)S(1)} %add_add_fusion.refs_0_), channel_id=1, source_target_pairs={{0,16},{2,18},{4,20},{6,22},{8,24},{10,26},{12,28},{14,30},{16,0},... | collective-permute-start | bytes 221192 | tf_op jit(solution)/shard_map/ppermute | solution.py:90
  69.3 5.9 %collective-permute-start.14 = (f32[16,1152]{1,0:T(8,128)S(1)}, f32[16,1152]{1,0:T(8,128)S(1)}, u32[]{:S(2)}, u32[]{:S(2)}) collective-permute-start(f32[16,1152]{1,0:T(8,128)S(1)} %add_add_fusion.refs_0_), channel_id=1, source_target_pairs={{0,8},{2,10},{4,12},{6,14},{8,0},{10,2},{12,4},{14,6},{16,24},{18,... | collective-permute-start | bytes 221192 | tf_op jit(solution)/shard_map/ppermute | solution.py:90
  75.3 5.3 %collective-permute-start.19 = (f32[16,1152]{1,0:T(8,128)S(1)}, f32[16,1152]{1,0:T(8,128)S(1)}, u32[]{:S(2)}, u32[]{:S(2)}) collective-permute-start(f32[16,1152]{1,0:T(8,128)S(1)} %shard_map.94.refs_0_), channel_id=1, source_target_pairs={{0,6},{2,4},{4,2},{6,0},{8,14},{10,12},{12,10},{14,8},{16,22},{18,... | collective-permute-start | bytes 221192 | tf_op jit(solution)/shard_map/ppermute | solution.py:90
  77.4 4.4 %collective-permute-start.18 = (f32[16,1152]{1,0:T(8,128)S(1)}, f32[16,1152]{1,0:T(8,128)S(1)}, u32[]{:S(2)}, u32[]{:S(2)}) collective-permute-start(f32[16,1152]{1,0:T(8,128)S(1)} %shard_map.94.refs_0_), channel_id=1, source_target_pairs={{0,4},{2,6},{4,0},{6,2},{8,12},{10,14},{12,8},{14,10},{16,20},{18,... | collective-permute-start | bytes 221192 | tf_op jit(solution)/shard_map/ppermute | solution.py:90
  78.2 4.4 %collective-permute-start.17 = (f32[16,1152]{1,0:T(8,128)S(1)}, f32[16,1152]{1,0:T(8,128)S(1)}, u32[]{:S(2)}, u32[]{:S(2)}) collective-permute-start(f32[16,1152]{1,0:T(8,128)S(1)} %shard_map.94.refs_0_), channel_id=1, source_target_pairs={{0,2},{2,0},{4,6},{6,4},{8,10},{10,8},{12,14},{14,12},{16,18},{18,... | collective-permute-start | bytes 221192 | tf_op jit(solution)/shard_map/ppermute | solution.py:90

commit v4 on v3

--- a/solution.py
+++ b/solution.py
@@ -59,6 +59,13 @@
     row = lax.broadcasted_iota(jnp.int32, shape, 0)
     col = lax.broadcasted_iota(jnp.int32, shape, 1)
     return (col == row + first).astype(F32)
+
+
+ORDER = ((0, 1, 2), (2, 1, 0), (2, 1, 0), (2, 1, 0))
+
+
+def permuted(masks, order):
+    return [masks[i] for i in order] if len(masks) == 3 else list(masks)
 
 
 class Sizes:
@@ -144,7 +151,7 @@
     return pl.multiple_of((me ^ k) * sz.chunk, BLOCK)
 
 
-def first_projection(sz, f_hbm, b_hbm, d_hbm, valid_hbm, fore_hbm, f_ref, packed_ref, own_ref, least_ref, valid_ref, *refs):
+def first_projection(sz, f_hbm, b_hbm, d_hbm, valid_hbm, fore_hbm, f_ref, packed_ref, own_ref, least_ref, bar_ref, valid_ref, *refs):
     stack_refs, (b_ref, d_ref, flags_ref, sems) = refs[: sz.group], refs[sz.group :]
     small = [
         pltpu.make_async_copy(d_hbm, d_ref, sems.at[0]),
@@ -156,23 +163,32 @@
     large = [pltpu.make_async_copy(f_hbm.at[:, s], f_ref.at[:, s], sems.at[4 + k]) for k, s in enumerate(spans)]
     for copy in small + large:
         copy.start()
-    for copy in small:
+    for copy in small[:2]:
         copy.wait()
-    valid = flags_ref[0:1, :] != 0
-    valid_ref[...] = jnp.broadcast_to(valid.astype(F32), valid_ref.shape)
-    least_ref[...] = jnp.broadcast_to(jnp.where(valid, flags_ref[8:9, :], ROW_PX), (BLOCK, sz.tile_dev)).T
     me = lax.axis_index("tiles") & (sz.group - 1)
     own_ref[:, 0 : sz.chunk] = b_ref[:, spans[0]]
     own_ref[:, sz.chunk :] = jnp.zeros((sz.rank, sz.extra), F32)
     for j in range(sz.blocks):
         own_ref[j % sz.rank, pl.ds(sz.chunk + j // sz.rank * BLOCK, BLOCK)] = d_ref[me * sz.blocks + j, :]
-    totals = None
+    bases = [b_ref[:, span] for span in spans]
+    darks = [[d_ref[pl.ds((me ^ k) * sz.blocks + j, 1), :] for j in range(sz.blocks)] for k in range(sz.group)]
     for k in range(sz.group):
-        d_rows = [d_ref[pl.ds((me ^ k) * sz.blocks + j, 1), :] for j in range(sz.blocks)]
-        b = b_ref[:, spans[k]]
-        large[k].wait()
-        totals = project_chunk(sz, f_ref[:, spans[k]], stack_refs[k], b, d_rows, totals)
-    pack_projections(sz, totals, packed_ref)
+        stack_block(sz, stack_refs[k], bases[k], darks[k])
+    parts = [ref[0 : 3 * sz.rank, :] for ref in stack_refs]
+    gram = tree([lax.dot_general(p, p, NT, preferred_element_type=F32) for p in parts])
+    dark = tree([b[:, j * BLOCK : (j + 1) * BLOCK] * d for b, rows in zip(bases, darks) for j, d in enumerate(rows)])
+    for copy in small[2:]:
+        copy.wait()
+    valid = flags_ref[0:1, :] != 0
+    valid_ref[...] = jnp.broadcast_to(valid.astype(F32), valid_ref.shape)
+    least = jnp.broadcast_to(jnp.where(valid, flags_ref[8:9, :], ROW_PX), (BLOCK, sz.tile_dev)).T
+    least_ref[...] = least
+    for block in range(bar_ref.shape[0]):
+        bar_ref[block] = jnp.where(least <= block, 1.0, jnp.inf)
+    for copy in large:
+        copy.wait()
+    proj = tree([lax.dot_general(p, f_ref[:, s], NT, preferred_element_type=F32) for p, s in zip(parts, spans)])
+    pack_projections(sz, (proj, gram, dark), packed_ref)
 
 
 def later_projection(sz, k, f_ref, chunk_ref, *refs):
@@ -245,16 +261,21 @@
     (inverse_ref[...],) = solve_spd(gram, [eye_at((r, BLOCK), 0)])
 
 
-def update_terms(sz, width, k, note_ref, f_ref, stack_ref, least_ref, three_ref, parts_ref, out_ref):
-    r = sz.rank
-    start = start_of(sz, k)
+def update_terms(sz, width, ks, note_ref, f_ref, bar_ref, three_ref, parts_ref, *refs):
+    r = sz.rank
     total = jnp.sum(note_ref[:, sz.spot : sz.spot + 1], axis=0, keepdims=True)
     spread = total / (sz.tiles_all * sz.pixels_all) + 1e-05
     scale = jnp.broadcast_to(1.0 / (4.0 * spread), (8, BLOCK))[0:1, :]
+    for k, stack_ref, out_ref in zip(ks, refs[: len(ks)], refs[len(ks) :]):
+        chunk_terms(sz, width, k, scale, f_ref, stack_ref, bar_ref, three_ref, parts_ref, out_ref)
+
+
+def chunk_terms(sz, width, k, scale, f_ref, stack_ref, bar_ref, three_ref, parts_ref, out_ref):
+    r = sz.rank
+    start = start_of(sz, k)
     parts = parts_ref[:, 0 : sz.stack]
     three = three_ref[...]
     two = three[0 : 2 * r + 16]
-    least = least_ref[...]
     each = width // BLOCK
 
     def place(flat):
@@ -267,7 +288,7 @@
         for j in range(each):
             block = (start // BLOCK + step * each + j) % (ROW_PX // BLOCK)
             x = res[:, j * BLOCK : (j + 1) * BLOCK]
-            g = jnp.where(least <= block, pl.reciprocal(x * x * scale + 1.0, approx=True), 0.0)
+            g = pl.reciprocal(x * x * scale + bar_ref[jnp.minimum(block, bar_ref.shape[0] - 1)], approx=True)
             out_ref[place(sz.blocks + step * each + j)] = jnp.sum(g, axis=0, keepdims=True)
             w = g * x
             w_hi = w.astype(BF16)
@@ -286,10 +307,10 @@
         out_ref[used % r :, sz.chunk + used // r * BLOCK :] = jnp.zeros((r - used % r, BLOCK), F32)
 
 
-def update_chunk(sz, inverse_ref, old_ref, *refs):
+def update_chunk(sz, places, inverse_ref, old_ref, *refs):
     total_refs, new_ref = refs[:-1], refs[-1]
     r = sz.rank
-    totals = tree([ref[...] for ref in total_refs])
+    totals = tree([total_refs[i][...] for i in places])
     inverse = inverse_ref[:, 0:r]
     change = jnp.dot(inverse, totals[:, 0 : sz.chunk] / sz.tiles_all, precision=lax.Precision.HIGHEST, preferred_element_type=F32)
     new_ref[:, 0 : sz.chunk] = old_ref[:, 0 : sz.chunk] + change
@@ -308,11 +329,11 @@
         )
 
 
-def assemble(sz, coef_ref, *refs):
+def assemble(sz, ks, coef_ref, *refs):
     chunks, (b_ref, d_ref, coef_out_ref) = refs[: sz.group], refs[sz.group :]
     coef_out_ref[...] = coef_ref[...]
     me = lax.axis_index("tiles") & (sz.group - 1)
-    for k, ref in enumerate(chunks):
+    for k, ref in zip(ks, chunks):
         c = me ^ k
         b_ref[:, pl.ds(pl.multiple_of(c * sz.chunk, BLOCK), sz.chunk)] = ref[:, 0 : sz.chunk]
         for j in range(sz.blocks):
@@ -345,9 +366,9 @@
     masks = sz.tile_levels[0]
     for iteration in range(ITERS):
         if iteration == 0:
-            frames, packed, old, least, valid, *stacks = call(
+            frames, packed, old, least, bar, valid, *stacks = call(
                 functools.partial(first_projection, sz),
-                [((td, pd), BF16), packed_out, (chunk_shape, F32), ((td, BLOCK), jnp.int32), ((8, td), F32)]
+                [((td, pd), BF16), packed_out, (chunk_shape, F32), ((td, BLOCK), jnp.int32), ((ROW_PX // BLOCK // 2 + 1, td, BLOCK), F32), ((8, td), F32)]
                 + [stack_out] * sz.group,
                 [frames, basis_start, dark_start.reshape(pd // BLOCK, BLOCK), tile_valid.reshape(1, td), foreground_blocks.reshape(1, td)],
                 in_hbm=True,
@@ -360,7 +381,7 @@
             )
         else:
             before, stacks = [], [None] * sz.group
-            for k in [0] + list(masks)[::-1]:
+            for k in [0] + permuted(masks, ORDER[2]):
                 packed, stacks[k] = call(
                     functools.partial(later_projection, sz, k), [packed_out, stack_out], [frames, chunks[k]] + before
                 )
@@ -374,23 +395,30 @@
         notes = lax.all_to_all(note, everyone, 0, 0, tiled=True)
         (inverse,) = call(functools.partial(invert_gram, sz), [((r, BLOCK), F32)], [notes])
         terms = {}
-        for k in list(masks) + [0]:
-            (terms[k],) = call(
-                functools.partial(update_terms, sz, width, k),
-                [(chunk_shape, F32)],
-                [notes, frames, stacks[k], least, three, parts],
+        for ks in (list(masks), [0]):
+            outs = call(
+                functools.partial(update_terms, sz, width, ks),
+                [(chunk_shape, F32)] * len(ks),
+                [notes, frames, bar, three, parts] + [stacks[k] for k in ks],
             )
-        total = tree([terms[0]] + [partner(terms[m], "tiles", m) for m in masks])
+            terms.update(zip(ks, outs))
+        order = permuted(masks, ORDER[0])
+        got = dict(zip(order, lax.optimization_barrier([partner(terms[m], "tiles", m) for m in order])))
+        total = tree([terms[0]] + [got[m] for m in masks])
         later = sz.tile_levels[1:]
         for level in later[:-1]:
             total = sum_level(total, "tiles", level)
-        totals = [total] + [partner(total, "tiles", m) for m in (later[-1] if later else ())]
-        (old,) = call(functools.partial(update_chunk, sz), [(chunk_shape, F32)], [inverse, old] + totals)
+        last = later[-1] if later else ()
+        order = permuted(last, ORDER[1])
+        totals = [total] + [partner(total, "tiles", m) for m in order]
+        places = [0] + [1 + order.index(m) for m in last]
+        (old,) = call(functools.partial(update_chunk, sz, places), [(chunk_shape, F32)], [inverse, old] + totals)
         chunks = [old] + [partner(old, "tiles", m) for m in masks]
+    ks = [0] + permuted(masks, ORDER[3])
     basis, dark, coef = call(
-        functools.partial(assemble, sz),
+        functools.partial(assemble, sz, ks),
         [((r, pd), F32), ((pd // BLOCK, BLOCK), F32), ((r, td), F32)],
-        [coef] + chunks,
+        [coef] + [chunks[k] for k in ks],
     )
     return basis, dark.reshape(pd), coef.T
 

time: 83.5 us -> 82.1 us (0.983)
  Pallas kernels: 15.6 us -> 14.1 us
    pallas_call x20 -> x16, Pallas kernels: 15.6 us -> 14.1 us  [call(): pl.pallas_call(body, out_shape=[jax.ShapeDtypeStruct(s, t) for s, t in ou...]
where the time goes in v4:
time: 82.1 us; the launch traced here: 81.8 us
  blocking collectives  24.2 us (29%)
  starting transfers between devices  23.6 us (29%)
  waiting for transfers between devices  19.2 us (23%)
  Pallas kernels  14.1 us (17%)
    all_to_all x2, blocking collectives, local(): notes = lax.all_to_all(note, everyone, 0, 0, tiled=True)  24.2 us
    ppermute x20, starting transfers between devices, partner(): return lax.ppermute(x, axis, [(i, i ^ mask) for i in range(n)])  23.6 us
    ppermute x20, waiting for transfers between devices, partner(): return lax.ppermute(x, axis, [(i, i ^ mask) for i in range(n)])  19.2 us
    pallas_call x16, Pallas kernels, call(): pl.pallas_call(body, out_shape=[jax.ShapeDtypeStruct(s, t) for s, t in ou...  14.1 us
  transfers between devices with their start and end apart: 20, of which 18 were waited for; matrix products, arithmetic and copies ran while one was open for 0% of the time, Pallas kernels for 4%

profile of v4, /device:TPU:0, one launch (start us, length us, event | category | flops | bytes accessed | tf_op | source)
XLA Modules:
  0.0 81.8 jit_solution(11448600511353130460)
XLA Ops:
  0.6 2.6 %shard_map.76 = (bf16[256,4096]{1,0:T(8,128)(2,1)S(1)}, f32[16,384]{1,0:T(8,128)S(1)}, f32[16,1152]{1,0:T(8,128)S(1)}, s32[256,128]{1,0:T(8,128)S(1)}, f32[9,256...) custom-call(bf16[256,4096]{1,0:T(8,128)(2,1)} %f_hbm.1, ...), custom_call_target="tpu_custom_call" | custom-call | tf_op jit(solution)/shard_map/pallas_call | solution.py:345
  3.7 0.8 %collective-permute-done.refs_1_ = f32[16,384]{1,0:T(8,128)S(1)} collective-permute-done((f32[16,384]{1,0:T(8,128)S(1)}, f32[16,384]{1,0:T(8,128)S(1)}, u32[]{:S(2)}, u32[]{:S(2)}) %collective-permute-start) | collective-permute-done | bytes 24608 | tf_op jit(solution)/shard_map/ppermute | solution.py:97
  4.6 2.0 %shard_map.77 = (f32[16,256]{1,0:T(8,128)}, bf16[64,256]{1,0:T(8,128)(2,1)S(1)}, bf16[256,128]{1,0:T(8,128)(2,1)S(1)}, f32[32,256]{1,0:T(8,128)S(1)}) custom-call(f32[16,384]{1,0:T(8,128)S(1)} %get-tuple-element.44.refs_0_, f32[16,384]{1,0:T(8,128)S(1)} %collective-permute-done.refs_1_, bf16[112,1024]{1,0:T(8,128)(2,1)S(1)} %get-tuple-element.45.refs_2_.refs_0_, ...), custom_call_target="tpu_custom_call" | custom-call | tf_op jit(solution)/shard_map/pallas_call | solution.py:345
  6.6 14.3 %all_to_all.22 = f32[32,1,256]{2,1,0:T(1,128)S(1)} all-to-all(f32[32,1,256]{2,1,0:T(1,128)S(1)} %copy.8), channel_id=1, replica_groups=mesh['tiles'=16,'pix'=2] {'tiles','pix'}, dimensions={0} | all-to-all | bytes 65536 | tf_op jit(solution)/shard_map/all_to_all | solution.py:395
  20.9 1.6 %shard_map.80 = (f32[16,1152]{1,0:T(8,128)S(1)}, f32[16,1152]{1,0:T(8,128)S(1)}, f32[16,1152]{1,0:T(8,128)S(1)}) custom-call(f32[32,256]{1,0:T(8,128)S(1)} %bitcast.16, bf16[256,4096]{1,0:T(8,128)(2,1)S(1)} %get-tuple-element.43.refs_6_.f_ref, f32[9,256,128]{2,1,0:T(8,128)S(1)} %get-tuple-element.53.bar_ref, ...), custom_call_target="tpu_custom_call" | custom-call | tf_op jit(solution)/shard_map/pallas_call | solution.py:345
  23.8 2.3 %collective-permute-start.3 = (f32[16,1152]{1,0:T(8,128)S(1)}, f32[16,1152]{1,0:T(8,128)S(1)}, u32[]{:S(2)}, u32[]{:S(2)}) collective-permute-start(f32[16,1152]{1,0:T(8,128)S(1)} %get-tuple-element.58), channel_id=1, source_target_pairs={{0,6},{2,4},{4,2},{6,0},{8,14},{10,12},{12,10},{14,8},{16,22},{18,... | collective-permute-start | bytes 221192 | tf_op jit(solution)/shard_map/ppermute | solution.py:97
  27.2 1.0 %collective-permute-done.2 = f32[16,1152]{1,0:T(8,128)S(1)} collective-permute-done((f32[16,1152]{1,0:T(8,128)S(1)}, f32[16,1152]{1,0:T(8,128)S(1)}, u32[]{:S(2)}, u32[]{:S(2)}) %collective-permute-start.2) | collective-permute-done | bytes 73760 | tf_op jit(solution)/shard_map/ppermute | solution.py:97
  28.2 0.8 collective-permute-done.3
  29.7 1.5 %collective-permute-start.5 = (f32[16,1152]{1,0:T(8,128)S(1)}, f32[16,1152]{1,0:T(8,128)S(1)}, u32[]{:S(2)}, u32[]{:S(2)}) collective-permute-start(f32[16,1152]{1,0:T(8,128)S(1)} %add_add_fusion.1.refs_0_), channel_id=1, source_target_pairs={{0,16},{2,18},{4,20},{6,22},{8,24},{10,26},{12,28},{14,30},{16,0},... | collective-permute-start | bytes 221192 | tf_op jit(solution)/shard_map/ppermute | solution.py:97
  31.2 2.3 %collective-permute-start.6 = (f32[16,1152]{1,0:T(8,128)S(1)}, f32[16,1152]{1,0:T(8,128)S(1)}, u32[]{:S(2)}, u32[]{:S(2)}) collective-permute-start(f32[16,1152]{1,0:T(8,128)S(1)} %add_add_fusion.1.refs_0_), channel_id=1, source_target_pairs={{0,8},{2,10},{4,12},{6,14},{8,0},{10,2},{12,4},{14,6},{16,24},{18,... | collective-permute-start | bytes 221192 | tf_op jit(solution)/shard_map/ppermute | solution.py:97
  33.8 1.6 %collective-permute-done.4.refs_1_ = f32[16,1152]{1,0:T(8,128)S(1)} collective-permute-done((f32[16,1152]{1,0:T(8,128)S(1)}, f32[16,1152]{1,0:T(8,128)S(1)}, u32[]{:S(2)}, u32[]{:S(2)}) %collective-permute-start.4) | collective-permute-done | bytes 73760 | tf_op jit(solution)/shard_map/ppermute | solution.py:97
  35.4 1.6 %collective-permute-done.5.refs_2_ = f32[16,1152]{1,0:T(8,128)S(1)} collective-permute-done((f32[16,1152]{1,0:T(8,128)S(1)}, f32[16,1152]{1,0:T(8,128)S(1)}, u32[]{:S(2)}, u32[]{:S(2)}) %collective-permute-start.5) | collective-permute-done | bytes 73760 | tf_op jit(solution)/shard_map/ppermute | solution.py:97
  37.2 2.1 %collective-permute-start.9 = (f32[16,1152]{1,0:T(8,128)S(1)}, f32[16,1152]{1,0:T(8,128)S(1)}, u32[]{:S(2)}, u32[]{:S(2)}) collective-permute-start(f32[16,1152]{1,0:T(8,128)S(1)} %shard_map.81.chunk_ref.old_ref), channel_id=1, source_target_pairs={{0,6},{2,4},{4,2},{6,0},{8,14},{10,12},{12,10},{14,8},{16,22},{18,... | collective-permute-start | bytes 221192 | tf_op jit(solution)/shard_map/ppermute | solution.py:97
  39.3 0.7 collective-permute-start.8
  41.1 1.4 %collective-permute-done.9.chunk_ref = f32[16,1152]{1,0:T(8,128)S(1)} collective-permute-done((f32[16,1152]{1,0:T(8,128)S(1)}, f32[16,1152]{1,0:T(8,128)S(1)}, u32[]{:S(2)}, u32[]{:S(2)}) %collective-permute-start.9) | collective-permute-done | bytes 73760 | tf_op jit(solution)/shard_map/ppermute | solution.py:97
  42.9 0.8 collective-permute-done.8.chunk_ref
  44.8 1.2 %collective-permute-done.10.refs_1_ = f32[16,384]{1,0:T(8,128)S(1)} collective-permute-done((f32[16,384]{1,0:T(8,128)S(1)}, f32[16,384]{1,0:T(8,128)S(1)}, u32[]{:S(2)}, u32[]{:S(2)}) %collective-permute-start.10) | collective-permute-done | bytes 24608 | tf_op jit(solution)/shard_map/ppermute | solution.py:97
  46.0 1.5 %shard_map.86 = (f32[16,256]{1,0:T(8,128)S(1)}, bf16[64,256]{1,0:T(8,128)(2,1)S(1)}, bf16[256,128]{1,0:T(8,128)(2,1)S(1)}, f32[32,256]{1,0:T(8,128)S(1)}) custom-call(f32[16,384]{1,0:T(8,128)S(1)} %get-tuple-element.65.refs_0_, f32[16,384]{1,0:T(8,128)S(1)} %collective-permute-done.10.refs_1_, bf16[112,1024]{1,0:T(8,128)(2,1)S(1)} %get-tuple-element.66.refs_2_.refs_0_, ...), custom_call_target="tpu_custom_call" | custom-call | tf_op jit(solution)/shard_map/pallas_call | solution.py:345
  47.6 10.0 %all_to_all.23 = f32[32,1,256]{2,1,0:T(1,128)S(1)} all-to-all(f32[32,1,256]{2,1,0:T(1,128)S(1)} %copy.9), channel_id=1, replica_groups=mesh['tiles'=16,'pix'=2] {'tiles','pix'}, dimensions={0} | all-to-all | bytes 65536 | tf_op jit(solution)/shard_map/all_to_all | solution.py:395
  57.5 1.7 %shard_map.89 = (f32[16,1152]{1,0:T(8,128)S(1)}, f32[16,1152]{1,0:T(8,128)S(1)}, f32[16,1152]{1,0:T(8,128)S(1)}) custom-call(f32[32,256]{1,0:T(8,128)S(1)} %bitcast.13, bf16[256,4096]{1,0:T(8,128)(2,1)S(1)} %get-tuple-element.43.refs_6_.f_ref, f32[9,256,128]{2,1,0:T(8,128)S(1)} %get-tuple-element.53.bar_ref, ...), custom_call_target="tpu_custom_call" | custom-call | tf_op jit(solution)/shard_map/pallas_call | solution.py:345
  60.4 2.3 %collective-permute-start.13 = (f32[16,1152]{1,0:T(8,128)S(1)}, f32[16,1152]{1,0:T(8,128)S(1)}, u32[]{:S(2)}, u32[]{:S(2)}) collective-permute-start(f32[16,1152]{1,0:T(8,128)S(1)} %get-tuple-element.76), channel_id=1, source_target_pairs={{0,6},{2,4},{4,2},{6,0},{8,14},{10,12},{12,10},{14,8},{16,22},{18,... | collective-permute-start | bytes 221192 | tf_op jit(solution)/shard_map/ppermute | solution.py:97
  63.9 1.0 %collective-permute-done.12 = f32[16,1152]{1,0:T(8,128)S(1)} collective-permute-done((f32[16,1152]{1,0:T(8,128)S(1)}, f32[16,1152]{1,0:T(8,128)S(1)}, u32[]{:S(2)}, u32[]{:S(2)}) %collective-permute-start.12) | collective-permute-done | bytes 73760 | tf_op jit(solution)/shard_map/ppermute | solution.py:97
  64.9 0.8 collective-permute-done.13
  66.4 1.5 %collective-permute-start.15 = (f32[16,1152]{1,0:T(8,128)S(1)}, f32[16,1152]{1,0:T(8,128)S(1)}, u32[]{:S(2)}, u32[]{:S(2)}) collective-permute-start(f32[16,1152]{1,0:T(8,128)S(1)} %add_add_fusion.refs_0_), channel_id=1, source_target_pairs={{0,16},{2,18},{4,20},{6,22},{8,24},{10,26},{12,28},{14,30},{16,0},... | collective-permute-start | bytes 221192 | tf_op jit(solution)/shard_map/ppermute | solution.py:97
  67.8 2.3 %collective-permute-start.16 = (f32[16,1152]{1,0:T(8,128)S(1)}, f32[16,1152]{1,0:T(8,128)S(1)}, u32[]{:S(2)}, u32[]{:S(2)}) collective-permute-start(f32[16,1152]{1,0:T(8,128)S(1)} %add_add_fusion.refs_0_), channel_id=1, source_target_pairs={{0,8},{2,10},{4,12},{6,14},{8,0},{10,2},{12,4},{14,6},{16,24},{18,... | collective-permute-start | bytes 221192 | tf_op jit(solution)/shard_map/ppermute | solution.py:97
  70.5 1.5 %collective-permute-done.14.refs_1_ = f32[16,1152]{1,0:T(8,128)S(1)} collective-permute-done((f32[16,1152]{1,0:T(8,128)S(1)}, f32[16,1152]{1,0:T(8,128)S(1)}, u32[]{:S(2)}, u32[]{:S(2)}) %collective-permute-start.14) | collective-permute-done | bytes 73760 | tf_op jit(solution)/shard_map/ppermute | solution.py:97
  72.1 1.6 %collective-permute-done.15.refs_2_ = f32[16,1152]{1,0:T(8,128)S(1)} collective-permute-done((f32[16,1152]{1,0:T(8,128)S(1)}, f32[16,1152]{1,0:T(8,128)S(1)}, u32[]{:S(2)}, u32[]{:S(2)}) %collective-permute-start.15) | collective-permute-done | bytes 73760 | tf_op jit(solution)/shard_map/ppermute | solution.py:97
  73.9 2.1 %collective-permute-start.17 = (f32[16,1152]{1,0:T(8,128)S(1)}, f32[16,1152]{1,0:T(8,128)S(1)}, u32[]{:S(2)}, u32[]{:S(2)}) collective-permute-start(f32[16,1152]{1,0:T(8,128)S(1)} %shard_map.90.refs_0_), channel_id=1, source_target_pairs={{0,6},{2,4},{4,2},{6,0},{8,14},{10,12},{12,10},{14,8},{16,22},{18,... | collective-permute-start | bytes 221192 | tf_op jit(solution)/shard_map/ppermute | solution.py:97
  76.0 0.7 collective-permute-start.18
  77.4 1.8 %collective-permute-done.17.refs_1_ = f32[16,1152]{1,0:T(8,128)S(1)} collective-permute-done((f32[16,1152]{1,0:T(8,128)S(1)}, f32[16,1152]{1,0:T(8,128)S(1)}, u32[]{:S(2)}, u32[]{:S(2)}) %collective-permute-start.17) | collective-permute-done | bytes 73760 | tf_op jit(solution)/shard_map/ppermute | solution.py:97
  79.2 1.1 %collective-permute-done.18.refs_2_ = f32[16,1152]{1,0:T(8,128)S(1)} collective-permute-done((f32[16,1152]{1,0:T(8,128)S(1)}, f32[16,1152]{1,0:T(8,128)S(1)}, u32[]{:S(2)}, u32[]{:S(2)}) %collective-permute-start.18) | collective-permute-done | bytes 73760 | tf_op jit(solution)/shard_map/ppermute | solution.py:97
  81.1 0.8 shard_map.91
  (32 shorter events, 11.8 us)
Async XLA Ops:
  3.2 1.4 %collective-permute-start = (f32[16,384]{1,0:T(8,128)S(1)}, f32[16,384]{1,0:T(8,128)S(1)}, u32[]{:S(2)}, u32[]{:S(2)}) collective-permute-start(f32[16,384]{1,0:T(8,128)S(1)} %get-tuple-element.44.refs_0_), channel_id=1, source_target_pairs={{0,1},{1,0},{2,3},{3,2},{4,5},{5,4},{6,7},{7,6},{8,9},{9,8},{10,11... | collective-permute-start | bytes 73736 | tf_op jit(solution)/shard_map/ppermute | solution.py:97
  22.5 4.7 %collective-permute-start.1 = (f32[16,1152]{1,0:T(8,128)S(1)}, f32[16,1152]{1,0:T(8,128)S(1)}, u32[]{:S(2)}, u32[]{:S(2)}) collective-permute-start(f32[16,1152]{1,0:T(8,128)S(1)} %get-tuple-element.56), channel_id=1, source_target_pairs={{0,2},{2,0},{4,6},{6,4},{8,10},{10,8},{12,14},{14,12},{16,18},{18,... | collective-permute-start | bytes 221192 | tf_op jit(solution)/shard_map/ppermute | solution.py:97
  23.1 5.1 %collective-permute-start.2 = (f32[16,1152]{1,0:T(8,128)S(1)}, f32[16,1152]{1,0:T(8,128)S(1)}, u32[]{:S(2)}, u32[]{:S(2)}) collective-permute-start(f32[16,1152]{1,0:T(8,128)S(1)} %get-tuple-element.57), channel_id=1, source_target_pairs={{0,4},{2,6},{4,0},{6,2},{8,12},{10,14},{12,8},{14,10},{16,20},{18,... | collective-permute-start | bytes 221192 | tf_op jit(solution)/shard_map/ppermute | solution.py:97
  23.8 5.3 %collective-permute-start.3 = (f32[16,1152]{1,0:T(8,128)S(1)}, f32[16,1152]{1,0:T(8,128)S(1)}, u32[]{:S(2)}, u32[]{:S(2)}) collective-permute-start(f32[16,1152]{1,0:T(8,128)S(1)} %get-tuple-element.58), channel_id=1, source_target_pairs={{0,6},{2,4},{4,2},{6,0},{8,14},{10,12},{12,10},{14,8},{16,22},{18,... | collective-permute-start | bytes 221192 | tf_op jit(solution)/shard_map/ppermute | solution.py:97
  29.0 6.4 %collective-permute-start.4 = (f32[16,1152]{1,0:T(8,128)S(1)}, f32[16,1152]{1,0:T(8,128)S(1)}, u32[]{:S(2)}, u32[]{:S(2)}) collective-permute-start(f32[16,1152]{1,0:T(8,128)S(1)} %add_add_fusion.1.refs_0_), channel_id=1, source_target_pairs={{0,24},{2,26},{4,28},{6,30},{8,16},{10,18},{12,20},{14,22},{16,8},... | collective-permute-start | bytes 221192 | tf_op jit(solution)/shard_map/ppermute | solution.py:97
  29.7 7.3 %collective-permute-start.5 = (f32[16,1152]{1,0:T(8,128)S(1)}, f32[16,1152]{1,0:T(8,128)S(1)}, u32[]{:S(2)}, u32[]{:S(2)}) collective-permute-start(f32[16,1152]{1,0:T(8,128)S(1)} %add_add_fusion.1.refs_0_), channel_id=1, source_target_pairs={{0,16},{2,18},{4,20},{6,22},{8,24},{10,26},{12,28},{14,30},{16,0},... | collective-permute-start | bytes 221192 | tf_op jit(solution)/shard_map/ppermute | solution.py:97
  31.2 5.9 %collective-permute-start.6 = (f32[16,1152]{1,0:T(8,128)S(1)}, f32[16,1152]{1,0:T(8,128)S(1)}, u32[]{:S(2)}, u32[]{:S(2)}) collective-permute-start(f32[16,1152]{1,0:T(8,128)S(1)} %add_add_fusion.1.refs_0_), channel_id=1, source_target_pairs={{0,8},{2,10},{4,12},{6,14},{8,0},{10,2},{12,4},{14,6},{16,24},{18,... | collective-permute-start | bytes 221192 | tf_op jit(solution)/shard_map/ppermute | solution.py:97
  37.2 5.3 %collective-permute-start.9 = (f32[16,1152]{1,0:T(8,128)S(1)}, f32[16,1152]{1,0:T(8,128)S(1)}, u32[]{:S(2)}, u32[]{:S(2)}) collective-permute-start(f32[16,1152]{1,0:T(8,128)S(1)} %shard_map.81.chunk_ref.old_ref), channel_id=1, source_target_pairs={{0,6},{2,4},{4,2},{6,0},{8,14},{10,12},{12,10},{14,8},{16,22},{18,... | collective-permute-start | bytes 221192 | tf_op jit(solution)/shard_map/ppermute | solution.py:97
  39.3 4.4 %collective-permute-start.8 = (f32[16,1152]{1,0:T(8,128)S(1)}, f32[16,1152]{1,0:T(8,128)S(1)}, u32[]{:S(2)}, u32[]{:S(2)}) collective-permute-start(f32[16,1152]{1,0:T(8,128)S(1)} %shard_map.81.chunk_ref.old_ref), channel_id=1, source_target_pairs={{0,4},{2,6},{4,0},{6,2},{8,12},{10,14},{12,8},{14,10},{16,20},{18,... | collective-permute-start | bytes 221192 | tf_op jit(solution)/shard_map/ppermute | solution.py:97
  40.1 4.4 %collective-permute-start.7 = (f32[16,1152]{1,0:T(8,128)S(1)}, f32[16,1152]{1,0:T(8,128)S(1)}, u32[]{:S(2)}, u32[]{:S(2)}) collective-permute-start(f32[16,1152]{1,0:T(8,128)S(1)} %shard_map.81.chunk_ref.old_ref), channel_id=1, source_target_pairs={{0,2},{2,0},{4,6},{6,4},{8,10},{10,8},{12,14},{14,12},{16,18},{18,... | collective-permute-start | bytes 221192 | tf_op jit(solution)/shard_map/ppermute | solution.py:97
  44.8 1.2 %collective-permute-start.10 = (f32[16,384]{1,0:T(8,128)S(1)}, f32[16,384]{1,0:T(8,128)S(1)}, u32[]{:S(2)}, u32[]{:S(2)}) collective-permute-start(f32[16,384]{1,0:T(8,128)S(1)} %get-tuple-element.65.refs_0_), channel_id=1, source_target_pairs={{0,1},{1,0},{2,3},{3,2},{4,5},{5,4},{6,7},{7,6},{8,9},{9,8},{10,11... | collective-permute-start | bytes 73736 | tf_op jit(solution)/shard_map/ppermute | solution.py:97
  59.2 4.7 %collective-permute-start.11 = (f32[16,1152]{1,0:T(8,128)S(1)}, f32[16,1152]{1,0:T(8,128)S(1)}, u32[]{:S(2)}, u32[]{:S(2)}) collective-permute-start(f32[16,1152]{1,0:T(8,128)S(1)} %get-tuple-element.74), channel_id=1, source_target_pairs={{0,2},{2,0},{4,6},{6,4},{8,10},{10,8},{12,14},{14,12},{16,18},{18,... | collective-permute-start | bytes 221192 | tf_op jit(solution)/shard_map/ppermute | solution.py:97
  59.7 5.1 %collective-permute-start.12 = (f32[16,1152]{1,0:T(8,128)S(1)}, f32[16,1152]{1,0:T(8,128)S(1)}, u32[]{:S(2)}, u32[]{:S(2)}) collective-permute-start(f32[16,1152]{1,0:T(8,128)S(1)} %get-tuple-element.75), channel_id=1, source_target_pairs={{0,4},{2,6},{4,0},{6,2},{8,12},{10,14},{12,8},{14,10},{16,20},{18,... | collective-permute-start | bytes 221192 | tf_op jit(solution)/shard_map/ppermute | solution.py:97
  60.4 5.3 %collective-permute-start.13 = (f32[16,1152]{1,0:T(8,128)S(1)}, f32[16,1152]{1,0:T(8,128)S(1)}, u32[]{:S(2)}, u32[]{:S(2)}) collective-permute-start(f32[16,1152]{1,0:T(8,128)S(1)} %get-tuple-element.76), channel_id=1, source_target_pairs={{0,6},{2,4},{4,2},{6,0},{8,14},{10,12},{12,10},{14,8},{16,22},{18,... | collective-permute-start | bytes 221192 | tf_op jit(solution)/shard_map/ppermute | solution.py:97
  65.7 6.4 %collective-permute-start.14 = (f32[16,1152]{1,0:T(8,128)S(1)}, f32[16,1152]{1,0:T(8,128)S(1)}, u32[]{:S(2)}, u32[]{:S(2)}) collective-permute-start(f32[16,1152]{1,0:T(8,128)S(1)} %add_add_fusion.refs_0_), channel_id=1, source_target_pairs={{0,24},{2,26},{4,28},{6,30},{8,16},{10,18},{12,20},{14,22},{16,8},... | collective-permute-start | bytes 221192 | tf_op jit(solution)/shard_map/ppermute | solution.py:97
  66.4 7.3 %collective-permute-start.15 = (f32[16,1152]{1,0:T(8,128)S(1)}, f32[16,1152]{1,0:T(8,128)S(1)}, u32[]{:S(2)}, u32[]{:S(2)}) collective-permute-start(f32[16,1152]{1,0:T(8,128)S(1)} %add_add_fusion.refs_0_), channel_id=1, source_target_pairs={{0,16},{2,18},{4,20},{6,22},{8,24},{10,26},{12,28},{14,30},{16,0},... | collective-permute-start | bytes 221192 | tf_op jit(solution)/shard_map/ppermute | solution.py:97
  67.8 5.9 %collective-permute-start.16 = (f32[16,1152]{1,0:T(8,128)S(1)}, f32[16,1152]{1,0:T(8,128)S(1)}, u32[]{:S(2)}, u32[]{:S(2)}) collective-permute-start(f32[16,1152]{1,0:T(8,128)S(1)} %add_add_fusion.refs_0_), channel_id=1, source_target_pairs={{0,8},{2,10},{4,12},{6,14},{8,0},{10,2},{12,4},{14,6},{16,24},{18,... | collective-permute-start | bytes 221192 | tf_op jit(solution)/shard_map/ppermute | solution.py:97
  73.9 5.3 %collective-permute-start.17 = (f32[16,1152]{1,0:T(8,128)S(1)}, f32[16,1152]{1,0:T(8,128)S(1)}, u32[]{:S(2)}, u32[]{:S(2)}) collective-permute-start(f32[16,1152]{1,0:T(8,128)S(1)} %shard_map.90.refs_0_), channel_id=1, source_target_pairs={{0,6},{2,4},{4,2},{6,0},{8,14},{10,12},{12,10},{14,8},{16,22},{18,... | collective-permute-start | bytes 221192 | tf_op jit(solution)/shard_map/ppermute | solution.py:97
  76.0 4.4 %collective-permute-start.18 = (f32[16,1152]{1,0:T(8,128)S(1)}, f32[16,1152]{1,0:T(8,128)S(1)}, u32[]{:S(2)}, u32[]{:S(2)}) collective-permute-start(f32[16,1152]{1,0:T(8,128)S(1)} %shard_map.90.refs_0_), channel_id=1, source_target_pairs={{0,4},{2,6},{4,0},{6,2},{8,12},{10,14},{12,8},{14,10},{16,20},{18,... | collective-permute-start | bytes 221192 | tf_op jit(solution)/shard_map/ppermute | solution.py:97
  76.7 4.4 %collective-permute-start.19 = (f32[16,1152]{1,0:T(8,128)S(1)}, f32[16,1152]{1,0:T(8,128)S(1)}, u32[]{:S(2)}, u32[]{:S(2)}) collective-permute-start(f32[16,1152]{1,0:T(8,128)S(1)} %shard_map.90.refs_0_), channel_id=1, source_target_pairs={{0,2},{2,0},{4,6},{6,4},{8,10},{10,8},{12,14},{14,12},{16,18},{18,... | collective-permute-start | bytes 221192 | tf_op jit(solution)/shard_map/ppermute | solution.py:97

commit v5 on v4

--- a/solution.py
+++ b/solution.py
@@ -61,7 +61,7 @@
     return (col == row + first).astype(F32)
 
 
-ORDER = ((0, 1, 2), (2, 1, 0), (2, 1, 0), (2, 1, 0))
+ORDER = ((0, 1, 2), (2, 0, 1), (2, 1, 0), (2, 1, 0))
 
 
 def permuted(masks, order):
@@ -95,6 +95,15 @@
 def partner(x, axis, mask):
     n = lax.axis_size(axis)
     return lax.ppermute(x, axis, [(i, i ^ mask) for i in range(n)])
+
+
+def crossed(x, mask, swap):
+    n, cores = lax.axis_size("tiles"), lax.axis_size("pix")
+    pairs = []
+    for i in range(n):
+        for p in range(cores):
+            pairs.append((i * cores + p, (i ^ (swap.get(mask, mask) if p & 1 else mask)) * cores + p))
+    return lax.ppermute(x, ("tiles", "pix"), pairs)
 
 
 def tree(parts):
@@ -410,7 +419,8 @@
             total = sum_level(total, "tiles", level)
         last = later[-1] if later else ()
         order = permuted(last, ORDER[1])
-        totals = [total] + [partner(total, "tiles", m) for m in order]
+        swap = {last[0]: last[1], last[1]: last[0]} if len(last) == 3 else {}
+        totals = [total] + [crossed(total, m, swap) for m in order]
         places = [0] + [1 + order.index(m) for m in last]
         (old,) = call(functools.partial(update_chunk, sz, places), [(chunk_shape, F32)], [inverse, old] + totals)
         chunks = [old] + [partner(old, "tiles", m) for m in masks]

time: 82.1 us -> 81.4 us (level)
  waiting for transfers between devices: 19.2 us -> 17.7 us
  blocking collectives: 24.2 us -> 25.1 us
    ppermute x0 -> x6, starting transfers between devices: none -> 8.91 us  [crossed(): return lax.ppermute(x, ('tiles', 'pix'), pairs)]
    ppermute x20 -> x14, starting transfers between devices: 23.6 us -> 14.6 us  [partner(): return lax.ppermute(x, axis, [(i, i ^ mask) for i in range(n)])]
    ppermute x20 -> x14, waiting for transfers between devices: 19.2 us -> 11.3 us  [partner(): return lax.ppermute(x, axis, [(i, i ^ mask) for i in range(n)])]
    ppermute x0 -> x6, waiting for transfers between devices: none -> 6.36 us  [crossed(): return lax.ppermute(x, ('tiles', 'pix'), pairs)]
    all_to_all x2, blocking collectives: 24.2 us -> 25.1 us  [local(): notes = lax.all_to_all(note, everyone, 0, 0, tiled=True)]
  transfers between devices with their start and end apart: 20 -> 20, of which waited for: 18 -> 17; matrix products, arithmetic and copies ran while one was open for 0% -> 0% of each run, Pallas kernels for 4% -> 4%
where the time goes in v5:
time: 81.4 us; the launch traced here: 81.2 us
  blocking collectives  25.1 us (31%)
  starting transfers between devices  23.6 us (29%)
  waiting for transfers between devices  17.7 us (22%)
  Pallas kernels  14.1 us (17%)
    all_to_all x2, blocking collectives, local(): notes = lax.all_to_all(note, everyone, 0, 0, tiled=True)  25.1 us
    ppermute x14, starting transfers between devices, partner(): return lax.ppermute(x, axis, [(i, i ^ mask) for i in range(n)])  14.6 us
    pallas_call x16, Pallas kernels, call(): pl.pallas_call(body, out_shape=[jax.ShapeDtypeStruct(s, t) for s, t in ou...  14.1 us
    ppermute x14, waiting for transfers between devices, partner(): return lax.ppermute(x, axis, [(i, i ^ mask) for i in range(n)])  11.3 us
    ppermute x6, starting transfers between devices, crossed(): return lax.ppermute(x, ('tiles', 'pix'), pairs)  8.91 us
    ppermute x6, waiting for transfers between devices, crossed(): return lax.ppermute(x, ('tiles', 'pix'), pairs)  6.36 us
  transfers between devices with their start and end apart: 20, of which 17 were waited for; matrix products, arithmetic and copies ran while one was open for 0% of the time, Pallas kernels for 4%

profile of v5, /device:TPU:0, one launch (start us, length us, event | category | flops | bytes accessed | tf_op | source)
XLA Modules:
  0.0 81.2 jit_solution(7573286179228239809)
XLA Ops:
  0.6 2.6 %shard_map.76 = (bf16[256,4096]{1,0:T(8,128)(2,1)S(1)}, f32[16,384]{1,0:T(8,128)S(1)}, f32[16,1152]{1,0:T(8,128)S(1)}, s32[256,128]{1,0:T(8,128)S(1)}, f32[9,256...) custom-call(bf16[256,4096]{1,0:T(8,128)(2,1)} %f_hbm.1, ...), custom_call_target="tpu_custom_call" | custom-call | tf_op jit(solution)/shard_map/pallas_call | solution.py:354
  3.7 0.8 %collective-permute-done.refs_1_ = f32[16,384]{1,0:T(8,128)S(1)} collective-permute-done((f32[16,384]{1,0:T(8,128)S(1)}, f32[16,384]{1,0:T(8,128)S(1)}, u32[]{:S(2)}, u32[]{:S(2)}) %collective-permute-start) | collective-permute-done | bytes 24608 | tf_op jit(solution)/shard_map/ppermute | solution.py:97
  4.6 2.0 %shard_map.77 = (f32[16,256]{1,0:T(8,128)}, bf16[64,256]{1,0:T(8,128)(2,1)S(1)}, bf16[256,128]{1,0:T(8,128)(2,1)S(1)}, f32[32,256]{1,0:T(8,128)S(1)}) custom-call(f32[16,384]{1,0:T(8,128)S(1)} %get-tuple-element.44.refs_0_, f32[16,384]{1,0:T(8,128)S(1)} %collective-permute-done.refs_1_, bf16[112,1024]{1,0:T(8,128)(2,1)S(1)} %get-tuple-element.45.refs_2_.refs_0_, ...), custom_call_target="tpu_custom_call" | custom-call | tf_op jit(solution)/shard_map/pallas_call | solution.py:354
  6.6 14.3 %all_to_all.22 = f32[32,1,256]{2,1,0:T(1,128)S(1)} all-to-all(f32[32,1,256]{2,1,0:T(1,128)S(1)} %copy.8), channel_id=1, replica_groups=mesh['tiles'=16,'pix'=2] {'tiles','pix'}, dimensions={0} | all-to-all | bytes 65536 | tf_op jit(solution)/shard_map/all_to_all | solution.py:404
  20.9 1.6 %shard_map.80 = (f32[16,1152]{1,0:T(8,128)S(1)}, f32[16,1152]{1,0:T(8,128)S(1)}, f32[16,1152]{1,0:T(8,128)S(1)}) custom-call(f32[32,256]{1,0:T(8,128)S(1)} %bitcast.16, bf16[256,4096]{1,0:T(8,128)(2,1)S(1)} %get-tuple-element.43.refs_6_.f_ref, f32[9,256,128]{2,1,0:T(8,128)S(1)} %get-tuple-element.53.bar_ref, ...), custom_call_target="tpu_custom_call" | custom-call | tf_op jit(solution)/shard_map/pallas_call | solution.py:354
  23.1 0.7 collective-permute-start.2
  23.8 2.3 %collective-permute-start.3 = (f32[16,1152]{1,0:T(8,128)S(1)}, f32[16,1152]{1,0:T(8,128)S(1)}, u32[]{:S(2)}, u32[]{:S(2)}) collective-permute-start(f32[16,1152]{1,0:T(8,128)S(1)} %get-tuple-element.58), channel_id=1, source_target_pairs={{0,6},{2,4},{4,2},{6,0},{8,14},{10,12},{12,10},{14,8},{16,22},{18,... | collective-permute-start | bytes 221192 | tf_op jit(solution)/shard_map/ppermute | solution.py:97
  27.2 1.0 %collective-permute-done.2 = f32[16,1152]{1,0:T(8,128)S(1)} collective-permute-done((f32[16,1152]{1,0:T(8,128)S(1)}, f32[16,1152]{1,0:T(8,128)S(1)}, u32[]{:S(2)}, u32[]{:S(2)}) %collective-permute-start.2) | collective-permute-done | bytes 73760 | tf_op jit(solution)/shard_map/ppermute | solution.py:97
  28.2 0.8 %collective-permute-done.3 = f32[16,1152]{1,0:T(8,128)S(1)} collective-permute-done((f32[16,1152]{1,0:T(8,128)S(1)}, f32[16,1152]{1,0:T(8,128)S(1)}, u32[]{:S(2)}, u32[]{:S(2)}) %collective-permute-start.3) | collective-permute-done | bytes 73760 | tf_op jit(solution)/shard_map/ppermute | solution.py:97
  30.3 3.2 %collective-permute-start.6 = (f32[16,1152]{1,0:T(8,128)S(1)}, f32[16,1152]{1,0:T(8,128)S(1)}, u32[]{:S(2)}, u32[]{:S(2)}) collective-permute-start(f32[16,1152]{1,0:T(8,128)S(1)} %add_add_fusion.1.refs_0_), channel_id=1, source_target_pairs={{0,16},{1,9},{2,18},{3,11},{4,20},{5,13},{6,22},{7,15},{8,24},{9,1... | collective-permute-start | bytes 221192 | tf_op jit(solution)/shard_map/ppermute | solution.py:106
  33.8 1.6 %collective-permute-done.4.refs_1_ = f32[16,1152]{1,0:T(8,128)S(1)} collective-permute-done((f32[16,1152]{1,0:T(8,128)S(1)}, f32[16,1152]{1,0:T(8,128)S(1)}, u32[]{:S(2)}, u32[]{:S(2)}) %collective-permute-start.4) | collective-permute-done | bytes 73760 | tf_op jit(solution)/shard_map/ppermute | solution.py:106
  35.5 1.6 %collective-permute-done.6.refs_3_ = f32[16,1152]{1,0:T(8,128)S(1)} collective-permute-done((f32[16,1152]{1,0:T(8,128)S(1)}, f32[16,1152]{1,0:T(8,128)S(1)}, u32[]{:S(2)}, u32[]{:S(2)}) %collective-permute-start.6) | collective-permute-done | bytes 73760 | tf_op jit(solution)/shard_map/ppermute | solution.py:106
  37.2 1.4 %collective-permute-start.9 = (f32[16,1152]{1,0:T(8,128)S(1)}, f32[16,1152]{1,0:T(8,128)S(1)}, u32[]{:S(2)}, u32[]{:S(2)}) collective-permute-start(f32[16,1152]{1,0:T(8,128)S(1)} %shard_map.81.chunk_ref.old_ref), channel_id=1, source_target_pairs={{0,6},{2,4},{4,2},{6,0},{8,14},{10,12},{12,10},{14,8},{16,22},{18,... | collective-permute-start | bytes 221192 | tf_op jit(solution)/shard_map/ppermute | solution.py:97
  39.3 1.5 %collective-permute-start.7 = (f32[16,1152]{1,0:T(8,128)S(1)}, f32[16,1152]{1,0:T(8,128)S(1)}, u32[]{:S(2)}, u32[]{:S(2)}) collective-permute-start(f32[16,1152]{1,0:T(8,128)S(1)} %shard_map.81.chunk_ref.old_ref), channel_id=1, source_target_pairs={{0,2},{2,0},{4,6},{6,4},{8,10},{10,8},{12,14},{14,12},{16,18},{18,... | collective-permute-start | bytes 221192 | tf_op jit(solution)/shard_map/ppermute | solution.py:97
  41.1 1.4 %collective-permute-done.9.chunk_ref = f32[16,1152]{1,0:T(8,128)S(1)} collective-permute-done((f32[16,1152]{1,0:T(8,128)S(1)}, f32[16,1152]{1,0:T(8,128)S(1)}, u32[]{:S(2)}, u32[]{:S(2)}) %collective-permute-start.9) | collective-permute-done | bytes 73760 | tf_op jit(solution)/shard_map/ppermute | solution.py:97
  44.1 1.2 %collective-permute-done.10.refs_1_ = f32[16,384]{1,0:T(8,128)S(1)} collective-permute-done((f32[16,384]{1,0:T(8,128)S(1)}, f32[16,384]{1,0:T(8,128)S(1)}, u32[]{:S(2)}, u32[]{:S(2)}) %collective-permute-start.10) | collective-permute-done | bytes 24608 | tf_op jit(solution)/shard_map/ppermute | solution.py:97
  45.3 1.5 %shard_map.86 = (f32[16,256]{1,0:T(8,128)S(1)}, bf16[64,256]{1,0:T(8,128)(2,1)S(1)}, bf16[256,128]{1,0:T(8,128)(2,1)S(1)}, f32[32,256]{1,0:T(8,128)S(1)}) custom-call(f32[16,384]{1,0:T(8,128)S(1)} %get-tuple-element.65.refs_0_, f32[16,384]{1,0:T(8,128)S(1)} %collective-permute-done.10.refs_1_, bf16[112,1024]{1,0:T(8,128)(2,1)S(1)} %get-tuple-element.66.refs_2_.refs_0_, ...), custom_call_target="tpu_custom_call" | custom-call | tf_op jit(solution)/shard_map/pallas_call | solution.py:354
  46.9 10.8 %all_to_all.23 = f32[32,1,256]{2,1,0:T(1,128)S(1)} all-to-all(f32[32,1,256]{2,1,0:T(1,128)S(1)} %copy.9), channel_id=1, replica_groups=mesh['tiles'=16,'pix'=2] {'tiles','pix'}, dimensions={0} | all-to-all | bytes 65536 | tf_op jit(solution)/shard_map/all_to_all | solution.py:404
  57.7 1.7 %shard_map.89 = (f32[16,1152]{1,0:T(8,128)S(1)}, f32[16,1152]{1,0:T(8,128)S(1)}, f32[16,1152]{1,0:T(8,128)S(1)}) custom-call(f32[32,256]{1,0:T(8,128)S(1)} %bitcast.13, bf16[256,4096]{1,0:T(8,128)(2,1)S(1)} %get-tuple-element.43.refs_6_.f_ref, f32[9,256,128]{2,1,0:T(8,128)S(1)} %get-tuple-element.53.bar_ref, ...), custom_call_target="tpu_custom_call" | custom-call | tf_op jit(solution)/shard_map/pallas_call | solution.py:354
  59.9 0.7 collective-permute-start.12
  60.6 2.3 %collective-permute-start.13 = (f32[16,1152]{1,0:T(8,128)S(1)}, f32[16,1152]{1,0:T(8,128)S(1)}, u32[]{:S(2)}, u32[]{:S(2)}) collective-permute-start(f32[16,1152]{1,0:T(8,128)S(1)} %get-tuple-element.76), channel_id=1, source_target_pairs={{0,6},{2,4},{4,2},{6,0},{8,14},{10,12},{12,10},{14,8},{16,22},{18,... | collective-permute-start | bytes 221192 | tf_op jit(solution)/shard_map/ppermute | solution.py:97
  62.9 0.7 shard_map.88
  64.0 1.0 %collective-permute-done.12 = f32[16,1152]{1,0:T(8,128)S(1)} collective-permute-done((f32[16,1152]{1,0:T(8,128)S(1)}, f32[16,1152]{1,0:T(8,128)S(1)}, u32[]{:S(2)}, u32[]{:S(2)}) %collective-permute-start.12) | collective-permute-done | bytes 73760 | tf_op jit(solution)/shard_map/ppermute | solution.py:97
  65.0 0.8 %collective-permute-done.13 = f32[16,1152]{1,0:T(8,128)S(1)} collective-permute-done((f32[16,1152]{1,0:T(8,128)S(1)}, f32[16,1152]{1,0:T(8,128)S(1)}, u32[]{:S(2)}, u32[]{:S(2)}) %collective-permute-start.13) | collective-permute-done | bytes 73760 | tf_op jit(solution)/shard_map/ppermute | solution.py:97
  67.1 3.2 %collective-permute-start.16 = (f32[16,1152]{1,0:T(8,128)S(1)}, f32[16,1152]{1,0:T(8,128)S(1)}, u32[]{:S(2)}, u32[]{:S(2)}) collective-permute-start(f32[16,1152]{1,0:T(8,128)S(1)} %add_add_fusion.refs_0_), channel_id=1, source_target_pairs={{0,16},{1,9},{2,18},{3,11},{4,20},{5,13},{6,22},{7,15},{8,24},{9,1... | collective-permute-start | bytes 221192 | tf_op jit(solution)/shard_map/ppermute | solution.py:106
  70.6 1.6 %collective-permute-done.14.refs_1_ = f32[16,1152]{1,0:T(8,128)S(1)} collective-permute-done((f32[16,1152]{1,0:T(8,128)S(1)}, f32[16,1152]{1,0:T(8,128)S(1)}, u32[]{:S(2)}, u32[]{:S(2)}) %collective-permute-start.14) | collective-permute-done | bytes 73760 | tf_op jit(solution)/shard_map/ppermute | solution.py:106
  72.2 1.6 %collective-permute-done.16.refs_3_ = f32[16,1152]{1,0:T(8,128)S(1)} collective-permute-done((f32[16,1152]{1,0:T(8,128)S(1)}, f32[16,1152]{1,0:T(8,128)S(1)}, u32[]{:S(2)}, u32[]{:S(2)}) %collective-permute-start.16) | collective-permute-done | bytes 73760 | tf_op jit(solution)/shard_map/ppermute | solution.py:106
  74.0 1.4 %collective-permute-start.17 = (f32[16,1152]{1,0:T(8,128)S(1)}, f32[16,1152]{1,0:T(8,128)S(1)}, u32[]{:S(2)}, u32[]{:S(2)}) collective-permute-start(f32[16,1152]{1,0:T(8,128)S(1)} %shard_map.90.refs_0_), channel_id=1, source_target_pairs={{0,6},{2,4},{4,2},{6,0},{8,14},{10,12},{12,10},{14,8},{16,22},{18,... | collective-permute-start | bytes 221192 | tf_op jit(solution)/shard_map/ppermute | solution.py:97
  76.1 1.5 %collective-permute-start.19 = (f32[16,1152]{1,0:T(8,128)S(1)}, f32[16,1152]{1,0:T(8,128)S(1)}, u32[]{:S(2)}, u32[]{:S(2)}) collective-permute-start(f32[16,1152]{1,0:T(8,128)S(1)} %shard_map.90.refs_0_), channel_id=1, source_target_pairs={{0,2},{2,0},{4,6},{6,4},{8,10},{10,8},{12,14},{14,12},{16,18},{18,... | collective-permute-start | bytes 221192 | tf_op jit(solution)/shard_map/ppermute | solution.py:97
  77.6 1.8 %collective-permute-done.17.refs_1_ = f32[16,1152]{1,0:T(8,128)S(1)} collective-permute-done((f32[16,1152]{1,0:T(8,128)S(1)}, f32[16,1152]{1,0:T(8,128)S(1)}, u32[]{:S(2)}, u32[]{:S(2)}) %collective-permute-start.17) | collective-permute-done | bytes 73760 | tf_op jit(solution)/shard_map/ppermute | solution.py:97
  79.4 0.8 collective-permute-done.18.refs_2_
  80.4 0.8 shard_map.91
  (32 shorter events, 10.5 us)
Async XLA Ops:
  3.2 1.4 %collective-permute-start = (f32[16,384]{1,0:T(8,128)S(1)}, f32[16,384]{1,0:T(8,128)S(1)}, u32[]{:S(2)}, u32[]{:S(2)}) collective-permute-start(f32[16,384]{1,0:T(8,128)S(1)} %get-tuple-element.44.refs_0_), channel_id=1, source_target_pairs={{0,1},{1,0},{2,3},{3,2},{4,5},{5,4},{6,7},{7,6},{8,9},{9,8},{10,11... | collective-permute-start | bytes 73736 | tf_op jit(solution)/shard_map/ppermute | solution.py:97
  22.5 4.7 %collective-permute-start.1 = (f32[16,1152]{1,0:T(8,128)S(1)}, f32[16,1152]{1,0:T(8,128)S(1)}, u32[]{:S(2)}, u32[]{:S(2)}) collective-permute-start(f32[16,1152]{1,0:T(8,128)S(1)} %get-tuple-element.56), channel_id=1, source_target_pairs={{0,2},{2,0},{4,6},{6,4},{8,10},{10,8},{12,14},{14,12},{16,18},{18,... | collective-permute-start | bytes 221192 | tf_op jit(solution)/shard_map/ppermute | solution.py:97
  23.1 5.1 %collective-permute-start.2 = (f32[16,1152]{1,0:T(8,128)S(1)}, f32[16,1152]{1,0:T(8,128)S(1)}, u32[]{:S(2)}, u32[]{:S(2)}) collective-permute-start(f32[16,1152]{1,0:T(8,128)S(1)} %get-tuple-element.57), channel_id=1, source_target_pairs={{0,4},{2,6},{4,0},{6,2},{8,12},{10,14},{12,8},{14,10},{16,20},{18,... | collective-permute-start | bytes 221192 | tf_op jit(solution)/shard_map/ppermute | solution.py:97
  23.8 5.3 %collective-permute-start.3 = (f32[16,1152]{1,0:T(8,128)S(1)}, f32[16,1152]{1,0:T(8,128)S(1)}, u32[]{:S(2)}, u32[]{:S(2)}) collective-permute-start(f32[16,1152]{1,0:T(8,128)S(1)} %get-tuple-element.58), channel_id=1, source_target_pairs={{0,6},{2,4},{4,2},{6,0},{8,14},{10,12},{12,10},{14,8},{16,22},{18,... | collective-permute-start | bytes 221192 | tf_op jit(solution)/shard_map/ppermute | solution.py:97
  29.0 6.4 %collective-permute-start.4 = (f32[16,1152]{1,0:T(8,128)S(1)}, f32[16,1152]{1,0:T(8,128)S(1)}, u32[]{:S(2)}, u32[]{:S(2)}) collective-permute-start(f32[16,1152]{1,0:T(8,128)S(1)} %add_add_fusion.1.refs_0_), channel_id=1, source_target_pairs={{0,24},{1,25},{2,26},{3,27},{4,28},{5,29},{6,30},{7,31},{8,16},{9,... | collective-permute-start | bytes 221192 | tf_op jit(solution)/shard_map/ppermute | solution.py:106
  29.7 5.8 %collective-permute-start.5 = (f32[16,1152]{1,0:T(8,128)S(1)}, f32[16,1152]{1,0:T(8,128)S(1)}, u32[]{:S(2)}, u32[]{:S(2)}) collective-permute-start(f32[16,1152]{1,0:T(8,128)S(1)} %add_add_fusion.1.refs_0_), channel_id=1, source_target_pairs={{0,8},{1,17},{2,10},{3,19},{4,12},{5,21},{6,14},{7,23},{8,0},{9,25... | collective-permute-start | bytes 221192 | tf_op jit(solution)/shard_map/ppermute | solution.py:106
  30.3 6.8 %collective-permute-start.6 = (f32[16,1152]{1,0:T(8,128)S(1)}, f32[16,1152]{1,0:T(8,128)S(1)}, u32[]{:S(2)}, u32[]{:S(2)}) collective-permute-start(f32[16,1152]{1,0:T(8,128)S(1)} %add_add_fusion.1.refs_0_), channel_id=1, source_target_pairs={{0,16},{1,9},{2,18},{3,11},{4,20},{5,13},{6,22},{7,15},{8,24},{9,1... | collective-permute-start | bytes 221192 | tf_op jit(solution)/shard_map/ppermute | solution.py:106
  37.2 5.3 %collective-permute-start.9 = (f32[16,1152]{1,0:T(8,128)S(1)}, f32[16,1152]{1,0:T(8,128)S(1)}, u32[]{:S(2)}, u32[]{:S(2)}) collective-permute-start(f32[16,1152]{1,0:T(8,128)S(1)} %shard_map.81.chunk_ref.old_ref), channel_id=1, source_target_pairs={{0,6},{2,4},{4,2},{6,0},{8,14},{10,12},{12,10},{14,8},{16,22},{18,... | collective-permute-start | bytes 221192 | tf_op jit(solution)/shard_map/ppermute | solution.py:97
  38.6 4.7 %collective-permute-start.8 = (f32[16,1152]{1,0:T(8,128)S(1)}, f32[16,1152]{1,0:T(8,128)S(1)}, u32[]{:S(2)}, u32[]{:S(2)}) collective-permute-start(f32[16,1152]{1,0:T(8,128)S(1)} %shard_map.81.chunk_ref.old_ref), channel_id=1, source_target_pairs={{0,4},{2,6},{4,0},{6,2},{8,12},{10,14},{12,8},{14,10},{16,20},{18,... | collective-permute-start | bytes 221192 | tf_op jit(solution)/shard_map/ppermute | solution.py:97
  39.3 4.4 %collective-permute-start.7 = (f32[16,1152]{1,0:T(8,128)S(1)}, f32[16,1152]{1,0:T(8,128)S(1)}, u32[]{:S(2)}, u32[]{:S(2)}) collective-permute-start(f32[16,1152]{1,0:T(8,128)S(1)} %shard_map.81.chunk_ref.old_ref), channel_id=1, source_target_pairs={{0,2},{2,0},{4,6},{6,4},{8,10},{10,8},{12,14},{14,12},{16,18},{18,... | collective-permute-start | bytes 221192 | tf_op jit(solution)/shard_map/ppermute | solution.py:97
  44.1 1.2 %collective-permute-start.10 = (f32[16,384]{1,0:T(8,128)S(1)}, f32[16,384]{1,0:T(8,128)S(1)}, u32[]{:S(2)}, u32[]{:S(2)}) collective-permute-start(f32[16,384]{1,0:T(8,128)S(1)} %get-tuple-element.65.refs_0_), channel_id=1, source_target_pairs={{0,1},{1,0},{2,3},{3,2},{4,5},{5,4},{6,7},{7,6},{8,9},{9,8},{10,11... | collective-permute-start | bytes 73736 | tf_op jit(solution)/shard_map/ppermute | solution.py:97
  59.3 4.7 %collective-permute-start.11 = (f32[16,1152]{1,0:T(8,128)S(1)}, f32[16,1152]{1,0:T(8,128)S(1)}, u32[]{:S(2)}, u32[]{:S(2)}) collective-permute-start(f32[16,1152]{1,0:T(8,128)S(1)} %get-tuple-element.74), channel_id=1, source_target_pairs={{0,2},{2,0},{4,6},{6,4},{8,10},{10,8},{12,14},{14,12},{16,18},{18,... | collective-permute-start | bytes 221192 | tf_op jit(solution)/shard_map/ppermute | solution.py:97
  59.9 5.1 %collective-permute-start.12 = (f32[16,1152]{1,0:T(8,128)S(1)}, f32[16,1152]{1,0:T(8,128)S(1)}, u32[]{:S(2)}, u32[]{:S(2)}) collective-permute-start(f32[16,1152]{1,0:T(8,128)S(1)} %get-tuple-element.75), channel_id=1, source_target_pairs={{0,4},{2,6},{4,0},{6,2},{8,12},{10,14},{12,8},{14,10},{16,20},{18,... | collective-permute-start | bytes 221192 | tf_op jit(solution)/shard_map/ppermute | solution.py:97
  60.6 5.3 %collective-permute-start.13 = (f32[16,1152]{1,0:T(8,128)S(1)}, f32[16,1152]{1,0:T(8,128)S(1)}, u32[]{:S(2)}, u32[]{:S(2)}) collective-permute-start(f32[16,1152]{1,0:T(8,128)S(1)} %get-tuple-element.76), channel_id=1, source_target_pairs={{0,6},{2,4},{4,2},{6,0},{8,14},{10,12},{12,10},{14,8},{16,22},{18,... | collective-permute-start | bytes 221192 | tf_op jit(solution)/shard_map/ppermute | solution.py:97
  65.8 6.4 %collective-permute-start.14 = (f32[16,1152]{1,0:T(8,128)S(1)}, f32[16,1152]{1,0:T(8,128)S(1)}, u32[]{:S(2)}, u32[]{:S(2)}) collective-permute-start(f32[16,1152]{1,0:T(8,128)S(1)} %add_add_fusion.refs_0_), channel_id=1, source_target_pairs={{0,24},{1,25},{2,26},{3,27},{4,28},{5,29},{6,30},{7,31},{8,16},{9,... | collective-permute-start | bytes 221192 | tf_op jit(solution)/shard_map/ppermute | solution.py:106
  66.5 5.8 %collective-permute-start.15 = (f32[16,1152]{1,0:T(8,128)S(1)}, f32[16,1152]{1,0:T(8,128)S(1)}, u32[]{:S(2)}, u32[]{:S(2)}) collective-permute-start(f32[16,1152]{1,0:T(8,128)S(1)} %add_add_fusion.refs_0_), channel_id=1, source_target_pairs={{0,8},{1,17},{2,10},{3,19},{4,12},{5,21},{6,14},{7,23},{8,0},{9,25... | collective-permute-start | bytes 221192 | tf_op jit(solution)/shard_map/ppermute | solution.py:106
  67.1 6.8 %collective-permute-start.16 = (f32[16,1152]{1,0:T(8,128)S(1)}, f32[16,1152]{1,0:T(8,128)S(1)}, u32[]{:S(2)}, u32[]{:S(2)}) collective-permute-start(f32[16,1152]{1,0:T(8,128)S(1)} %add_add_fusion.refs_0_), channel_id=1, source_target_pairs={{0,16},{1,9},{2,18},{3,11},{4,20},{5,13},{6,22},{7,15},{8,24},{9,1... | collective-permute-start | bytes 221192 | tf_op jit(solution)/shard_map/ppermute | solution.py:106
  74.0 5.3 %collective-permute-start.17 = (f32[16,1152]{1,0:T(8,128)S(1)}, f32[16,1152]{1,0:T(8,128)S(1)}, u32[]{:S(2)}, u32[]{:S(2)}) collective-permute-start(f32[16,1152]{1,0:T(8,128)S(1)} %shard_map.90.refs_0_), channel_id=1, source_target_pairs={{0,6},{2,4},{4,2},{6,0},{8,14},{10,12},{12,10},{14,8},{16,22},{18,... | collective-permute-start | bytes 221192 | tf_op jit(solution)/shard_map/ppermute | solution.py:97
  75.4 4.7 %collective-permute-start.18 = (f32[16,1152]{1,0:T(8,128)S(1)}, f32[16,1152]{1,0:T(8,128)S(1)}, u32[]{:S(2)}, u32[]{:S(2)}) collective-permute-start(f32[16,1152]{1,0:T(8,128)S(1)} %shard_map.90.refs_0_), channel_id=1, source_target_pairs={{0,4},{2,6},{4,0},{6,2},{8,12},{10,14},{12,8},{14,10},{16,20},{18,... | collective-permute-start | bytes 221192 | tf_op jit(solution)/shard_map/ppermute | solution.py:97
  76.1 4.4 %collective-permute-start.19 = (f32[16,1152]{1,0:T(8,128)S(1)}, f32[16,1152]{1,0:T(8,128)S(1)}, u32[]{:S(2)}, u32[]{:S(2)}) collective-permute-start(f32[16,1152]{1,0:T(8,128)S(1)} %shard_map.90.refs_0_), channel_id=1, source_target_pairs={{0,2},{2,0},{4,6},{6,4},{8,10},{10,8},{12,14},{14,12},{16,18},{18,... | collective-permute-start | bytes 221192 | tf_op jit(solution)/shard_map/ppermute | solution.py:97

commit v6 on v5

--- a/solution.py
+++ b/solution.py
@@ -160,7 +160,7 @@
     return pl.multiple_of((me ^ k) * sz.chunk, BLOCK)
 
 
-def first_projection(sz, f_hbm, b_hbm, d_hbm, valid_hbm, fore_hbm, f_ref, packed_ref, own_ref, least_ref, bar_ref, valid_ref, *refs):
+def first_projection(sz, f_hbm, b_hbm, d_hbm, valid_hbm, fore_hbm, f_ref, packed_ref, own_ref, least_ref, valid_ref, *refs):
     stack_refs, (b_ref, d_ref, flags_ref, sems) = refs[: sz.group], refs[sz.group :]
     small = [
         pltpu.make_async_copy(d_hbm, d_ref, sems.at[0]),
@@ -190,14 +190,19 @@
         copy.wait()
     valid = flags_ref[0:1, :] != 0
     valid_ref[...] = jnp.broadcast_to(valid.astype(F32), valid_ref.shape)
-    least = jnp.broadcast_to(jnp.where(valid, flags_ref[8:9, :], ROW_PX), (BLOCK, sz.tile_dev)).T
-    least_ref[...] = least
-    for block in range(bar_ref.shape[0]):
-        bar_ref[block] = jnp.where(least <= block, 1.0, jnp.inf)
+    least_ref[...] = jnp.where(valid, flags_ref[8:9, :], ROW_PX) + jnp.zeros(least_ref.shape, jnp.int32)
     for copy in large:
         copy.wait()
     proj = tree([lax.dot_general(p, f_ref[:, s], NT, preferred_element_type=F32) for p, s in zip(parts, spans)])
     pack_projections(sz, (proj, gram, dark), packed_ref)
+
+
+def make_masks(least_ref, keep_ref, bar_ref):
+    least = jnp.broadcast_to(least_ref[0:1, :], (BLOCK, least_ref.shape[1])).T
+    for block in range(bar_ref.shape[0]):
+        usable = least <= block
+        keep_ref[block] = jnp.where(usable, 1.0, 0.0)
+        bar_ref[block] = jnp.where(usable, 1.0, jnp.inf)
 
 
 def later_projection(sz, k, f_ref, chunk_ref, *refs):
@@ -221,7 +226,7 @@
 def solve_tiles(sz, width, *refs):
     packed = refs[: sz.n_pix]
     stack_refs, refs = refs[sz.n_pix : sz.n_pix + sz.group], refs[sz.n_pix + sz.group :]
-    f_ref, least_ref, valid_ref, coef_ref, three_ref, parts_ref, note_ref = refs
+    f_ref, keep_ref, valid_ref, coef_ref, three_ref, parts_ref, note_ref = refs
     r, td = sz.rank, sz.tile_dev
     a = tree([ref[...] for ref in packed]) / sz.pixels_all
     gram = a[:, td : td + r] + RIDGE * eye_at((r, r), 0)
@@ -236,7 +241,6 @@
     parts = jnp.concatenate([hi, hi, hi, mid, mid, low, ones], axis=0).T.astype(BF16)
     parts_ref[...] = parts
     parts = parts[:, 0 : sz.stack]
-    least = least_ref[...]
 
     total = jnp.zeros((8, BLOCK), F32)
     for k, stack_ref in enumerate(stack_refs):
@@ -246,7 +250,8 @@
             square = res * res
             for j in range(width // BLOCK):
                 block = (start // BLOCK + step * (width // BLOCK) + j) % (ROW_PX // BLOCK)
-                term = jnp.where(least <= block, square[:, j * BLOCK : (j + 1) * BLOCK], 0.0)
+                keep = keep_ref[jnp.minimum(block, keep_ref.shape[0] - 1)]
+                term = keep * square[:, j * BLOCK : (j + 1) * BLOCK]
                 total = total + jnp.sum(term.reshape(td // 8, 8, BLOCK), axis=0)
     total = jnp.sum(jnp.sum(total, axis=0, keepdims=True), axis=1, keepdims=True)
     products = jnp.concatenate([coef[i : i + 1] * coef for i in range(r)], axis=0)
@@ -375,9 +380,9 @@
     masks = sz.tile_levels[0]
     for iteration in range(ITERS):
         if iteration == 0:
-            frames, packed, old, least, bar, valid, *stacks = call(
+            frames, packed, old, least, valid, *stacks = call(
                 functools.partial(first_projection, sz),
-                [((td, pd), BF16), packed_out, (chunk_shape, F32), ((td, BLOCK), jnp.int32), ((ROW_PX // BLOCK // 2 + 1, td, BLOCK), F32), ((8, td), F32)]
+                [((td, pd), BF16), packed_out, (chunk_shape, F32), ((8, td), jnp.int32), ((8, td), F32)]
                 + [stack_out] * sz.group,
                 [frames, basis_start, dark_start.reshape(pd // BLOCK, BLOCK), tile_valid.reshape(1, td), foreground_blocks.reshape(1, td)],
                 in_hbm=True,
@@ -395,11 +400,14 @@
                     functools.partial(later_projection, sz, k), [packed_out, stack_out], [frames, chunks[k]] + before
                 )
                 before = [packed]
+        if iteration == 0:
+            mask = ((ROW_PX // BLOCK // 2 + 1, td, BLOCK), F32)
+            keep, bar = call(make_masks, [mask, mask], [least])
         both = [packed] + [partner(packed, "pix", m) for m in pix_masks]
         coef, three, parts, note = call(
             functools.partial(solve_tiles, sz, width),
             [((r, td), F32), ((3 * r + 16, td), BF16), ((td, BLOCK), BF16), ((devices, r * r), F32)],
-            both + stacks + [frames, least, valid],
+            both + stacks + [frames, keep, valid],
         )
         notes = lax.all_to_all(note, everyone, 0, 0, tiled=True)
         (inverse,) = call(functools.partial(invert_gram, sz), [((r, BLOCK), F32)], [notes])

time: 81.4 us -> 81.2 us (level)
    pallas_call x16 -> x17, Pallas kernels: 14.1 us -> 14.2 us  [call(): pl.pallas_call(body, out_shape=[jax.ShapeDtypeStruct(s, t) for s, t in ou...]
where the time goes in v6:
time: 81.2 us; the launch traced here: 81 us
  blocking collectives  25.1 us (31%)
  starting transfers between devices  23.6 us (29%)
  waiting for transfers between devices  17.3 us (21%)
  Pallas kernels  14.2 us (17%)
    all_to_all x2, blocking collectives, local(): notes = lax.all_to_all(note, everyone, 0, 0, tiled=True)  25.1 us
    ppermute x14, starting transfers between devices, partner(): return lax.ppermute(x, axis, [(i, i ^ mask) for i in range(n)])  14.7 us
    pallas_call x17, Pallas kernels, call(): pl.pallas_call(body, out_shape=[jax.ShapeDtypeStruct(s, t) for s, t in ou...  14.2 us
    ppermute x14, waiting for transfers between devices, partner(): return lax.ppermute(x, axis, [(i, i ^ mask) for i in range(n)])  11 us
    ppermute x6, starting transfers between devices, crossed(): return lax.ppermute(x, ('tiles', 'pix'), pairs)  8.91 us
    ppermute x6, waiting for transfers between devices, crossed(): return lax.ppermute(x, ('tiles', 'pix'), pairs)  6.35 us
  transfers between devices with their start and end apart: 20, of which 17 were waited for; matrix products, arithmetic and copies ran while one was open for 0% of the time, Pallas kernels for 4%

profile of v6, /device:TPU:0, one launch (start us, length us, event | category | flops | bytes accessed | tf_op | source)
XLA Modules:
  0.0 81.0 jit_solution(4657831187468059864)
XLA Ops:
  0.6 2.6 %shard_map.76 = (bf16[256,4096]{1,0:T(8,128)(2,1)S(1)}, f32[16,384]{1,0:T(8,128)S(1)}, f32[16,1152]{1,0:T(8,128)S(1)}, s32[8,256]{1,0:T(8,128)S(1)}, f32[8,256]{...) custom-call(bf16[256,4096]{1,0:T(8,128)(2,1)} %f_hbm.1, ...), custom_call_target="tpu_custom_call" | custom-call | tf_op jit(solution)/shard_map/pallas_call | solution.py:359
  4.6 1.9 %shard_map.78 = (f32[16,256]{1,0:T(8,128)}, bf16[64,256]{1,0:T(8,128)(2,1)S(1)}, bf16[256,128]{1,0:T(8,128)(2,1)S(1)}, f32[32,256]{1,0:T(8,128)S(1)}) custom-call(f32[16,384]{1,0:T(8,128)S(1)} %get-tuple-element.45.refs_0_, f32[16,384]{1,0:T(8,128)S(1)} %collective-permute-done.refs_1_, bf16[112,1024]{1,0:T(8,128)(2,1)S(1)} %get-tuple-element.46.refs_2_.refs_0_, ...), custom_call_target="tpu_custom_call" | custom-call | tf_op jit(solution)/shard_map/pallas_call | solution.py:359
  6.5 14.3 %all_to_all.22 = f32[32,1,256]{2,1,0:T(1,128)S(1)} all-to-all(f32[32,1,256]{2,1,0:T(1,128)S(1)} %copy.8), channel_id=1, replica_groups=mesh['tiles'=16,'pix'=2] {'tiles','pix'}, dimensions={0} | all-to-all | bytes 65536 | tf_op jit(solution)/shard_map/all_to_all | solution.py:412
  20.7 1.7 %shard_map.81 = (f32[16,1152]{1,0:T(8,128)S(1)}, f32[16,1152]{1,0:T(8,128)S(1)}, f32[16,1152]{1,0:T(8,128)S(1)}) custom-call(f32[32,256]{1,0:T(8,128)S(1)} %bitcast.13, bf16[256,4096]{1,0:T(8,128)(2,1)S(1)} %get-tuple-element.44.refs_6_.f_ref, f32[9,256,128]{2,1,0:T(8,128)S(1)} %get-tuple-element.55.bar_ref, ...), custom_call_target="tpu_custom_call" | custom-call | tf_op jit(solution)/shard_map/pallas_call | solution.py:359
  22.9 0.7 collective-permute-start.2
  23.6 2.3 %collective-permute-start.3 = (f32[16,1152]{1,0:T(8,128)S(1)}, f32[16,1152]{1,0:T(8,128)S(1)}, u32[]{:S(2)}, u32[]{:S(2)}) collective-permute-start(f32[16,1152]{1,0:T(8,128)S(1)} %get-tuple-element.60), channel_id=1, source_target_pairs={{0,6},{2,4},{4,2},{6,0},{8,14},{10,12},{12,10},{14,8},{16,22},{18,... | collective-permute-start | bytes 221192 | tf_op jit(solution)/shard_map/ppermute | solution.py:97
  25.9 0.7 shard_map.80
  27.1 1.0 %collective-permute-done.2 = f32[16,1152]{1,0:T(8,128)S(1)} collective-permute-done((f32[16,1152]{1,0:T(8,128)S(1)}, f32[16,1152]{1,0:T(8,128)S(1)}, u32[]{:S(2)}, u32[]{:S(2)}) %collective-permute-start.2) | collective-permute-done | bytes 73760 | tf_op jit(solution)/shard_map/ppermute | solution.py:97
  28.1 0.8 %collective-permute-done.3 = f32[16,1152]{1,0:T(8,128)S(1)} collective-permute-done((f32[16,1152]{1,0:T(8,128)S(1)}, f32[16,1152]{1,0:T(8,128)S(1)}, u32[]{:S(2)}, u32[]{:S(2)}) %collective-permute-start.3) | collective-permute-done | bytes 73760 | tf_op jit(solution)/shard_map/ppermute | solution.py:97
  30.1 3.2 %collective-permute-start.6 = (f32[16,1152]{1,0:T(8,128)S(1)}, f32[16,1152]{1,0:T(8,128)S(1)}, u32[]{:S(2)}, u32[]{:S(2)}) collective-permute-start(f32[16,1152]{1,0:T(8,128)S(1)} %add_add_fusion.1.refs_0_), channel_id=1, source_target_pairs={{0,16},{1,9},{2,18},{3,11},{4,20},{5,13},{6,22},{7,15},{8,24},{9,1... | collective-permute-start | bytes 221192 | tf_op jit(solution)/shard_map/ppermute | solution.py:106
  33.7 1.6 %collective-permute-done.4.refs_1_ = f32[16,1152]{1,0:T(8,128)S(1)} collective-permute-done((f32[16,1152]{1,0:T(8,128)S(1)}, f32[16,1152]{1,0:T(8,128)S(1)}, u32[]{:S(2)}, u32[]{:S(2)}) %collective-permute-start.4) | collective-permute-done | bytes 73760 | tf_op jit(solution)/shard_map/ppermute | solution.py:106
  35.3 1.6 %collective-permute-done.6.refs_3_ = f32[16,1152]{1,0:T(8,128)S(1)} collective-permute-done((f32[16,1152]{1,0:T(8,128)S(1)}, f32[16,1152]{1,0:T(8,128)S(1)}, u32[]{:S(2)}, u32[]{:S(2)}) %collective-permute-start.6) | collective-permute-done | bytes 73760 | tf_op jit(solution)/shard_map/ppermute | solution.py:106
  37.1 1.4 %collective-permute-start.9 = (f32[16,1152]{1,0:T(8,128)S(1)}, f32[16,1152]{1,0:T(8,128)S(1)}, u32[]{:S(2)}, u32[]{:S(2)}) collective-permute-start(f32[16,1152]{1,0:T(8,128)S(1)} %shard_map.82.chunk_ref.old_ref), channel_id=1, source_target_pairs={{0,6},{2,4},{4,2},{6,0},{8,14},{10,12},{12,10},{14,8},{16,22},{18,... | collective-permute-start | bytes 221192 | tf_op jit(solution)/shard_map/ppermute | solution.py:97
  39.1 1.5 %collective-permute-start.7 = (f32[16,1152]{1,0:T(8,128)S(1)}, f32[16,1152]{1,0:T(8,128)S(1)}, u32[]{:S(2)}, u32[]{:S(2)}) collective-permute-start(f32[16,1152]{1,0:T(8,128)S(1)} %shard_map.82.chunk_ref.old_ref), channel_id=1, source_target_pairs={{0,2},{2,0},{4,6},{6,4},{8,10},{10,8},{12,14},{14,12},{16,18},{18,... | collective-permute-start | bytes 221192 | tf_op jit(solution)/shard_map/ppermute | solution.py:97
  41.0 1.4 %collective-permute-done.9.chunk_ref = f32[16,1152]{1,0:T(8,128)S(1)} collective-permute-done((f32[16,1152]{1,0:T(8,128)S(1)}, f32[16,1152]{1,0:T(8,128)S(1)}, u32[]{:S(2)}, u32[]{:S(2)}) %collective-permute-start.9) | collective-permute-done | bytes 73760 | tf_op jit(solution)/shard_map/ppermute | solution.py:97
  44.0 1.2 %collective-permute-done.10.refs_1_ = f32[16,384]{1,0:T(8,128)S(1)} collective-permute-done((f32[16,384]{1,0:T(8,128)S(1)}, f32[16,384]{1,0:T(8,128)S(1)}, u32[]{:S(2)}, u32[]{:S(2)}) %collective-permute-start.10) | collective-permute-done | bytes 24608 | tf_op jit(solution)/shard_map/ppermute | solution.py:97
  45.2 1.5 %shard_map.87 = (f32[16,256]{1,0:T(8,128)S(1)}, bf16[64,256]{1,0:T(8,128)(2,1)S(1)}, bf16[256,128]{1,0:T(8,128)(2,1)S(1)}, f32[32,256]{1,0:T(8,128)S(1)}) custom-call(f32[16,384]{1,0:T(8,128)S(1)} %get-tuple-element.67.refs_0_, f32[16,384]{1,0:T(8,128)S(1)} %collective-permute-done.10.refs_1_, bf16[112,1024]{1,0:T(8,128)(2,1)S(1)} %get-tuple-element.68.refs_2_.refs_0_, ...), custom_call_target="tpu_custom_call" | custom-call | tf_op jit(solution)/shard_map/pallas_call | solution.py:359
  46.7 10.8 %all_to_all.23 = f32[32,1,256]{2,1,0:T(1,128)S(1)} all-to-all(f32[32,1,256]{2,1,0:T(1,128)S(1)} %copy.9), channel_id=1, replica_groups=mesh['tiles'=16,'pix'=2] {'tiles','pix'}, dimensions={0} | all-to-all | bytes 65536 | tf_op jit(solution)/shard_map/all_to_all | solution.py:412
  57.5 1.7 %shard_map.90 = (f32[16,1152]{1,0:T(8,128)S(1)}, f32[16,1152]{1,0:T(8,128)S(1)}, f32[16,1152]{1,0:T(8,128)S(1)}) custom-call(f32[32,256]{1,0:T(8,128)S(1)} %bitcast.16, bf16[256,4096]{1,0:T(8,128)(2,1)S(1)} %get-tuple-element.44.refs_6_.f_ref, f32[9,256,128]{2,1,0:T(8,128)S(1)} %get-tuple-element.55.bar_ref, ...), custom_call_target="tpu_custom_call" | custom-call | tf_op jit(solution)/shard_map/pallas_call | solution.py:359
  59.7 0.7 collective-permute-start.12
  60.4 2.3 %collective-permute-start.13 = (f32[16,1152]{1,0:T(8,128)S(1)}, f32[16,1152]{1,0:T(8,128)S(1)}, u32[]{:S(2)}, u32[]{:S(2)}) collective-permute-start(f32[16,1152]{1,0:T(8,128)S(1)} %get-tuple-element.78), channel_id=1, source_target_pairs={{0,6},{2,4},{4,2},{6,0},{8,14},{10,12},{12,10},{14,8},{16,22},{18,... | collective-permute-start | bytes 221192 | tf_op jit(solution)/shard_map/ppermute | solution.py:97
  62.7 0.7 shard_map.89
  63.8 1.0 %collective-permute-done.12 = f32[16,1152]{1,0:T(8,128)S(1)} collective-permute-done((f32[16,1152]{1,0:T(8,128)S(1)}, f32[16,1152]{1,0:T(8,128)S(1)}, u32[]{:S(2)}, u32[]{:S(2)}) %collective-permute-start.12) | collective-permute-done | bytes 73760 | tf_op jit(solution)/shard_map/ppermute | solution.py:97
  64.8 0.8 %collective-permute-done.13 = f32[16,1152]{1,0:T(8,128)S(1)} collective-permute-done((f32[16,1152]{1,0:T(8,128)S(1)}, f32[16,1152]{1,0:T(8,128)S(1)}, u32[]{:S(2)}, u32[]{:S(2)}) %collective-permute-start.13) | collective-permute-done | bytes 73760 | tf_op jit(solution)/shard_map/ppermute | solution.py:97
  66.9 3.2 %collective-permute-start.16 = (f32[16,1152]{1,0:T(8,128)S(1)}, f32[16,1152]{1,0:T(8,128)S(1)}, u32[]{:S(2)}, u32[]{:S(2)}) collective-permute-start(f32[16,1152]{1,0:T(8,128)S(1)} %add_add_fusion.refs_0_), channel_id=1, source_target_pairs={{0,16},{1,9},{2,18},{3,11},{4,20},{5,13},{6,22},{7,15},{8,24},{9,1... | collective-permute-start | bytes 221192 | tf_op jit(solution)/shard_map/ppermute | solution.py:106
  70.4 1.6 %collective-permute-done.14.refs_1_ = f32[16,1152]{1,0:T(8,128)S(1)} collective-permute-done((f32[16,1152]{1,0:T(8,128)S(1)}, f32[16,1152]{1,0:T(8,128)S(1)}, u32[]{:S(2)}, u32[]{:S(2)}) %collective-permute-start.14) | collective-permute-done | bytes 73760 | tf_op jit(solution)/shard_map/ppermute | solution.py:106
  72.0 1.6 %collective-permute-done.16.refs_3_ = f32[16,1152]{1,0:T(8,128)S(1)} collective-permute-done((f32[16,1152]{1,0:T(8,128)S(1)}, f32[16,1152]{1,0:T(8,128)S(1)}, u32[]{:S(2)}, u32[]{:S(2)}) %collective-permute-start.16) | collective-permute-done | bytes 73760 | tf_op jit(solution)/shard_map/ppermute | solution.py:106
  73.8 1.4 %collective-permute-start.17 = (f32[16,1152]{1,0:T(8,128)S(1)}, f32[16,1152]{1,0:T(8,128)S(1)}, u32[]{:S(2)}, u32[]{:S(2)}) collective-permute-start(f32[16,1152]{1,0:T(8,128)S(1)} %shard_map.91.refs_0_), channel_id=1, source_target_pairs={{0,6},{2,4},{4,2},{6,0},{8,14},{10,12},{12,10},{14,8},{16,22},{18,... | collective-permute-start | bytes 221192 | tf_op jit(solution)/shard_map/ppermute | solution.py:97
  75.9 1.5 %collective-permute-start.19 = (f32[16,1152]{1,0:T(8,128)S(1)}, f32[16,1152]{1,0:T(8,128)S(1)}, u32[]{:S(2)}, u32[]{:S(2)}) collective-permute-start(f32[16,1152]{1,0:T(8,128)S(1)} %shard_map.91.refs_0_), channel_id=1, source_target_pairs={{0,2},{2,0},{4,6},{6,4},{8,10},{10,8},{12,14},{14,12},{16,18},{18,... | collective-permute-start | bytes 221192 | tf_op jit(solution)/shard_map/ppermute | solution.py:97
  77.4 1.8 %collective-permute-done.17.refs_1_ = f32[16,1152]{1,0:T(8,128)S(1)} collective-permute-done((f32[16,1152]{1,0:T(8,128)S(1)}, f32[16,1152]{1,0:T(8,128)S(1)}, u32[]{:S(2)}, u32[]{:S(2)}) %collective-permute-start.17) | collective-permute-done | bytes 73760 | tf_op jit(solution)/shard_map/ppermute | solution.py:97
  79.2 0.8 collective-permute-done.18.refs_2_
  80.2 0.8 shard_map.92
  (33 shorter events, 10.6 us)
Async XLA Ops:
  3.2 1.4 %collective-permute-start = (f32[16,384]{1,0:T(8,128)S(1)}, f32[16,384]{1,0:T(8,128)S(1)}, u32[]{:S(2)}, u32[]{:S(2)}) collective-permute-start(f32[16,384]{1,0:T(8,128)S(1)} %get-tuple-element.45.refs_0_), channel_id=1, source_target_pairs={{0,1},{1,0},{2,3},{3,2},{4,5},{5,4},{6,7},{7,6},{8,9},{9,8},{10,11... | collective-permute-start | bytes 73736 | tf_op jit(solution)/shard_map/ppermute | solution.py:97
  22.4 4.7 %collective-permute-start.1 = (f32[16,1152]{1,0:T(8,128)S(1)}, f32[16,1152]{1,0:T(8,128)S(1)}, u32[]{:S(2)}, u32[]{:S(2)}) collective-permute-start(f32[16,1152]{1,0:T(8,128)S(1)} %get-tuple-element.58), channel_id=1, source_target_pairs={{0,2},{2,0},{4,6},{6,4},{8,10},{10,8},{12,14},{14,12},{16,18},{18,... | collective-permute-start | bytes 221192 | tf_op jit(solution)/shard_map/ppermute | solution.py:97
  22.9 5.1 %collective-permute-start.2 = (f32[16,1152]{1,0:T(8,128)S(1)}, f32[16,1152]{1,0:T(8,128)S(1)}, u32[]{:S(2)}, u32[]{:S(2)}) collective-permute-start(f32[16,1152]{1,0:T(8,128)S(1)} %get-tuple-element.59), channel_id=1, source_target_pairs={{0,4},{2,6},{4,0},{6,2},{8,12},{10,14},{12,8},{14,10},{16,20},{18,... | collective-permute-start | bytes 221192 | tf_op jit(solution)/shard_map/ppermute | solution.py:97
  23.6 5.3 %collective-permute-start.3 = (f32[16,1152]{1,0:T(8,128)S(1)}, f32[16,1152]{1,0:T(8,128)S(1)}, u32[]{:S(2)}, u32[]{:S(2)}) collective-permute-start(f32[16,1152]{1,0:T(8,128)S(1)} %get-tuple-element.60), channel_id=1, source_target_pairs={{0,6},{2,4},{4,2},{6,0},{8,14},{10,12},{12,10},{14,8},{16,22},{18,... | collective-permute-start | bytes 221192 | tf_op jit(solution)/shard_map/ppermute | solution.py:97
  28.9 6.4 %collective-permute-start.4 = (f32[16,1152]{1,0:T(8,128)S(1)}, f32[16,1152]{1,0:T(8,128)S(1)}, u32[]{:S(2)}, u32[]{:S(2)}) collective-permute-start(f32[16,1152]{1,0:T(8,128)S(1)} %add_add_fusion.1.refs_0_), channel_id=1, source_target_pairs={{0,24},{1,25},{2,26},{3,27},{4,28},{5,29},{6,30},{7,31},{8,16},{9,... | collective-permute-start | bytes 221192 | tf_op jit(solution)/shard_map/ppermute | solution.py:106
  29.6 5.8 %collective-permute-start.5 = (f32[16,1152]{1,0:T(8,128)S(1)}, f32[16,1152]{1,0:T(8,128)S(1)}, u32[]{:S(2)}, u32[]{:S(2)}) collective-permute-start(f32[16,1152]{1,0:T(8,128)S(1)} %add_add_fusion.1.refs_0_), channel_id=1, source_target_pairs={{0,8},{1,17},{2,10},{3,19},{4,12},{5,21},{6,14},{7,23},{8,0},{9,25... | collective-permute-start | bytes 221192 | tf_op jit(solution)/shard_map/ppermute | solution.py:106
  30.1 6.8 %collective-permute-start.6 = (f32[16,1152]{1,0:T(8,128)S(1)}, f32[16,1152]{1,0:T(8,128)S(1)}, u32[]{:S(2)}, u32[]{:S(2)}) collective-permute-start(f32[16,1152]{1,0:T(8,128)S(1)} %add_add_fusion.1.refs_0_), channel_id=1, source_target_pairs={{0,16},{1,9},{2,18},{3,11},{4,20},{5,13},{6,22},{7,15},{8,24},{9,1... | collective-permute-start | bytes 221192 | tf_op jit(solution)/shard_map/ppermute | solution.py:106
  37.1 5.3 %collective-permute-start.9 = (f32[16,1152]{1,0:T(8,128)S(1)}, f32[16,1152]{1,0:T(8,128)S(1)}, u32[]{:S(2)}, u32[]{:S(2)}) collective-permute-start(f32[16,1152]{1,0:T(8,128)S(1)} %shard_map.82.chunk_ref.old_ref), channel_id=1, source_target_pairs={{0,6},{2,4},{4,2},{6,0},{8,14},{10,12},{12,10},{14,8},{16,22},{18,... | collective-permute-start | bytes 221192 | tf_op jit(solution)/shard_map/ppermute | solution.py:97
  38.4 4.7 %collective-permute-start.8 = (f32[16,1152]{1,0:T(8,128)S(1)}, f32[16,1152]{1,0:T(8,128)S(1)}, u32[]{:S(2)}, u32[]{:S(2)}) collective-permute-start(f32[16,1152]{1,0:T(8,128)S(1)} %shard_map.82.chunk_ref.old_ref), channel_id=1, source_target_pairs={{0,4},{2,6},{4,0},{6,2},{8,12},{10,14},{12,8},{14,10},{16,20},{18,... | collective-permute-start | bytes 221192 | tf_op jit(solution)/shard_map/ppermute | solution.py:97
  39.1 4.4 %collective-permute-start.7 = (f32[16,1152]{1,0:T(8,128)S(1)}, f32[16,1152]{1,0:T(8,128)S(1)}, u32[]{:S(2)}, u32[]{:S(2)}) collective-permute-start(f32[16,1152]{1,0:T(8,128)S(1)} %shard_map.82.chunk_ref.old_ref), channel_id=1, source_target_pairs={{0,2},{2,0},{4,6},{6,4},{8,10},{10,8},{12,14},{14,12},{16,18},{18,... | collective-permute-start | bytes 221192 | tf_op jit(solution)/shard_map/ppermute | solution.py:97
  43.9 1.2 %collective-permute-start.10 = (f32[16,384]{1,0:T(8,128)S(1)}, f32[16,384]{1,0:T(8,128)S(1)}, u32[]{:S(2)}, u32[]{:S(2)}) collective-permute-start(f32[16,384]{1,0:T(8,128)S(1)} %get-tuple-element.67.refs_0_), channel_id=1, source_target_pairs={{0,1},{1,0},{2,3},{3,2},{4,5},{5,4},{6,7},{7,6},{8,9},{9,8},{10,11... | collective-permute-start | bytes 73736 | tf_op jit(solution)/shard_map/ppermute | solution.py:97
  59.1 4.7 %collective-permute-start.11 = (f32[16,1152]{1,0:T(8,128)S(1)}, f32[16,1152]{1,0:T(8,128)S(1)}, u32[]{:S(2)}, u32[]{:S(2)}) collective-permute-start(f32[16,1152]{1,0:T(8,128)S(1)} %get-tuple-element.76), channel_id=1, source_target_pairs={{0,2},{2,0},{4,6},{6,4},{8,10},{10,8},{12,14},{14,12},{16,18},{18,... | collective-permute-start | bytes 221192 | tf_op jit(solution)/shard_map/ppermute | solution.py:97
  59.7 5.1 %collective-permute-start.12 = (f32[16,1152]{1,0:T(8,128)S(1)}, f32[16,1152]{1,0:T(8,128)S(1)}, u32[]{:S(2)}, u32[]{:S(2)}) collective-permute-start(f32[16,1152]{1,0:T(8,128)S(1)} %get-tuple-element.77), channel_id=1, source_target_pairs={{0,4},{2,6},{4,0},{6,2},{8,12},{10,14},{12,8},{14,10},{16,20},{18,... | collective-permute-start | bytes 221192 | tf_op jit(solution)/shard_map/ppermute | solution.py:97
  60.4 5.3 %collective-permute-start.13 = (f32[16,1152]{1,0:T(8,128)S(1)}, f32[16,1152]{1,0:T(8,128)S(1)}, u32[]{:S(2)}, u32[]{:S(2)}) collective-permute-start(f32[16,1152]{1,0:T(8,128)S(1)} %get-tuple-element.78), channel_id=1, source_target_pairs={{0,6},{2,4},{4,2},{6,0},{8,14},{10,12},{12,10},{14,8},{16,22},{18,... | collective-permute-start | bytes 221192 | tf_op jit(solution)/shard_map/ppermute | solution.py:97
  65.6 6.4 %collective-permute-start.14 = (f32[16,1152]{1,0:T(8,128)S(1)}, f32[16,1152]{1,0:T(8,128)S(1)}, u32[]{:S(2)}, u32[]{:S(2)}) collective-permute-start(f32[16,1152]{1,0:T(8,128)S(1)} %add_add_fusion.refs_0_), channel_id=1, source_target_pairs={{0,24},{1,25},{2,26},{3,27},{4,28},{5,29},{6,30},{7,31},{8,16},{9,... | collective-permute-start | bytes 221192 | tf_op jit(solution)/shard_map/ppermute | solution.py:106
  66.3 5.8 %collective-permute-start.15 = (f32[16,1152]{1,0:T(8,128)S(1)}, f32[16,1152]{1,0:T(8,128)S(1)}, u32[]{:S(2)}, u32[]{:S(2)}) collective-permute-start(f32[16,1152]{1,0:T(8,128)S(1)} %add_add_fusion.refs_0_), channel_id=1, source_target_pairs={{0,8},{1,17},{2,10},{3,19},{4,12},{5,21},{6,14},{7,23},{8,0},{9,25... | collective-permute-start | bytes 221192 | tf_op jit(solution)/shard_map/ppermute | solution.py:106
  66.9 6.8 %collective-permute-start.16 = (f32[16,1152]{1,0:T(8,128)S(1)}, f32[16,1152]{1,0:T(8,128)S(1)}, u32[]{:S(2)}, u32[]{:S(2)}) collective-permute-start(f32[16,1152]{1,0:T(8,128)S(1)} %add_add_fusion.refs_0_), channel_id=1, source_target_pairs={{0,16},{1,9},{2,18},{3,11},{4,20},{5,13},{6,22},{7,15},{8,24},{9,1... | collective-permute-start | bytes 221192 | tf_op jit(solution)/shard_map/ppermute | solution.py:106
  73.8 5.3 %collective-permute-start.17 = (f32[16,1152]{1,0:T(8,128)S(1)}, f32[16,1152]{1,0:T(8,128)S(1)}, u32[]{:S(2)}, u32[]{:S(2)}) collective-permute-start(f32[16,1152]{1,0:T(8,128)S(1)} %shard_map.91.refs_0_), channel_id=1, source_target_pairs={{0,6},{2,4},{4,2},{6,0},{8,14},{10,12},{12,10},{14,8},{16,22},{18,... | collective-permute-start | bytes 221192 | tf_op jit(solution)/shard_map/ppermute | solution.py:97
  75.2 4.7 %collective-permute-start.18 = (f32[16,1152]{1,0:T(8,128)S(1)}, f32[16,1152]{1,0:T(8,128)S(1)}, u32[]{:S(2)}, u32[]{:S(2)}) collective-permute-start(f32[16,1152]{1,0:T(8,128)S(1)} %shard_map.91.refs_0_), channel_id=1, source_target_pairs={{0,4},{2,6},{4,0},{6,2},{8,12},{10,14},{12,8},{14,10},{16,20},{18,... | collective-permute-start | bytes 221192 | tf_op jit(solution)/shard_map/ppermute | solution.py:97
  75.9 4.4 %collective-permute-start.19 = (f32[16,1152]{1,0:T(8,128)S(1)}, f32[16,1152]{1,0:T(8,128)S(1)}, u32[]{:S(2)}, u32[]{:S(2)}) collective-permute-start(f32[16,1152]{1,0:T(8,128)S(1)} %shard_map.91.refs_0_), channel_id=1, source_target_pairs={{0,2},{2,0},{4,6},{6,4},{8,10},{10,8},{12,14},{14,12},{16,18},{18,... | collective-permute-start | bytes 221192 | tf_op jit(solution)/shard_map/ppermute | solution.py:97

commit v7 on v6

--- a/solution.py
+++ b/solution.py
@@ -242,7 +242,7 @@
     parts_ref[...] = parts
     parts = parts[:, 0 : sz.stack]
 
-    total = jnp.zeros((8, BLOCK), F32)
+    total = jnp.zeros((32, BLOCK), F32)
     for k, stack_ref in enumerate(stack_refs):
         start = start_of(sz, k)
         for step in range(sz.chunk // width):
@@ -252,7 +252,7 @@
                 block = (start // BLOCK + step * (width // BLOCK) + j) % (ROW_PX // BLOCK)
                 keep = keep_ref[jnp.minimum(block, keep_ref.shape[0] - 1)]
                 term = keep * square[:, j * BLOCK : (j + 1) * BLOCK]
-                total = total + jnp.sum(term.reshape(td // 8, 8, BLOCK), axis=0)
+                total = total + jnp.sum(term.reshape(td // 32, 32, BLOCK), axis=0)
     total = jnp.sum(jnp.sum(total, axis=0, keepdims=True), axis=1, keepdims=True)
     products = jnp.concatenate([coef[i : i + 1] * coef for i in range(r)], axis=0)
     ones = valid_ref[...].astype(BF16)

time: 81.2 us -> 81.3 us (level)
  no operation moved by 1% of the time
where the time goes in v7:
time: 81.3 us; the launch traced here: 81 us
  blocking collectives  25 us (31%)
  starting transfers between devices  23.6 us (29%)
  waiting for transfers between devices  17.3 us (21%)
  Pallas kernels  14.3 us (18%)
    all_to_all x2, blocking collectives, local(): notes = lax.all_to_all(note, everyone, 0, 0, tiled=True)  25 us
    ppermute x14, starting transfers between devices, partner(): return lax.ppermute(x, axis, [(i, i ^ mask) for i in range(n)])  14.6 us
    pallas_call x17, Pallas kernels, call(): pl.pallas_call(body, out_shape=[jax.ShapeDtypeStruct(s, t) for s, t in ou...  14.3 us
    ppermute x14, waiting for transfers between devices, partner(): return lax.ppermute(x, axis, [(i, i ^ mask) for i in range(n)])  11 us
    ppermute x6, starting transfers between devices, crossed(): return lax.ppermute(x, ('tiles', 'pix'), pairs)  8.91 us
    ppermute x6, waiting for transfers between devices, crossed(): return lax.ppermute(x, ('tiles', 'pix'), pairs)  6.36 us
  transfers between devices with their start and end apart: 20, of which 17 were waited for; matrix products, arithmetic and copies ran while one was open for 0% of the time, Pallas kernels for 4%

profile of v7, /device:TPU:0, one launch (start us, length us, event | category | flops | bytes accessed | tf_op | source)
XLA Modules:
  0.0 81.0 jit_solution(14122874168818757083)
XLA Ops:
  0.6 2.6 %shard_map.76 = (bf16[256,4096]{1,0:T(8,128)(2,1)S(1)}, f32[16,384]{1,0:T(8,128)S(1)}, f32[16,1152]{1,0:T(8,128)S(1)}, s32[8,256]{1,0:T(8,128)S(1)}, f32[8,256]{...) custom-call(bf16[256,4096]{1,0:T(8,128)(2,1)} %f_hbm.1, ...), custom_call_target="tpu_custom_call" | custom-call | tf_op jit(solution)/shard_map/pallas_call | solution.py:359
  4.6 1.9 %shard_map.78 = (f32[16,256]{1,0:T(8,128)}, bf16[64,256]{1,0:T(8,128)(2,1)S(1)}, bf16[256,128]{1,0:T(8,128)(2,1)S(1)}, f32[32,256]{1,0:T(8,128)S(1)}) custom-call(f32[16,384]{1,0:T(8,128)S(1)} %get-tuple-element.45.refs_0_, f32[16,384]{1,0:T(8,128)S(1)} %collective-permute-done.refs_1_, bf16[112,1024]{1,0:T(8,128)(2,1)S(1)} %get-tuple-element.46.refs_2_.refs_0_, ...), custom_call_target="tpu_custom_call" | custom-call | tf_op jit(solution)/shard_map/pallas_call | solution.py:359
  6.5 14.2 %all_to_all.22 = f32[32,1,256]{2,1,0:T(1,128)S(1)} all-to-all(f32[32,1,256]{2,1,0:T(1,128)S(1)} %copy.8), channel_id=1, replica_groups=mesh['tiles'=16,'pix'=2] {'tiles','pix'}, dimensions={0} | all-to-all | bytes 65536 | tf_op jit(solution)/shard_map/all_to_all | solution.py:412
  20.8 1.7 %shard_map.81 = (f32[16,1152]{1,0:T(8,128)S(1)}, f32[16,1152]{1,0:T(8,128)S(1)}, f32[16,1152]{1,0:T(8,128)S(1)}) custom-call(f32[32,256]{1,0:T(8,128)S(1)} %bitcast.13, bf16[256,4096]{1,0:T(8,128)(2,1)S(1)} %get-tuple-element.44.refs_6_.f_ref, f32[9,256,128]{2,1,0:T(8,128)S(1)} %get-tuple-element.55.bar_ref, ...), custom_call_target="tpu_custom_call" | custom-call | tf_op jit(solution)/shard_map/pallas_call | solution.py:359
  22.9 0.7 collective-permute-start.2
  23.6 2.3 %collective-permute-start.3 = (f32[16,1152]{1,0:T(8,128)S(1)}, f32[16,1152]{1,0:T(8,128)S(1)}, u32[]{:S(2)}, u32[]{:S(2)}) collective-permute-start(f32[16,1152]{1,0:T(8,128)S(1)} %get-tuple-element.60), channel_id=1, source_target_pairs={{0,6},{2,4},{4,2},{6,0},{8,14},{10,12},{12,10},{14,8},{16,22},{18,... | collective-permute-start | bytes 221192 | tf_op jit(solution)/shard_map/ppermute | solution.py:97
  25.9 0.7 shard_map.80
  27.1 1.0 %collective-permute-done.2 = f32[16,1152]{1,0:T(8,128)S(1)} collective-permute-done((f32[16,1152]{1,0:T(8,128)S(1)}, f32[16,1152]{1,0:T(8,128)S(1)}, u32[]{:S(2)}, u32[]{:S(2)}) %collective-permute-start.2) | collective-permute-done | bytes 73760 | tf_op jit(solution)/shard_map/ppermute | solution.py:97
  28.1 0.8 %collective-permute-done.3 = f32[16,1152]{1,0:T(8,128)S(1)} collective-permute-done((f32[16,1152]{1,0:T(8,128)S(1)}, f32[16,1152]{1,0:T(8,128)S(1)}, u32[]{:S(2)}, u32[]{:S(2)}) %collective-permute-start.3) | collective-permute-done | bytes 73760 | tf_op jit(solution)/shard_map/ppermute | solution.py:97
  30.1 3.2 %collective-permute-start.6 = (f32[16,1152]{1,0:T(8,128)S(1)}, f32[16,1152]{1,0:T(8,128)S(1)}, u32[]{:S(2)}, u32[]{:S(2)}) collective-permute-start(f32[16,1152]{1,0:T(8,128)S(1)} %add_add_fusion.1.refs_0_), channel_id=1, source_target_pairs={{0,16},{1,9},{2,18},{3,11},{4,20},{5,13},{6,22},{7,15},{8,24},{9,1... | collective-permute-start | bytes 221192 | tf_op jit(solution)/shard_map/ppermute | solution.py:106
  33.7 1.6 %collective-permute-done.4.refs_1_ = f32[16,1152]{1,0:T(8,128)S(1)} collective-permute-done((f32[16,1152]{1,0:T(8,128)S(1)}, f32[16,1152]{1,0:T(8,128)S(1)}, u32[]{:S(2)}, u32[]{:S(2)}) %collective-permute-start.4) | collective-permute-done | bytes 73760 | tf_op jit(solution)/shard_map/ppermute | solution.py:106
  35.3 1.6 %collective-permute-done.6.refs_3_ = f32[16,1152]{1,0:T(8,128)S(1)} collective-permute-done((f32[16,1152]{1,0:T(8,128)S(1)}, f32[16,1152]{1,0:T(8,128)S(1)}, u32[]{:S(2)}, u32[]{:S(2)}) %collective-permute-start.6) | collective-permute-done | bytes 73760 | tf_op jit(solution)/shard_map/ppermute | solution.py:106
  37.1 1.4 %collective-permute-start.9 = (f32[16,1152]{1,0:T(8,128)S(1)}, f32[16,1152]{1,0:T(8,128)S(1)}, u32[]{:S(2)}, u32[]{:S(2)}) collective-permute-start(f32[16,1152]{1,0:T(8,128)S(1)} %shard_map.82.chunk_ref.old_ref), channel_id=1, source_target_pairs={{0,6},{2,4},{4,2},{6,0},{8,14},{10,12},{12,10},{14,8},{16,22},{18,... | collective-permute-start | bytes 221192 | tf_op jit(solution)/shard_map/ppermute | solution.py:97
  39.1 1.5 %collective-permute-start.7 = (f32[16,1152]{1,0:T(8,128)S(1)}, f32[16,1152]{1,0:T(8,128)S(1)}, u32[]{:S(2)}, u32[]{:S(2)}) collective-permute-start(f32[16,1152]{1,0:T(8,128)S(1)} %shard_map.82.chunk_ref.old_ref), channel_id=1, source_target_pairs={{0,2},{2,0},{4,6},{6,4},{8,10},{10,8},{12,14},{14,12},{16,18},{18,... | collective-permute-start | bytes 221192 | tf_op jit(solution)/shard_map/ppermute | solution.py:97
  41.0 1.4 %collective-permute-done.9.chunk_ref = f32[16,1152]{1,0:T(8,128)S(1)} collective-permute-done((f32[16,1152]{1,0:T(8,128)S(1)}, f32[16,1152]{1,0:T(8,128)S(1)}, u32[]{:S(2)}, u32[]{:S(2)}) %collective-permute-start.9) | collective-permute-done | bytes 73760 | tf_op jit(solution)/shard_map/ppermute | solution.py:97
  44.0 1.2 %collective-permute-done.10.refs_1_ = f32[16,384]{1,0:T(8,128)S(1)} collective-permute-done((f32[16,384]{1,0:T(8,128)S(1)}, f32[16,384]{1,0:T(8,128)S(1)}, u32[]{:S(2)}, u32[]{:S(2)}) %collective-permute-start.10) | collective-permute-done | bytes 24608 | tf_op jit(solution)/shard_map/ppermute | solution.py:97
  45.2 1.5 %shard_map.87 = (f32[16,256]{1,0:T(8,128)S(1)}, bf16[64,256]{1,0:T(8,128)(2,1)S(1)}, bf16[256,128]{1,0:T(8,128)(2,1)S(1)}, f32[32,256]{1,0:T(8,128)S(1)}) custom-call(f32[16,384]{1,0:T(8,128)S(1)} %get-tuple-element.67.refs_0_, f32[16,384]{1,0:T(8,128)S(1)} %collective-permute-done.10.refs_1_, bf16[112,1024]{1,0:T(8,128)(2,1)S(1)} %get-tuple-element.68.refs_2_.refs_0_, ...), custom_call_target="tpu_custom_call" | custom-call | tf_op jit(solution)/shard_map/pallas_call | solution.py:359
  46.7 10.8 %all_to_all.23 = f32[32,1,256]{2,1,0:T(1,128)S(1)} all-to-all(f32[32,1,256]{2,1,0:T(1,128)S(1)} %copy.9), channel_id=1, replica_groups=mesh['tiles'=16,'pix'=2] {'tiles','pix'}, dimensions={0} | all-to-all | bytes 65536 | tf_op jit(solution)/shard_map/all_to_all | solution.py:412
  57.5 1.7 %shard_map.90 = (f32[16,1152]{1,0:T(8,128)S(1)}, f32[16,1152]{1,0:T(8,128)S(1)}, f32[16,1152]{1,0:T(8,128)S(1)}) custom-call(f32[32,256]{1,0:T(8,128)S(1)} %bitcast.16, bf16[256,4096]{1,0:T(8,128)(2,1)S(1)} %get-tuple-element.44.refs_6_.f_ref, f32[9,256,128]{2,1,0:T(8,128)S(1)} %get-tuple-element.55.bar_ref, ...), custom_call_target="tpu_custom_call" | custom-call | tf_op jit(solution)/shard_map/pallas_call | solution.py:359
  59.7 0.7 collective-permute-start.12
  60.4 2.3 %collective-permute-start.13 = (f32[16,1152]{1,0:T(8,128)S(1)}, f32[16,1152]{1,0:T(8,128)S(1)}, u32[]{:S(2)}, u32[]{:S(2)}) collective-permute-start(f32[16,1152]{1,0:T(8,128)S(1)} %get-tuple-element.78), channel_id=1, source_target_pairs={{0,6},{2,4},{4,2},{6,0},{8,14},{10,12},{12,10},{14,8},{16,22},{18,... | collective-permute-start | bytes 221192 | tf_op jit(solution)/shard_map/ppermute | solution.py:97
  62.7 0.7 shard_map.89
  63.8 1.0 %collective-permute-done.12 = f32[16,1152]{1,0:T(8,128)S(1)} collective-permute-done((f32[16,1152]{1,0:T(8,128)S(1)}, f32[16,1152]{1,0:T(8,128)S(1)}, u32[]{:S(2)}, u32[]{:S(2)}) %collective-permute-start.12) | collective-permute-done | bytes 73760 | tf_op jit(solution)/shard_map/ppermute | solution.py:97
  64.8 0.8 %collective-permute-done.13 = f32[16,1152]{1,0:T(8,128)S(1)} collective-permute-done((f32[16,1152]{1,0:T(8,128)S(1)}, f32[16,1152]{1,0:T(8,128)S(1)}, u32[]{:S(2)}, u32[]{:S(2)}) %collective-permute-start.13) | collective-permute-done | bytes 73760 | tf_op jit(solution)/shard_map/ppermute | solution.py:97
  66.9 3.2 %collective-permute-start.16 = (f32[16,1152]{1,0:T(8,128)S(1)}, f32[16,1152]{1,0:T(8,128)S(1)}, u32[]{:S(2)}, u32[]{:S(2)}) collective-permute-start(f32[16,1152]{1,0:T(8,128)S(1)} %add_add_fusion.refs_0_), channel_id=1, source_target_pairs={{0,16},{1,9},{2,18},{3,11},{4,20},{5,13},{6,22},{7,15},{8,24},{9,1... | collective-permute-start | bytes 221192 | tf_op jit(solution)/shard_map/ppermute | solution.py:106
  70.5 1.6 %collective-permute-done.14.refs_1_ = f32[16,1152]{1,0:T(8,128)S(1)} collective-permute-done((f32[16,1152]{1,0:T(8,128)S(1)}, f32[16,1152]{1,0:T(8,128)S(1)}, u32[]{:S(2)}, u32[]{:S(2)}) %collective-permute-start.14) | collective-permute-done | bytes 73760 | tf_op jit(solution)/shard_map/ppermute | solution.py:106
  72.1 1.6 %collective-permute-done.16.refs_3_ = f32[16,1152]{1,0:T(8,128)S(1)} collective-permute-done((f32[16,1152]{1,0:T(8,128)S(1)}, f32[16,1152]{1,0:T(8,128)S(1)}, u32[]{:S(2)}, u32[]{:S(2)}) %collective-permute-start.16) | collective-permute-done | bytes 73760 | tf_op jit(solution)/shard_map/ppermute | solution.py:106
  73.9 1.3 %collective-permute-start.17 = (f32[16,1152]{1,0:T(8,128)S(1)}, f32[16,1152]{1,0:T(8,128)S(1)}, u32[]{:S(2)}, u32[]{:S(2)}) collective-permute-start(f32[16,1152]{1,0:T(8,128)S(1)} %shard_map.91.refs_0_), channel_id=1, source_target_pairs={{0,6},{2,4},{4,2},{6,0},{8,14},{10,12},{12,10},{14,8},{16,22},{18,... | collective-permute-start | bytes 221192 | tf_op jit(solution)/shard_map/ppermute | solution.py:97
  75.9 1.5 %collective-permute-start.19 = (f32[16,1152]{1,0:T(8,128)S(1)}, f32[16,1152]{1,0:T(8,128)S(1)}, u32[]{:S(2)}, u32[]{:S(2)}) collective-permute-start(f32[16,1152]{1,0:T(8,128)S(1)} %shard_map.91.refs_0_), channel_id=1, source_target_pairs={{0,2},{2,0},{4,6},{6,4},{8,10},{10,8},{12,14},{14,12},{16,18},{18,... | collective-permute-start | bytes 221192 | tf_op jit(solution)/shard_map/ppermute | solution.py:97
  77.4 1.8 %collective-permute-done.17.refs_1_ = f32[16,1152]{1,0:T(8,128)S(1)} collective-permute-done((f32[16,1152]{1,0:T(8,128)S(1)}, f32[16,1152]{1,0:T(8,128)S(1)}, u32[]{:S(2)}, u32[]{:S(2)}) %collective-permute-start.17) | collective-permute-done | bytes 73760 | tf_op jit(solution)/shard_map/ppermute | solution.py:97
  79.2 0.8 collective-permute-done.18.refs_2_
  80.3 0.8 shard_map.92
  (33 shorter events, 10.6 us)
Async XLA Ops:
  3.2 1.4 %collective-permute-start = (f32[16,384]{1,0:T(8,128)S(1)}, f32[16,384]{1,0:T(8,128)S(1)}, u32[]{:S(2)}, u32[]{:S(2)}) collective-permute-start(f32[16,384]{1,0:T(8,128)S(1)} %get-tuple-element.45.refs_0_), channel_id=1, source_target_pairs={{0,1},{1,0},{2,3},{3,2},{4,5},{5,4},{6,7},{7,6},{8,9},{9,8},{10,11... | collective-permute-start | bytes 73736 | tf_op jit(solution)/shard_map/ppermute | solution.py:97
  22.4 4.7 %collective-permute-start.1 = (f32[16,1152]{1,0:T(8,128)S(1)}, f32[16,1152]{1,0:T(8,128)S(1)}, u32[]{:S(2)}, u32[]{:S(2)}) collective-permute-start(f32[16,1152]{1,0:T(8,128)S(1)} %get-tuple-element.58), channel_id=1, source_target_pairs={{0,2},{2,0},{4,6},{6,4},{8,10},{10,8},{12,14},{14,12},{16,18},{18,... | collective-permute-start | bytes 221192 | tf_op jit(solution)/shard_map/ppermute | solution.py:97
  22.9 5.1 %collective-permute-start.2 = (f32[16,1152]{1,0:T(8,128)S(1)}, f32[16,1152]{1,0:T(8,128)S(1)}, u32[]{:S(2)}, u32[]{:S(2)}) collective-permute-start(f32[16,1152]{1,0:T(8,128)S(1)} %get-tuple-element.59), channel_id=1, source_target_pairs={{0,4},{2,6},{4,0},{6,2},{8,12},{10,14},{12,8},{14,10},{16,20},{18,... | collective-permute-start | bytes 221192 | tf_op jit(solution)/shard_map/ppermute | solution.py:97
  23.6 5.3 %collective-permute-start.3 = (f32[16,1152]{1,0:T(8,128)S(1)}, f32[16,1152]{1,0:T(8,128)S(1)}, u32[]{:S(2)}, u32[]{:S(2)}) collective-permute-start(f32[16,1152]{1,0:T(8,128)S(1)} %get-tuple-element.60), channel_id=1, source_target_pairs={{0,6},{2,4},{4,2},{6,0},{8,14},{10,12},{12,10},{14,8},{16,22},{18,... | collective-permute-start | bytes 221192 | tf_op jit(solution)/shard_map/ppermute | solution.py:97
  28.9 6.4 %collective-permute-start.4 = (f32[16,1152]{1,0:T(8,128)S(1)}, f32[16,1152]{1,0:T(8,128)S(1)}, u32[]{:S(2)}, u32[]{:S(2)}) collective-permute-start(f32[16,1152]{1,0:T(8,128)S(1)} %add_add_fusion.1.refs_0_), channel_id=1, source_target_pairs={{0,24},{1,25},{2,26},{3,27},{4,28},{5,29},{6,30},{7,31},{8,16},{9,... | collective-permute-start | bytes 221192 | tf_op jit(solution)/shard_map/ppermute | solution.py:106
  29.6 5.8 %collective-permute-start.5 = (f32[16,1152]{1,0:T(8,128)S(1)}, f32[16,1152]{1,0:T(8,128)S(1)}, u32[]{:S(2)}, u32[]{:S(2)}) collective-permute-start(f32[16,1152]{1,0:T(8,128)S(1)} %add_add_fusion.1.refs_0_), channel_id=1, source_target_pairs={{0,8},{1,17},{2,10},{3,19},{4,12},{5,21},{6,14},{7,23},{8,0},{9,25... | collective-permute-start | bytes 221192 | tf_op jit(solution)/shard_map/ppermute | solution.py:106
  30.1 6.8 %collective-permute-start.6 = (f32[16,1152]{1,0:T(8,128)S(1)}, f32[16,1152]{1,0:T(8,128)S(1)}, u32[]{:S(2)}, u32[]{:S(2)}) collective-permute-start(f32[16,1152]{1,0:T(8,128)S(1)} %add_add_fusion.1.refs_0_), channel_id=1, source_target_pairs={{0,16},{1,9},{2,18},{3,11},{4,20},{5,13},{6,22},{7,15},{8,24},{9,1... | collective-permute-start | bytes 221192 | tf_op jit(solution)/shard_map/ppermute | solution.py:106
  37.1 5.3 %collective-permute-start.9 = (f32[16,1152]{1,0:T(8,128)S(1)}, f32[16,1152]{1,0:T(8,128)S(1)}, u32[]{:S(2)}, u32[]{:S(2)}) collective-permute-start(f32[16,1152]{1,0:T(8,128)S(1)} %shard_map.82.chunk_ref.old_ref), channel_id=1, source_target_pairs={{0,6},{2,4},{4,2},{6,0},{8,14},{10,12},{12,10},{14,8},{16,22},{18,... | collective-permute-start | bytes 221192 | tf_op jit(solution)/shard_map/ppermute | solution.py:97
  38.5 4.7 %collective-permute-start.8 = (f32[16,1152]{1,0:T(8,128)S(1)}, f32[16,1152]{1,0:T(8,128)S(1)}, u32[]{:S(2)}, u32[]{:S(2)}) collective-permute-start(f32[16,1152]{1,0:T(8,128)S(1)} %shard_map.82.chunk_ref.old_ref), channel_id=1, source_target_pairs={{0,4},{2,6},{4,0},{6,2},{8,12},{10,14},{12,8},{14,10},{16,20},{18,... | collective-permute-start | bytes 221192 | tf_op jit(solution)/shard_map/ppermute | solution.py:97
  39.1 4.4 %collective-permute-start.7 = (f32[16,1152]{1,0:T(8,128)S(1)}, f32[16,1152]{1,0:T(8,128)S(1)}, u32[]{:S(2)}, u32[]{:S(2)}) collective-permute-start(f32[16,1152]{1,0:T(8,128)S(1)} %shard_map.82.chunk_ref.old_ref), channel_id=1, source_target_pairs={{0,2},{2,0},{4,6},{6,4},{8,10},{10,8},{12,14},{14,12},{16,18},{18,... | collective-permute-start | bytes 221192 | tf_op jit(solution)/shard_map/ppermute | solution.py:97
  43.9 1.2 %collective-permute-start.10 = (f32[16,384]{1,0:T(8,128)S(1)}, f32[16,384]{1,0:T(8,128)S(1)}, u32[]{:S(2)}, u32[]{:S(2)}) collective-permute-start(f32[16,384]{1,0:T(8,128)S(1)} %get-tuple-element.67.refs_0_), channel_id=1, source_target_pairs={{0,1},{1,0},{2,3},{3,2},{4,5},{5,4},{6,7},{7,6},{8,9},{9,8},{10,11... | collective-permute-start | bytes 73736 | tf_op jit(solution)/shard_map/ppermute | solution.py:97
  59.2 4.7 %collective-permute-start.11 = (f32[16,1152]{1,0:T(8,128)S(1)}, f32[16,1152]{1,0:T(8,128)S(1)}, u32[]{:S(2)}, u32[]{:S(2)}) collective-permute-start(f32[16,1152]{1,0:T(8,128)S(1)} %get-tuple-element.76), channel_id=1, source_target_pairs={{0,2},{2,0},{4,6},{6,4},{8,10},{10,8},{12,14},{14,12},{16,18},{18,... | collective-permute-start | bytes 221192 | tf_op jit(solution)/shard_map/ppermute | solution.py:97
  59.7 5.1 %collective-permute-start.12 = (f32[16,1152]{1,0:T(8,128)S(1)}, f32[16,1152]{1,0:T(8,128)S(1)}, u32[]{:S(2)}, u32[]{:S(2)}) collective-permute-start(f32[16,1152]{1,0:T(8,128)S(1)} %get-tuple-element.77), channel_id=1, source_target_pairs={{0,4},{2,6},{4,0},{6,2},{8,12},{10,14},{12,8},{14,10},{16,20},{18,... | collective-permute-start | bytes 221192 | tf_op jit(solution)/shard_map/ppermute | solution.py:97
  60.4 5.3 %collective-permute-start.13 = (f32[16,1152]{1,0:T(8,128)S(1)}, f32[16,1152]{1,0:T(8,128)S(1)}, u32[]{:S(2)}, u32[]{:S(2)}) collective-permute-start(f32[16,1152]{1,0:T(8,128)S(1)} %get-tuple-element.78), channel_id=1, source_target_pairs={{0,6},{2,4},{4,2},{6,0},{8,14},{10,12},{12,10},{14,8},{16,22},{18,... | collective-permute-start | bytes 221192 | tf_op jit(solution)/shard_map/ppermute | solution.py:97
  65.7 6.4 %collective-permute-start.14 = (f32[16,1152]{1,0:T(8,128)S(1)}, f32[16,1152]{1,0:T(8,128)S(1)}, u32[]{:S(2)}, u32[]{:S(2)}) collective-permute-start(f32[16,1152]{1,0:T(8,128)S(1)} %add_add_fusion.refs_0_), channel_id=1, source_target_pairs={{0,24},{1,25},{2,26},{3,27},{4,28},{5,29},{6,30},{7,31},{8,16},{9,... | collective-permute-start | bytes 221192 | tf_op jit(solution)/shard_map/ppermute | solution.py:106
  66.3 5.8 %collective-permute-start.15 = (f32[16,1152]{1,0:T(8,128)S(1)}, f32[16,1152]{1,0:T(8,128)S(1)}, u32[]{:S(2)}, u32[]{:S(2)}) collective-permute-start(f32[16,1152]{1,0:T(8,128)S(1)} %add_add_fusion.refs_0_), channel_id=1, source_target_pairs={{0,8},{1,17},{2,10},{3,19},{4,12},{5,21},{6,14},{7,23},{8,0},{9,25... | collective-permute-start | bytes 221192 | tf_op jit(solution)/shard_map/ppermute | solution.py:106
  66.9 6.8 %collective-permute-start.16 = (f32[16,1152]{1,0:T(8,128)S(1)}, f32[16,1152]{1,0:T(8,128)S(1)}, u32[]{:S(2)}, u32[]{:S(2)}) collective-permute-start(f32[16,1152]{1,0:T(8,128)S(1)} %add_add_fusion.refs_0_), channel_id=1, source_target_pairs={{0,16},{1,9},{2,18},{3,11},{4,20},{5,13},{6,22},{7,15},{8,24},{9,1... | collective-permute-start | bytes 221192 | tf_op jit(solution)/shard_map/ppermute | solution.py:106
  73.9 5.3 %collective-permute-start.17 = (f32[16,1152]{1,0:T(8,128)S(1)}, f32[16,1152]{1,0:T(8,128)S(1)}, u32[]{:S(2)}, u32[]{:S(2)}) collective-permute-start(f32[16,1152]{1,0:T(8,128)S(1)} %shard_map.91.refs_0_), channel_id=1, source_target_pairs={{0,6},{2,4},{4,2},{6,0},{8,14},{10,12},{12,10},{14,8},{16,22},{18,... | collective-permute-start | bytes 221192 | tf_op jit(solution)/shard_map/ppermute | solution.py:97
  75.2 4.7 %collective-permute-start.18 = (f32[16,1152]{1,0:T(8,128)S(1)}, f32[16,1152]{1,0:T(8,128)S(1)}, u32[]{:S(2)}, u32[]{:S(2)}) collective-permute-start(f32[16,1152]{1,0:T(8,128)S(1)} %shard_map.91.refs_0_), channel_id=1, source_target_pairs={{0,4},{2,6},{4,0},{6,2},{8,12},{10,14},{12,8},{14,10},{16,20},{18,... | collective-permute-start | bytes 221192 | tf_op jit(solution)/shard_map/ppermute | solution.py:97
  75.9 4.4 %collective-permute-start.19 = (f32[16,1152]{1,0:T(8,128)S(1)}, f32[16,1152]{1,0:T(8,128)S(1)}, u32[]{:S(2)}, u32[]{:S(2)}) collective-permute-start(f32[16,1152]{1,0:T(8,128)S(1)} %shard_map.91.refs_0_), channel_id=1, source_target_pairs={{0,2},{2,0},{4,6},{6,4},{8,10},{10,8},{12,14},{14,12},{16,18},{18,... | collective-permute-start | bytes 221192 | tf_op jit(solution)/shard_map/ppermute | solution.py:97
